TPU v7x, 32 devices: a whole 2x2x4 slice. The times are simulated.
32 devices in a mesh: groups: 1, seq: 32 (over z, y, x, core).
Axes of the slice: x: 2, y: 2, z: 4, core: 2. Of those that a mesh axis runs over, the one named last changes fastest.
Arguments:
- queries: bfloat16 [8192, 2048], P(('groups', 'seq')), may hold values from -6 to 6
- keys: bfloat16 [8192, 2048], P(('groups', 'seq')), may hold values from -6 to 6
- values: bfloat16 [8192, 2048], P(('groups', 'seq')), may hold values from -6 to 6
- out_weight: bfloat16 [2048, 2048], replicated, may hold values from -0.125 to 0.125
- out_grad: bfloat16 [8192, 2048], P(('groups', 'seq')), may hold values from -6 to 6
Outputs:
- query_grad: bfloat16 [8192, 2048], P(('groups', 'seq'))
- key_grad: bfloat16 [8192, 2048], P(('groups', 'seq'))
- value_grad: bfloat16 [8192, 2048], P(('groups', 'seq'))
- weight_grad: float32 [2048, 2048], P(('groups', 'seq'))
All inputs are finite; a program needn't handle non-finite values.
Results may differ from a plain program's by a relative error of at most 0.0033.
Values sent between devices are 32-bit elements; how exact they have to be, the bound alone decides.
No kernel may reach another device: no remote copies, remote signals or barrier semaphores. Data moves between devices by JAX's collectives and lax.ppermute only.
A program may use at most 192 MiB of HBM per device.

v0:
```python
import jax
import jax.numpy as jnp
from jax import lax
from jax.sharding import PartitionSpec as P

HEADS = 16
HEAD = 128


def entering(part, axis, combine, identity, reverse):
    count = lax.axis_size(axis)
    place = lax.axis_index(axis)
    ahead = count - 1 - place if reverse else place
    gathered = jax.tree.map(lambda a: lax.all_gather(a, axis), part)
    state = jax.tree.map(lambda a, e: jnp.zeros_like(a) + jnp.asarray(e, a.dtype), part, identity)

    def one(turn, state):
        source = count - 1 - turn if reverse else turn
        return combine(
            state, jax.tree.map(lambda a: lax.dynamic_index_in_dim(a, source, 0, False), gathered)
        )

    return lax.fori_loop(0, ahead, one, state)


def feature(x):
    return jax.nn.elu(x) + 1.0


def attend_block(query_f, key_f, value_f, state, zsum):
    block_len = query_f.shape[0]
    fq = feature(query_f.reshape(block_len, HEADS, HEAD))
    fk = feature(key_f.reshape(block_len, HEADS, HEAD))
    vv = value_f.reshape(block_len, HEADS, HEAD)
    rows = lax.broadcasted_iota(jnp.int32, (block_len, block_len), 0)
    cols = lax.broadcasted_iota(jnp.int32, (block_len, block_len), 1)
    causal = (cols <= rows).astype(jnp.float32)
    scores = jnp.einsum("thd,shd->hts", fq, fk, precision=lax.Precision.HIGHEST) * causal[None]
    numer = jnp.einsum("hts,she->the", scores, vv, precision=lax.Precision.HIGHEST)
    numer = numer + jnp.einsum("thd,hde->the", fq, state, precision=lax.Precision.HIGHEST)
    denom = jnp.sum(scores, axis=2).T + jnp.einsum(
        "thd,hd->th", fq, zsum, precision=lax.Precision.HIGHEST
    )
    return (numer / denom[:, :, None]).reshape(block_len, HEADS * HEAD)


def summarize(key_f, value_f):
    block_len = key_f.shape[0]
    fk = feature(key_f.reshape(block_len, HEADS, HEAD))
    vv = value_f.reshape(block_len, HEADS, HEAD)
    state = jnp.einsum("thd,the->hde", fk, vv, precision=lax.Precision.HIGHEST)
    return (state, jnp.sum(fk, axis=0))


def add_pair(earlier, later):
    return (earlier[0] + later[0], earlier[1] + later[1])


def body(queries, keys, values, out_weight, out_grad):
    query_f = queries.astype(jnp.float32)
    key_f = keys.astype(jnp.float32)
    value_f = values.astype(jnp.float32)
    zeros_pair = (
        jnp.zeros((HEADS, HEAD, HEAD), jnp.float32),
        jnp.zeros((HEADS, HEAD), jnp.float32),
    )
    local_state, pull_state = jax.vjp(summarize, key_f, value_f)
    state_in, zsum_in = entering(local_state, "seq", add_pair, zeros_pair, False)
    attended, pull_attend = jax.vjp(attend_block, query_f, key_f, value_f, state_in, zsum_in)
    rounded = attended.astype(jnp.bfloat16)
    attended_grad = lax.dot_general(
        out_grad, out_weight, (((1,), (1,)), ((), ())), preferred_element_type=jnp.float32
    )
    query_part, key_part, value_part, state_grad, zsum_grad = pull_attend(attended_grad)
    later_state = entering((state_grad, zsum_grad), "seq", add_pair, zeros_pair, True)
    key_extra, value_extra = pull_state(later_state)
    weight_grad = lax.psum_scatter(
        lax.dot_general(
            rounded, out_grad, (((0,), (0,)), ((), ())), preferred_element_type=jnp.float32
        ),
        "seq",
        scatter_dimension=0,
        tiled=True,
    )
    query_grad = query_part.astype(jnp.bfloat16)
    key_grad = (key_part + key_extra).astype(jnp.bfloat16)
    value_grad = (value_part + value_extra).astype(jnp.bfloat16)
    return (query_grad, key_grad, value_grad, weight_grad)


def solution(mesh):
    placed = (
        P(("groups", "seq"), None),
        P(("groups", "seq"), None),
        P(("groups", "seq"), None),
        P(),
        P(("groups", "seq"), None),
    )
    return jax.shard_map(
        body,
        mesh=mesh,
        in_specs=placed,
        out_specs=(
            P(("groups", "seq"), None),
            P(("groups", "seq"), None),
            P(("groups", "seq"), None),
            P(("groups", "seq"), None),
        ),
        check_vma=False,
    )
```

profile of v0, /device:TPU:0, one launch (start us, length us, event | category | flops | bytes accessed | tf_op | source)
XLA Modules:
  0.0 676.5 jit_solution(14905975301412319601)
XLA Ops:
  7.2 1.6 copy.33
  8.8 4.9 fusion.43
  13.8 2.6 copy.32
  16.3 2.2 fusion.8
  18.5 48.0 %all_gather.27 = f32[32,16,128]{2,1,0:T(8,128)} all-gather(f32[1,16,128]{2,1,0:T(8,128)S(1)} %bitcast.170), channel_id=1, replica_groups=mesh['groups'=1,'seq'=32] {'seq'}, dimensions={0}, use_global_device_ids=true | all-gather | bytes 270336 | tf_op jit(solution)/shard_map/all_gather | solution.py:14
  66.6 9.4 %multiply_reduce_fusion = (f32[16,256]{1,0:T(8,128)S(1)}, f32[16,256,256]{1,2,0:T(8,128)}) fusion(f32[256,256]{0,1:T(8,128)S(1)} %fusion.49, f32[256,16,128]{0,2,1:T(8,128)S(1)} %bitcast.151, f32[256,16,128]{0,2,1:T(8,128)} %bitcast.155), kind=kOutput, calls=%fused_computation.13 | convolution fusion | flops 1616900096 | bytes 8667136 | tf_op jit(solution)/shard_map/jvp(thd,shd->hts)/dot_general | solution.py:38
  76.0 7.2 %fusion.67 = f32[256,2048]{0,1:T(8,128)} fusion(bf16[256,2048]{1,0:T(8,128)(2,1)S(1)} %copy-done, bf16[2048,2048]{1,0:T(8,128)(2,1)} %param.12), kind=kOutput, calls=%fused_computation.80 | convolution fusion | flops 2147483648 | bytes 11534336 | tf_op jit(solution)/shard_map/transpose(jvp())/reshape | solution.py:44
  83.2 129.2 %all-gather.6.cloned.1.call-done = f32[512,128,128]{2,1,0:T(8,128)} async-done(((f32[16,128,128]{2,1,0:T(8,128)}), f32[512,128,128]{2,1,0:T(8,128)}) %all-gather.6.cloned.1.call-update) | async-done | bytes 33554448 | tf_op jit(solution)/shard_map/all_gather | solution.py:14
  212.4 0.1 broadcast_in_dim.33.clone
  212.5 0.5 while.26
  213.0 3.6 fusion.63
  216.6 5.5 fusion.24
  222.2 4.5 fusion.61
  226.7 4.3 divide_convert_fusion
  231.0 8.1 %fusion.68 = f32[2048,2048]{1,0:T(8,128)} fusion(bf16[256,2048]{0,1:T(8,128)(2,1)S(1)} %bitcast.163, bf16[256,2048]{1,0:T(8,128)(2,1)S(1)} %copy-done), kind=kOutput, calls=%fused_computation.81 | convolution fusion | flops 2147483648 | bytes 18874368 | tf_op jit(solution)/shard_map/dot_general | solution.py:78
  239.1 1.2 copy-done.9
  240.3 3.8 fusion.26
  244.2 4.1 fusion.1
  248.2 3.1 fusion.19
  251.4 1.4 copy.52
  252.8 0.5 copy-done.6
  253.3 2.5 fusion.51
  255.8 107.7 %all-gather.2 = f32[512,128]{1,0:T(8,128)S(1)} all-gather(f32[16,128]{1,0:T(8,128)S(1)} %bitcast.171), channel_id=4, replica_groups=mesh['groups'=1,'seq'=32] {'seq'}, dimensions={0}, use_global_device_ids=true | all-gather | bytes 270336 | tf_op jit(solution)/shard_map/all_gather | solution.py:14
  363.4 9.3 %fusion = f32[16,256,128]{1,2,0:T(8,128)} fusion(f32[16,256,256]{1,2,0:T(8,128)} %copy-done.7, f32[16,256]{1,0:T(8,128)S(1)} %get-tuple-element.160, f32[256,256]{0,1:T(8,128)S(1)} %fusion.49, f32[256,16,128]{0,2,1:T(8,128)S(1)} %bitcast.161), kind=kOutput, calls=%fused_computation.7 | convolution fusion | flops 1614807040 | bytes 8667136 | tf_op jit(solution)/shard_map/transpose(jvp(thd,shd->hts))/dot_general | solution.py:38
  372.8 5.8 fusion.2
  378.6 107.3 %all-gather.8.cloned.1.call-done = f32[512,128,128]{2,1,0:T(8,128)} async-done(((f32[16,128,128]{2,1,0:T(8,128)}), f32[512,128,128]{2,1,0:T(8,128)}) %all-gather.8.cloned.1.call-update) | async-done | bytes 33554448 | tf_op jit(solution)/shard_map/all_gather | solution.py:14
  485.9 0.1 broadcast_in_dim.33
  486.0 48.1 %while.27 = (s32[]{:T(128)}, f32[16,128,128]{2,1,0:T(8,128)S(1)}, f32[16,128]{1,0:T(8,128)S(1)}, s32[]{:T(128)}, f32[32,16,128,128]{3,2,1,0:T(8,128)}, /*index=5...) while((s32[]{:T(128)}, f32[16,128,128]{2,1,0:T(8,128)S(1)}, ...), condition=%wide.region_6.7_spmd, body=%wide.region_5.6_spmd.sunk | while | flops 264198 | bytes 3170467 | solution.py:23
  486.1 1.5 bitcast_add_fusion.12
  487.6 1.5 bitcast_add_fusion.12
  489.1 1.5 bitcast_add_fusion.12
  490.7 1.5 bitcast_add_fusion.12
  492.2 1.7 bitcast_add_fusion.12
  493.9 1.5 bitcast_add_fusion.12
  495.4 1.5 bitcast_add_fusion.12
  496.9 1.5 bitcast_add_fusion.12
  498.5 1.5 bitcast_add_fusion.12
  500.0 1.5 bitcast_add_fusion.12
  501.6 1.5 bitcast_add_fusion.12
  503.1 1.5 bitcast_add_fusion.12
  504.7 1.5 bitcast_add_fusion.12
  506.2 1.5 bitcast_add_fusion.12
  507.8 1.5 bitcast_add_fusion.12
  509.3 1.5 bitcast_add_fusion.12
  510.8 1.5 bitcast_add_fusion.12
  512.4 1.5 bitcast_add_fusion.12
  513.9 1.5 bitcast_add_fusion.12
  515.5 1.5 bitcast_add_fusion.12
  517.0 1.5 bitcast_add_fusion.12
  518.6 1.5 bitcast_add_fusion.12
  520.1 1.5 bitcast_add_fusion.12
  521.6 1.5 bitcast_add_fusion.12
  523.2 1.5 bitcast_add_fusion.12
  524.7 1.5 bitcast_add_fusion.12
  526.3 1.5 bitcast_add_fusion.12
  527.8 1.5 bitcast_add_fusion.12
  529.4 1.5 bitcast_add_fusion.12
  530.9 1.5 bitcast_add_fusion.12
  532.5 1.5 bitcast_add_fusion.12
  534.2 5.0 add_convert_fusion
  539.2 1.4 copy.54
  540.6 5.1 fusion.11
  545.7 1.4 copy.53
  547.2 122.6 %reduce-scatter.2.cloned.1.call-done = f32[64,2048]{1,0:T(8,128)} async-done(((f32[2048,2048]{1,0:T(8,128)}), f32[64,2048]{1,0:T(8,128)}) %reduce-scatter.2.cloned.1.call-update) | async-done | bytes 524304 | tf_op jit(solution)/shard_map/reduce_scatter | solution.py:77
  (68 shorter events, 0.5 us)
Async XLA Ops:
  7.2 68.8 %copy-start = (bf16[256,2048]{1,0:T(8,128)(2,1)S(1)}, bf16[256,2048]{1,0:T(8,128)(2,1)}, u32[]{:S(2)}) copy-start(bf16[256,2048]{1,0:T(8,128)(2,1)} %param.13) | copy-start | bytes 3145732
  7.2 205.2 %all-gather.6.cloned.1.call-start = ((), (), s32[]{:S(2)}) async-start(), calls=%async_computation.2 | async-start | bytes 34603008 | tf_op jit(solution)/shard_map/all_gather | solution.py:14
  8.8 57.8 %copy-start.2 = (f32[256,2048]{0,1:T(8,128)}, f32[256,2048]{0,1:T(8,128)S(1)}, u32[]{:S(2)}) copy-start(f32[256,2048]{0,1:T(8,128)S(1)} %copy.33) | copy-start | bytes 6291460
  13.7 472.2 %all-gather.8.cloned.1.call-start = ((), (), s32[]{:S(2)}) async-start(), calls=%async_computation.3 | async-start | bytes 34603008 | tf_op jit(solution)/shard_map/all_gather | solution.py:14
  212.9 3.7 copy-start.4
  222.1 447.7 %reduce-scatter.2.cloned.1.call-start = ((), (), s32[]{:S(2)}) async-start(), calls=%async_computation.1 | async-start | bytes 17301504 | tf_op jit(solution)/shard_map/reduce_scatter | solution.py:77
  222.2 4.5 copy-start.8
  222.2 4.5 copy-start.10
  239.1 1.2 copy-start.9
  240.3 3.8 copy-start.3
  244.1 4.1 copy-start.7
  244.1 4.1 copy-start.5
  244.1 4.1 copy-start.12
  251.4 2.0 copy-start.6
  363.4 9.3 %copy-start.11 = (f32[16,256,256]{1,2,0:T(8,128)S(1)}, f32[16,256,256]{1,2,0:T(8,128)}, u32[]{:S(2)}) copy-start(f32[16,256,256]{1,2,0:T(8,128)} %get-tuple-element.162) | copy-start | bytes 12582916
  363.4 9.3 %copy-start.13 = (f32[256,2048]{0,1:T(8,128)S(1)}, f32[256,2048]{0,1:T(8,128)}, u32[]{:S(2)}) copy-start(f32[256,2048]{0,1:T(8,128)} %fusion.67) | copy-start | bytes 6291460
  540.6 129.2 %copy-start.1 = (bf16[256,2048]{1,0:T(8,128)(2,1)S(1)}, bf16[256,2048]{1,0:T(8,128)(2,1)}, u32[]{:S(2)}) copy-start(bf16[256,2048]{1,0:T(8,128)(2,1)} %param.13) | copy-start | bytes 3145732
Sparse Core Ops, SparseCore 0:
  13.8 198.4 all-gather.5
  222.2 263.6 all-gather.7
  488.8 180.9 reduce-scatter.1
where the time goes:
time: 687 us; the launch traced here: 677 us
  waiting for transfers between devices  359 us (52%)
  blocking collectives  156 us (23%)
  matrix products  86.2 us (13%)
  other arithmetic  49.2 us (7%)
  between operations  14.2 us (2%)
  local copies, waits for them, and re-layouts  10.4 us (2%)
    all_gather x2, waiting for transfers between devices, entering(): gathered = jax.tree.map(lambda a: lax.all_gather(a, axis), part)  237 us
    all_gather x2, blocking collectives, entering(): gathered = jax.tree.map(lambda a: lax.all_gather(a, axis), part)  156 us
    reduce_scatter x1, waiting for transfers between devices, body(): lax.psum_scatter(lax.dot_general(rounded, out_grad, (((0,), (0,)), ((), (...  123 us
    add x62, other arithmetic, add_pair(): return (earlier[0] + later[0], earlier[1] + later[1])  47 us
    dot_general x3, matrix products, attend_block(): jnp.einsum('thd,shd->hts', fq, fk, precision=lax.Precision.HIGHEST)  22.8 us
    dot_general x3, matrix products, summarize(): state = jnp.einsum('thd,the->hde', fk, vv, precision=lax.Precision.HIGHEST)  15 us
    dot_general x3, matrix products, attend_block(): jnp.einsum('hts,she->the', scores, vv, precision=lax.Precision.HIGHEST)  13.9 us
  transfers between devices with their start and end apart: 3, of which 3 were waited for; matrix products, arithmetic and copies ran while one was open for 19% of the time, Pallas kernels for 0%

commit v1 on v0

v1 whole, which is shorter than its diff:
```python
import functools

import jax
import jax.numpy as jnp
from jax import lax
from jax.experimental import pallas as pl
from jax.experimental.pallas import tpu as pltpu
from jax.sharding import PartitionSpec as P

HEADS = 16
HEAD = 128
HALF = HEAD // 2
ROWS = HEAD + 8
F32 = jnp.float32
BF16 = jnp.bfloat16
NN = (((1,), (0,)), ((), ()))
NT = (((1,), (1,)), ((), ()))
TN = (((0,), (0,)), ((), ()))
PARTS = ((0, 768, (0, 1, 2, 3)), (768, 768, (1, 0, 2, 3)), (1536, 512, (2, 0, 1, 3)))
VMEM_LIMIT = 40 * 1024 * 1024


def split(a):
    high = a.astype(BF16)
    return high, (a - high.astype(F32)).astype(BF16)


def mm(a, b, dims):
    out = lax.dot_general(a[0], b[0], dims, preferred_element_type=F32)
    if len(b) > 1:
        out = out + lax.dot_general(a[0], b[1], dims, preferred_element_type=F32)
    if len(a) > 1:
        out = out + lax.dot_general(a[1], b[0], dims, preferred_element_type=F32)
    return out


def feature(x):
    return jnp.where(x > 0, x + 1.0, jnp.exp(jnp.minimum(x, 0.0)))


def slope(x, f):
    return jnp.where(x > 0, 1.0, f)


def causal(t):
    rows = lax.broadcasted_iota(jnp.int32, (t, t), 0)
    cols = lax.broadcasted_iota(jnp.int32, (t, t), 1)
    return cols <= rows


def each_head(at_ref, one):
    me = at_ref[0]
    core, plane = me % 2, (me // 2) % 4

    def pair(turn, carry):
        place, r = turn // 2, turn % 2
        for side in range(2):
            head = (side ^ core) * 8 + (place ^ plane) * 2 + r
            one(side, place, r, head, pl.ds(pl.multiple_of(head * HEAD, HEAD), HEAD))
        return carry

    lax.fori_loop(0, HEADS // 2, pair, 0)


def put_state(ref, place, r, state, total):
    ref[place, r, :HEAD, :] = state
    first = lax.broadcasted_iota(jnp.int32, (8, HEAD), 0) == 0
    ref[place, r, HEAD:, :] = jnp.where(first, total, 0.0)


def summary_kernel(at_ref, k_ref, v_ref, keep_ref, send_ref):
    def one(side, place, r, head, cols):
        fk = feature(k_ref[:, cols].astype(F32))
        state = mm(split(fk), (v_ref[:, cols],), TN)
        put_state((keep_ref, send_ref)[side], place, r, state, jnp.sum(fk, axis=0, keepdims=True))

    each_head(at_ref, one)


def attend(q, k, v, state, total):
    fq, fk = feature(q.astype(F32)), feature(k.astype(F32))
    fqs, fks = split(fq), split(fk)
    scores = jnp.where(causal(q.shape[0]), mm(fqs, fks, NT), 0.0)
    ss, states = split(scores), split(state)
    numer = mm(ss, (v,), NN) + mm(fqs, states, NN)
    denom = jnp.sum(scores, axis=1, keepdims=True) + jnp.sum(fq * total, axis=1, keepdims=True)
    inv = 1.0 / denom
    return fq, fk, fqs, fks, ss, states, inv, numer * inv


def forward_kernel(at_ref, q_ref, k_ref, v_ref, s0_ref, s1_ref, keep_ref, send_ref):
    me = at_ref[0]
    core, chip = me % 2, me // 2

    def one(side, place, r, head, cols):
        s_ref = (s0_ref, s1_ref)[side]
        state, total = s_ref[place, r, :HEAD, :], s_ref[place, r, HEAD : HEAD + 1, :]
        att = attend(q_ref[:, cols], k_ref[:, cols], v_ref[:, cols], state, total)[-1]
        att = jnp.transpose(att)
        low, high = att[:HALF], att[HALF:]
        keep_ref[head ^ chip] = jnp.where(core == 0, low, high)
        send_ref[head ^ chip] = jnp.where(core == 0, high, low)

    each_head(at_ref, one)


def backward_kernel(
    at_ref, q_ref, k_ref, v_ref, g_ref, s0_ref, s1_ref, qg_ref, dk_ref, dv_ref, keep_ref, send_ref
):
    def one(side, place, r, head, cols):
        s_ref = (s0_ref, s1_ref)[side]
        state, total = s_ref[place, r, :HEAD, :], s_ref[place, r, HEAD : HEAD + 1, :]
        q, v, g = q_ref[:, cols], v_ref[:, cols], g_ref[:, cols]
        fq, fk, fqs, fks, ss, states, inv, att = attend(q, k_ref[:, cols], v, state, total)
        dn = g * inv
        dd = -jnp.sum(g * att, axis=1, keepdims=True) * inv
        dns = split(dn)
        ds = split(jnp.where(causal(q.shape[0]), mm(dns, (v,), NT) + dd, 0.0))
        dfq = mm(ds, fks, NN) + mm(dns, states, NT) + dd * total
        qg_ref[:, cols] = (dfq * slope(q.astype(F32), fq)).astype(BF16)
        dk_ref[:, cols] = mm(ds, fqs, TN)
        dv_ref[:, cols] = mm(ss, dns, TN)
        put_state(
            (keep_ref, send_ref)[side], place, r, mm(fqs, dns, TN), jnp.sum(fq * dd, axis=0, keepdims=True)
        )

    each_head(at_ref, one)


def finish_kernel(at_ref, k_ref, v_ref, dk_ref, dv_ref, s0_ref, s1_ref, kg_ref, vg_ref):
    def one(side, place, r, head, cols):
        s_ref = (s0_ref, s1_ref)[side]
        states, total = split(s_ref[place, r, :HEAD, :]), s_ref[place, r, HEAD : HEAD + 1, :]
        k = k_ref[:, cols].astype(F32)
        fk = feature(k)
        dfk = dk_ref[:, cols] + mm((v_ref[:, cols],), states, NT) + total
        kg_ref[:, cols] = (dfk * slope(k, fk)).astype(BF16)
        vg_ref[:, cols] = (dv_ref[:, cols] + mm(split(fk), states, NN)).astype(BF16)

    each_head(at_ref, one)


def weight_kernel(bit_set, a0_ref, a1_ref, g0_ref, g1_ref, *refs):
    outs, (a_ref, g_ref) = refs[:-2], refs[-2:]
    t = g0_ref.shape[0]
    a_ref[:, :, :t] = a0_ref[...].astype(BF16)
    a_ref[:, :, t:] = a1_ref[...].astype(BF16)
    g_ref[:t, :] = g0_ref[...]
    g_ref[t:, :] = g1_ref[...].astype(BF16)
    for out_ref, (start, width, order) in zip(outs, PARTS, strict=True):
        rels = [rel for rel in range(HEADS) if (rel >> order[0]) & 1 == bit_set]
        lhs = jnp.concatenate([a_ref[rel] for rel in rels], axis=0)
        for at in range(0, width, 256):
            got = jnp.dot(lhs, g_ref[:, start + at : start + at + 256], preferred_element_type=F32)
            out_ref[:, :, at : at + 256] = got.reshape(len(rels), HALF, 256)


def call(kernel, outs, flops, *args, scratch=()):
    moved = sum(a.size * a.dtype.itemsize for a in args) + sum(
        jnp.dtype(o.dtype).itemsize * o.size for o in outs
    )
    specs = [pl.BlockSpec(memory_space=pltpu.SMEM if a.size == 1 else pltpu.VMEM) for a in args]
    return pl.pallas_call(
        kernel,
        out_shape=tuple(outs),
        in_specs=specs,
        out_specs=tuple(pl.BlockSpec(memory_space=pltpu.VMEM) for _ in outs),
        scratch_shapes=list(scratch),
        compiler_params=pltpu.CompilerParams(vmem_limit_bytes=VMEM_LIMIT),
        cost_estimate=pl.CostEstimate(flops=flops, bytes_accessed=moved, transcendentals=0),
    )(*args)


def swap(x, mask):
    n = lax.axis_size("seq")
    return lax.ppermute(x, "seq", [(i, i ^ mask) for i in range(n)])


def entering(keep, send, me, later):
    n = lax.axis_size("seq")
    core, plane = me % 2, (me // 2) % 4
    own, mate = keep, swap(send, 1)
    total = own + mate
    got = [total[0]] + [swap(total[j], 2 * j) for j in range(1, 4)]
    layer = got[0] + got[1] + got[2] + got[3]
    outer = jnp.zeros_like(layer)
    for k in range(1, n // 8):
        pairs = [(i, i + 8 * k) for i in range(n - 8 * k)]
        if later:
            pairs = [(b, a) for a, b in pairs]
        outer = outer + lax.ppermute(layer, "seq", pairs)
    back = []
    for j in range(4):
        x = outer
        for i in range(4):
            if i != j:
                ahead = (plane ^ i) > (plane ^ j) if later else (plane ^ i) < (plane ^ j)
                x = x + jnp.where(ahead, got[i], 0.0)
        back.append(swap(x, 2 * j) if j else x)
    back = jnp.stack(back)
    first = 1 if later else 0
    mine = back + jnp.where(core == first, 0.0, mate)
    other = back + jnp.where(core == first, own, 0.0)
    return mine, swap(other, 1)


def scatter_sum(keeps, sends):
    out = []
    for keep, send, (_, width, order) in zip(keeps, sends, PARTS, strict=True):
        left = sorted(order[1:], reverse=True)
        shape = (2,) * len(left) + (HALF, width)
        got, keep = swap(send, 2 << order[0]).reshape(shape), keep.reshape(shape)
        for bit in order[1:]:
            axis = left.index(bit)
            take = lambda a, i: lax.index_in_dim(a, i, axis, keepdims=False)
            send = take(keep, 1) + take(got, 1)
            keep = take(keep, 0) + take(got, 0)
            got = swap(send, 2 << bit)
            left.remove(bit)
        out.append(keep + got)
    return jnp.concatenate(out, axis=1)


def body(queries, keys, values, out_weight, out_grad):
    t = queries.shape[0]
    unit = 2 * t * t * HEAD * HEADS
    shape = jax.ShapeDtypeStruct
    me = lax.axis_index("seq")
    at = me.astype(jnp.int32).reshape(1)
    state_half = shape((4, 2, ROWS, HEAD), F32)
    wide = shape((t, HEADS * HEAD), F32)
    narrow = shape((t, HEADS * HEAD), BF16)

    grad_mate = swap(out_grad.astype(F32), 1)
    keep, send = call(summary_kernel, [state_half] * 2, unit, at, keys, values)
    s0, s1 = entering(keep, send, me, False)
    attended_grad = lax.dot_general(out_grad, out_weight, NT, preferred_element_type=F32)

    half = shape((HEADS, HALF, t), F32)
    a_keep, a_send = call(forward_kernel, [half] * 2, 7 * unit, at, queries, keys, values, s0, s1)
    a_mate = swap(a_send, 1)
    part_shapes = [shape((HEADS // 2, HALF, width), F32) for _, width, _ in PARTS]
    scratch = (
        pltpu.VMEM((HEADS, HALF, 2 * t), BF16),
        pltpu.VMEM((2 * t, out_grad.shape[1]), BF16),
    )
    weight = lambda bit: call(
        functools.partial(weight_kernel, bit),
        part_shapes,
        4 * unit,
        a_keep,
        a_mate,
        out_grad,
        grad_mate,
        scratch=scratch,
    )
    sends, keeps = weight(1), weight(0)
    query_grad, dk, dv, keep, send = call(
        backward_kernel,
        [narrow, wide, wide, state_half, state_half],
        21 * unit,
        at,
        queries,
        keys,
        values,
        attended_grad,
        s0,
        s1,
    )
    weight_grad = scatter_sum(keeps, sends)
    l0, l1 = entering(keep, send, me, True)
    key_grad, value_grad = call(
        finish_kernel, [narrow, narrow], 3 * unit, at, keys, values, dk, dv, l0, l1
    )
    return (query_grad, key_grad, value_grad, weight_grad)


def solution(mesh):
    placed = (
        P(("groups", "seq"), None),
        P(("groups", "seq"), None),
        P(("groups", "seq"), None),
        P(),
        P(("groups", "seq"), None),
    )
    return jax.shard_map(
        body,
        mesh=mesh,
        in_specs=placed,
        out_specs=(
            P(("groups", "seq"), None),
            P(("groups", "seq"), None),
            P(("groups", "seq"), None),
            P(("groups", "seq"), None),
        ),
        check_vma=False,
    )
```

time: 687 us -> 218 us (0.32); the launches traced: 677 us -> 218 us
  waiting for transfers between devices: 359 us -> 93.1 us
  blocking collectives: 156 us -> 0 us
  matrix products: 86.2 us -> 5.89 us
  starting transfers between devices: 0.12 us -> 57.9 us
  Pallas kernels: 0 us -> 37.3 us
  other arithmetic: 49.2 us -> 15.4 us
  between operations: 14.2 us -> 1.1 us
    all_gather x2 -> x0, waiting for transfers between devices: 237 us -> none  [entering(): gathered = jax.tree.map(lambda a: lax.all_gather(a, axis), part)]
    all_gather x2 -> x0, blocking collectives: 156 us -> none  [entering(): gathered = jax.tree.map(lambda a: lax.all_gather(a, axis), part)]
    reduce_scatter x1 -> x0, waiting for transfers between devices: 123 us -> none  [body(): lax.psum_scatter(lax.dot_general(rounded, out_grad, (((0,), (0,)), ((), (...]
    ppermute x0 -> x36, waiting for transfers between devices: none -> 93.1 us  [the longest x30 88.6 us: swap(): return lax.ppermute(x, 'seq', [(i, i ^ mask) for i in range(n)])]
    dot_general x15 -> x1, matrix products: 79 us -> 5.89 us  [body(): lax.dot_general(out_grad, out_weight, NT, preferred_element_type=F32)]
    ppermute x0 -> x36, starting transfers between devices: none -> 57.9 us  [the longest x30 44.6 us: swap(): return lax.ppermute(x, 'seq', [(i, i ^ mask) for i in range(n)])]
    pallas_call x0 -> x6, Pallas kernels: none -> 37.3 us  [call(): pl.pallas_call(kernel, out_shape=tuple(outs), in_specs=specs, out_specs=t...]
    add x62 -> x20, other arithmetic: 47 us -> 11.1 us  [the longest x6 4.96 us: scatter_sum(): keep = take(keep, 0) + take(got, 0)]
  transfers between devices with their start and end apart: 3 -> 36, of which waited for: 3 -> 19; matrix products, arithmetic and copies ran while one was open for 19% -> 9% of each run, Pallas kernels for 0% -> 16%
where the time goes in v1:
time: 218 us
  waiting for transfers between devices  93.1 us (43%)
  starting transfers between devices  57.9 us (27%)
  Pallas kernels  37.3 us (17%)
  other arithmetic  15.4 us (7%)
  local copies, waits for them, and re-layouts  6.77 us (3%)
  matrix products  5.89 us (3%)
    ppermute x30, waiting for transfers between devices, swap(): return lax.ppermute(x, 'seq', [(i, i ^ mask) for i in range(n)])  88.6 us
    ppermute x30, starting transfers between devices, swap(): return lax.ppermute(x, 'seq', [(i, i ^ mask) for i in range(n)])  44.6 us
    pallas_call x6, Pallas kernels, call(): pl.pallas_call(kernel, out_shape=tuple(outs), in_specs=specs, out_specs=t...  37.3 us
    ppermute x6, starting transfers between devices, entering(): outer = outer + lax.ppermute(layer, 'seq', pairs)  13.3 us
    unnamed x48, local copies, waits for them, and re-layouts  6.72 us
    dot_general x1, matrix products, body(): lax.dot_general(out_grad, out_weight, NT, preferred_element_type=F32)  5.89 us
    add x6, other arithmetic, scatter_sum(): keep = take(keep, 0) + take(got, 0)  4.96 us
    ppermute x6, waiting for transfers between devices, entering(): outer = outer + lax.ppermute(layer, 'seq', pairs)  4.42 us
  transfers between devices with their start and end apart: 36, of which 19 were waited for; matrix products, arithmetic and copies ran while one was open for 9% of the time, Pallas kernels for 16%

profile of v1, /device:TPU:0, one launch (start us, length us, event | category | flops | bytes accessed | tf_op | source)
XLA Modules:
  0.0 217.6 jit_solution(11620189241644113399)
XLA Ops:
  0.6 1.2 copy-done.5
  1.9 1.2 copy-done.8
  3.1 2.4 %shard_map.84 = (f32[4,2,136,128]{3,2,1,0:T(8,128)S(1)}, f32[4,2,136,128]{3,2,1,0:T(8,128)S(1)}) custom-call(s32[1]{0:T(128)} %bitcast.at_ref, bf16[256,2048]{1,0:T(8,128)(2,1)S(1)} %copy-done.5, bf16[256,2048]{1,0:T(8,128)(2,1)S(1)} %copy-done.8), custom_call_target="tpu_custom_call" | custom-call | flops 268435456 | bytes 3211268 | tf_op jit(solution)/shard_map/pallas_call | solution.py:163
  6.1 1.6 collective-permute-done
  7.7 0.7 copy-done.21
  8.5 2.9 %collective-permute-start.1 = (f32[2,136,128]{2,1,0:T(8,128)S(1)}, f32[2,136,128]{2,1,0:T(8,128)S(1)}, u32[]{:S(2)}, u32[]{:S(2)}) collective-permute-start(f32[2,136,128]{2,1,0:T(8,128)S(1)} %get-tuple-element.69), channel_id=1, source_target_pairs={{0,2},{1,3},{2,0},{3,1},{4,6},{5,7},{6,4},{7,5},{8,10},{9,11},{10,... | collective-permute-start | bytes 417800 | tf_op jit(solution)/shard_map/ppermute | solution.py:176
  11.4 1.5 collective-permute-start.2
  13.0 2.7 %collective-permute-done.1 = f32[2,136,128]{2,1,0:T(8,128)S(1)} collective-permute-done((f32[2,136,128]{2,1,0:T(8,128)S(1)}, f32[2,136,128]{2,1,0:T(8,128)S(1)}, u32[]{:S(2)}, u32[]{:S(2)}) %collective-permute-start.1) | collective-permute-done | bytes 139296 | tf_op jit(solution)/shard_map/ppermute | solution.py:176
  15.7 4.2 %collective-permute-done.2 = f32[2,136,128]{2,1,0:T(8,128)S(1)} collective-permute-done((f32[2,136,128]{2,1,0:T(8,128)S(1)}, f32[2,136,128]{2,1,0:T(8,128)S(1)}, u32[]{:S(2)}, u32[]{:S(2)}) %collective-permute-start.2) | collective-permute-done | bytes 139296 | tf_op jit(solution)/shard_map/ppermute | solution.py:176
  19.9 3.5 %collective-permute-start.4 = (f32[2,136,128]{2,1,0:T(8,128)S(1)}, f32[2,136,128]{2,1,0:T(8,128)S(1)}, u32[]{:S(2)}, u32[]{:S(2)}) collective-permute-start(f32[2,136,128]{2,1,0:T(8,128)S(1)} %add_add_fusion.3), channel_id=1, source_target_pairs={{0,8},{1,9},{2,10},{3,11},{4,12},{5,13},{6,14},{7,15},{8,16},{9,17... | collective-permute-start | bytes 417800 | tf_op jit(solution)/shard_map/ppermute | solution.py:191
  23.4 4.5 %collective-permute-start.5 = (f32[2,136,128]{2,1,0:T(8,128)S(1)}, f32[2,136,128]{2,1,0:T(8,128)S(1)}, u32[]{:S(2)}, u32[]{:S(2)}) collective-permute-start(f32[2,136,128]{2,1,0:T(8,128)S(1)} %add_add_fusion.3), channel_id=1, source_target_pairs={{0,16},{1,17},{2,18},{3,19},{4,20},{5,21},{6,22},{7,23},{8,24},{9,... | collective-permute-start | bytes 417800 | tf_op jit(solution)/shard_map/ppermute | solution.py:191
  27.9 1.3 collective-permute-start.6
  29.2 1.9 collective-permute-done.5
  31.2 1.5 collective-permute-done.6
  32.7 0.8 select_add_fusion.9
  33.5 1.6 collective-permute-start.7
  35.7 1.4 collective-permute-start.9
  37.0 1.6 convert_element_type.3
  38.6 1.3 collective-permute-done.7
  40.5 1.5 collective-permute-done.9
  42.0 1.3 select_add_fusion.2
  43.3 5.9 %fusion.24.g_ref = f32[256,2048]{1,0:T(8,128)S(1)} fusion(bf16[256,2048]{1,0:T(8,128)(2,1)S(1)} %copy-done, bf16[2048,2048]{1,0:T(8,128)(2,1)} %param.8), kind=kOutput, calls=%fused_computation.81 | convolution fusion | flops 2147483648 | bytes 11534336 | tf_op jit(solution)/shard_map/dot_general | solution.py:237
  49.3 19.8 %shard_map.85 = (bf16[256,2048]{1,0:T(8,128)(2,1)}, f32[256,2048]{1,0:T(8,128)S(1)}, f32[256,2048]{1,0:T(8,128)S(1)}, f32[4,2,136,128]{3,2,1,0:T(8,128)S(1)}, f32[4,2,136,128]{3,2,1,0:T(8,128)S(1)}) custom-call(s32[1]{0:T(128)} %bitcast.at_ref, bf16[256,2048]{1,0:T(8,128)(2,1)S(1)} %copy-done.18, bf16[256,2048]{1,0:T(8,128)(2,1)S(1)} %copy-done.6, ...), custom_call_target="tpu_custom_call" | custom-call | flops 5637144576 | bytes 12713988 | tf_op jit(solution)/shard_map/pallas_call | solution.py:163
  69.1 1.3 copy-done.13
  70.7 7.9 %shard_map.87 = (f32[16,64,256]{2,1,0:T(8,128)S(1)}, f32[16,64,256]{2,1,0:T(8,128)S(1)}) custom-call(s32[1]{0:T(128)} %bitcast.at_ref, bf16[256,2048]{1,0:T(8,128)(2,1)S(1)} %copy-done.18, bf16[256,2048]{1,0:T(8,128)(2,1)S(1)} %copy-done.6, bf16[256,2048]{1,0:T(8,128)(2,1)S(1)} %copy-done.9, f32[4,2,136,128]{3,2,1,0:T(8,128)S(1)} %get-tuple-element.66.s0_ref, ...), custom_call_target="tpu_custom_call" | custom-call | flops 1879048192 | bytes 6356996 | tf_op jit(solution)/shard_map/pallas_call | solution.py:163
  79.0 1.4 collective-permute-start.12
  81.0 1.5 collective-permute-start.14
  82.5 3.0 %collective-permute-done.12 = f32[2,136,128]{2,1,0:T(8,128)S(1)} collective-permute-done((f32[2,136,128]{2,1,0:T(8,128)S(1)}, f32[2,136,128]{2,1,0:T(8,128)S(1)}, u32[]{:S(2)}, u32[]{:S(2)}) %collective-permute-start.12) | collective-permute-done | bytes 139296 | tf_op jit(solution)/shard_map/ppermute | solution.py:176
  85.5 3.5 %collective-permute-done.13 = f32[2,136,128]{2,1,0:T(8,128)S(1)} collective-permute-done((f32[2,136,128]{2,1,0:T(8,128)S(1)}, f32[2,136,128]{2,1,0:T(8,128)S(1)}, u32[]{:S(2)}, u32[]{:S(2)}) %collective-permute-start.13) | collective-permute-done | bytes 139296 | tf_op jit(solution)/shard_map/ppermute | solution.py:176
  89.1 0.7 add_add_fusion.1
  89.8 1.3 collective-permute-start.15
  91.1 1.3 collective-permute-start.16
  92.4 1.5 collective-permute-start.17
  93.9 1.9 shard_map.89
  95.8 1.2 copy-done.17
  97.0 1.0 copy-done.19
  98.6 1.4 collective-permute-start.28
  100.0 8.5 %collective-permute-start.32 = (f32[8,64,512]{2,1,0:T(8,128)}, f32[8,64,512]{2,1,0:T(8,128)}, u32[]{:S(2)}, u32[]{:S(2)}) collective-permute-start(f32[8,64,512]{2,1,0:T(8,128)} %copy-done.19), channel_id=1, source_target_pairs={{0,8},{1,9},{2,10},{3,11},{4,12},{5,13},{6,14},{7,15},{8,0},{9,1},... | collective-permute-start | bytes 3145736 | tf_op jit(solution)/shard_map/ppermute | solution.py:176
  108.6 1.0 collective-permute-done.16
  109.6 1.8 add_bitcast_fusion
  111.4 1.8 select_add_fusion.6
  113.2 0.9 collective-permute-start.18
  114.1 1.0 collective-permute-start.19
  115.1 21.7 %collective-permute-done.18 = f32[2,136,128]{2,1,0:T(8,128)S(1)} collective-permute-done((f32[2,136,128]{2,1,0:T(8,128)S(1)}, f32[2,136,128]{2,1,0:T(8,128)S(1)}, u32[]{:S(2)}, u32[]{:S(2)}) %collective-permute-start.18) | collective-permute-done | bytes 139296 | tf_op jit(solution)/shard_map/ppermute | solution.py:176
  136.8 1.4 collective-permute-start.20
  138.2 4.9 %collective-permute-done.20 = f32[2,136,128]{2,1,0:T(8,128)} collective-permute-done((f32[2,136,128]{2,1,0:T(8,128)}, f32[2,136,128]{2,1,0:T(8,128)}, u32[]{:S(2)}, u32[]{:S(2)}) %collective-permute-start.20) | collective-permute-done | bytes 139296 | tf_op jit(solution)/shard_map/ppermute | solution.py:176
  143.1 1.3 select_add_fusion
  144.5 1.3 shard_map.88
  145.7 1.4 fusion.11
  147.7 1.6 fusion.7
  149.3 1.6 collective-permute-start.25
  150.8 1.7 fusion.3
  153.2 8.7 %collective-permute-done.33 = f32[2,2,64,512]{3,2,1,0:T(8,128)S(1)} collective-permute-done((f32[2,2,64,512]{3,2,1,0:T(8,128)S(1)}, f32[2,2,64,512]{3,2,1,0:T(8,128)S(1)}, u32[]{:S(2)}, u32[]{:S(2)}) %collective-permute-start.33) | collective-permute-done | bytes 524320 | tf_op jit(solution)/shard_map/ppermute | solution.py:176
  162.7 4.1 %shard_map.86 = (bf16[256,2048]{1,0:T(8,128)(2,1)}, bf16[256,2048]{1,0:T(8,128)(2,1)}) custom-call(s32[1]{0:T(128)} %bitcast.at_ref, bf16[256,2048]{1,0:T(8,128)(2,1)S(1)} %copy-done.7, bf16[256,2048]{1,0:T(8,128)(2,1)S(1)} %copy-done.10, f32[256,2048]{1,0:T(8,128)S(1)} %copy-done.14, f32[256,2048]{1,0:T(8,128)S(1)} %copy-done.16, ...), custom_call_target="tpu_custom_call" | custom-call | flops 805306368 | bytes 9502724 | tf_op jit(solution)/shard_map/pallas_call | solution.py:163
  166.8 7.8 %collective-permute-done.34 = f32[2,64,512]{2,1,0:T(8,128)S(1)} collective-permute-done((f32[2,64,512]{2,1,0:T(8,128)S(1)}, f32[2,64,512]{2,1,0:T(8,128)S(1)}, u32[]{:S(2)}, u32[]{:S(2)}) %collective-permute-start.34) | collective-permute-done | bytes 262176 | tf_op jit(solution)/shard_map/ppermute | solution.py:176
  174.6 7.0 %collective-permute-start.35 = (f32[64,512]{1,0:T(8,128)S(1)}, f32[64,512]{1,0:T(8,128)S(1)}, u32[]{:S(2)}, u32[]{:S(2)}) collective-permute-start(f32[64,512]{1,0:T(8,128)S(1)} %fusion.21), channel_id=1, source_target_pairs={{0,16},{1,17},{2,18},{3,19},{4,20},{5,21},{6,22},{7,23},{8,24},{9,... | collective-permute-start | bytes 393224 | tf_op jit(solution)/shard_map/ppermute | solution.py:176
  181.7 2.9 %collective-permute-start.26 = (f32[2,64,768]{2,1,0:T(8,128)S(1)}, f32[2,64,768]{2,1,0:T(8,128)S(1)}, u32[]{:S(2)}, u32[]{:S(2)}) collective-permute-start(f32[2,64,768]{2,1,0:T(8,128)S(1)} %get-tuple-element.49), channel_id=1, source_target_pairs={{0,8},{1,9},{2,10},{3,11},{4,12},{5,13},{6,14},{7,15},{8,0},{9,1},... | collective-permute-start | bytes 1179656 | tf_op jit(solution)/shard_map/ppermute | solution.py:176
  184.8 1.8 collective-permute-done.35
  186.6 8.2 %collective-permute-done.26 = f32[2,64,768]{2,1,0:T(8,128)S(1)} collective-permute-done((f32[2,64,768]{2,1,0:T(8,128)S(1)}, f32[2,64,768]{2,1,0:T(8,128)S(1)}, u32[]{:S(2)}, u32[]{:S(2)}) %collective-permute-start.26) | collective-permute-done | bytes 393248 | tf_op jit(solution)/shard_map/ppermute | solution.py:176
  194.9 2.5 %collective-permute-start.27 = (f32[64,768]{1,0:T(8,128)S(1)}, f32[64,768]{1,0:T(8,128)S(1)}, u32[]{:S(2)}, u32[]{:S(2)}) collective-permute-start(f32[64,768]{1,0:T(8,128)S(1)} %fusion.18), channel_id=1, source_target_pairs={{0,16},{1,17},{2,18},{3,19},{4,20},{5,21},{6,22},{7,23},{8,24},{9,... | collective-permute-start | bytes 589832 | tf_op jit(solution)/shard_map/ppermute | solution.py:176
  197.4 8.7 %collective-permute-done.30 = f32[2,64,768]{2,1,0:T(8,128)S(1)} collective-permute-done((f32[2,64,768]{2,1,0:T(8,128)S(1)}, f32[2,64,768]{2,1,0:T(8,128)S(1)}, u32[]{:S(2)}, u32[]{:S(2)}) %collective-permute-start.30) | collective-permute-done | bytes 393248 | tf_op jit(solution)/shard_map/ppermute | solution.py:176
  206.1 2.0 collective-permute-start.31
  208.2 8.5 %collective-permute-done.31 = f32[64,768]{1,0:T(8,128)S(1)} collective-permute-done((f32[64,768]{1,0:T(8,128)S(1)}, f32[64,768]{1,0:T(8,128)S(1)}, u32[]{:S(2)}, u32[]{:S(2)}) %collective-permute-start.31) | collective-permute-done | bytes 196640 | tf_op jit(solution)/shard_map/ppermute | solution.py:176
  216.7 0.8 pad_maximum_fusion.2
  (89 shorter events, 6.4 us)
Async XLA Ops:
  0.6 1.2 copy-start.5
  1.9 1.2 copy-start.8
  5.5 2.1 copy-start.11
  5.5 2.1 collective-permute-start
  7.6 0.8 copy-start.21
  8.5 28.6 %copy-start = (bf16[256,2048]{1,0:T(8,128)(2,1)S(1)}, bf16[256,2048]{1,0:T(8,128)(2,1)}, u32[]{:S(2)}) copy-start(bf16[256,2048]{1,0:T(8,128)(2,1)} %g0_ref.3) | copy-start | bytes 3145732
  8.5 7.2 %collective-permute-start.1 = (f32[2,136,128]{2,1,0:T(8,128)S(1)}, f32[2,136,128]{2,1,0:T(8,128)S(1)}, u32[]{:S(2)}, u32[]{:S(2)}) collective-permute-start(f32[2,136,128]{2,1,0:T(8,128)S(1)} %get-tuple-element.69), channel_id=1, source_target_pairs={{0,2},{1,3},{2,0},{3,1},{4,6},{5,7},{6,4},{7,5},{8,10},{9,11},{10,... | collective-permute-start | bytes 417800 | tf_op jit(solution)/shard_map/ppermute | solution.py:176
  11.4 8.4 %collective-permute-start.2 = (f32[2,136,128]{2,1,0:T(8,128)S(1)}, f32[2,136,128]{2,1,0:T(8,128)S(1)}, u32[]{:S(2)}, u32[]{:S(2)}) collective-permute-start(f32[2,136,128]{2,1,0:T(8,128)S(1)} %get-tuple-element.68), channel_id=1, source_target_pairs={{0,4},{1,5},{2,6},{3,7},{4,0},{5,1},{6,2},{7,3},{8,12},{9,13},{10,... | collective-permute-start | bytes 417800 | tf_op jit(solution)/shard_map/ppermute | solution.py:176
  12.9 6.9 %collective-permute-start.3 = (f32[2,136,128]{2,1,0:T(8,128)S(1)}, f32[2,136,128]{2,1,0:T(8,128)S(1)}, u32[]{:S(2)}, u32[]{:S(2)}) collective-permute-start(f32[2,136,128]{2,1,0:T(8,128)S(1)} %get-tuple-element.67), channel_id=1, source_target_pairs={{0,6},{1,7},{2,4},{3,5},{4,2},{5,3},{6,0},{7,1},{8,14},{9,15},{10,... | collective-permute-start | bytes 417800 | tf_op jit(solution)/shard_map/ppermute | solution.py:176
  19.9 9.4 %collective-permute-start.4 = (f32[2,136,128]{2,1,0:T(8,128)S(1)}, f32[2,136,128]{2,1,0:T(8,128)S(1)}, u32[]{:S(2)}, u32[]{:S(2)}) collective-permute-start(f32[2,136,128]{2,1,0:T(8,128)S(1)} %add_add_fusion.3), channel_id=1, source_target_pairs={{0,8},{1,9},{2,10},{3,11},{4,12},{5,13},{6,14},{7,15},{8,16},{9,17... | collective-permute-start | bytes 417800 | tf_op jit(solution)/shard_map/ppermute | solution.py:191
  23.4 7.8 %collective-permute-start.5 = (f32[2,136,128]{2,1,0:T(8,128)S(1)}, f32[2,136,128]{2,1,0:T(8,128)S(1)}, u32[]{:S(2)}, u32[]{:S(2)}) collective-permute-start(f32[2,136,128]{2,1,0:T(8,128)S(1)} %add_add_fusion.3), channel_id=1, source_target_pairs={{0,16},{1,17},{2,18},{3,19},{4,20},{5,21},{6,22},{7,23},{8,24},{9,... | collective-permute-start | bytes 417800 | tf_op jit(solution)/shard_map/ppermute | solution.py:191
  27.9 4.8 %collective-permute-start.6 = (f32[2,136,128]{2,1,0:T(8,128)S(1)}, f32[2,136,128]{2,1,0:T(8,128)S(1)}, u32[]{:S(2)}, u32[]{:S(2)}) collective-permute-start(f32[2,136,128]{2,1,0:T(8,128)S(1)} %add_add_fusion.3), channel_id=1, source_target_pairs={{0,24},{1,25},{2,26},{3,27},{4,28},{5,29},{6,30},{7,31}} | collective-permute-start | bytes 417800 | tf_op jit(solution)/shard_map/ppermute | solution.py:191
  33.5 6.4 %collective-permute-start.7 = (f32[2,136,128]{2,1,0:T(8,128)}, f32[2,136,128]{2,1,0:T(8,128)S(1)}, u32[]{:S(2)}, u32[]{:S(2)}) collective-permute-start(f32[2,136,128]{2,1,0:T(8,128)} %get-tuple-element.57), channel_id=1, source_target_pairs={{0,2},{1,3},{2,0},{3,1},{4,6},{5,7},{6,4},{7,5},{8,10},{9,11},{10,... | collective-permute-start | bytes 417800 | tf_op jit(solution)/shard_map/ppermute | solution.py:176
  35.1 5.4 %collective-permute-start.8 = (f32[2,136,128]{2,1,0:T(8,128)}, f32[2,136,128]{2,1,0:T(8,128)}, u32[]{:S(2)}, u32[]{:S(2)}) collective-permute-start(f32[2,136,128]{2,1,0:T(8,128)} %get-tuple-element.59), channel_id=1, source_target_pairs={{0,4},{1,5},{2,6},{3,7},{4,0},{5,1},{6,2},{7,3},{8,12},{9,13},{10,... | collective-permute-start | bytes 417800 | tf_op jit(solution)/shard_map/ppermute | solution.py:176
  35.7 6.3 %collective-permute-start.9 = (f32[2,136,128]{2,1,0:T(8,128)}, f32[2,136,128]{2,1,0:T(8,128)}, u32[]{:S(2)}, u32[]{:S(2)}) collective-permute-start(f32[2,136,128]{2,1,0:T(8,128)} %get-tuple-element.58), channel_id=1, source_target_pairs={{0,6},{1,7},{2,4},{3,5},{4,2},{5,3},{6,0},{7,1},{8,14},{9,15},{10,... | collective-permute-start | bytes 417800 | tf_op jit(solution)/shard_map/ppermute | solution.py:176
  38.6 55.2 %collective-permute-start.23 = (f32[256,2048]{1,0:T(8,128)}, f32[256,2048]{1,0:T(8,128)S(1)}, u32[]{:S(2)}, u32[]{:S(2)}) collective-permute-start(f32[256,2048]{1,0:T(8,128)} %convert_element_type.3), channel_id=1, source_target_pairs={{0,1},{1,0},{2,3},{3,2},{4,5},{5,4},{6,7},{7,6},{8,9},{9,8},{10,11... | collective-permute-start | bytes 6291464 | tf_op jit(solution)/shard_map/ppermute | solution.py:176
  43.2 6.0 %copy-start.6 = (bf16[256,2048]{1,0:T(8,128)(2,1)S(1)}, bf16[256,2048]{1,0:T(8,128)(2,1)}, u32[]{:S(2)}) copy-start(bf16[256,2048]{1,0:T(8,128)(2,1)} %k_ref.7) | copy-start | bytes 3145732
  43.2 6.0 %copy-start.9 = (bf16[256,2048]{1,0:T(8,128)(2,1)S(1)}, bf16[256,2048]{1,0:T(8,128)(2,1)}, u32[]{:S(2)}) copy-start(bf16[256,2048]{1,0:T(8,128)(2,1)} %v_ref.7) | copy-start | bytes 3145732
  43.2 6.0 %copy-start.18 = (bf16[256,2048]{1,0:T(8,128)(2,1)S(1)}, bf16[256,2048]{1,0:T(8,128)(2,1)}, u32[]{:S(2)}) copy-start(bf16[256,2048]{1,0:T(8,128)(2,1)} %q_ref.3) | copy-start | bytes 3145732
  43.3 6.0 %collective-permute-start.10 = (f32[4,2,136,128]{3,2,1,0:T(8,128)S(1)}, f32[4,2,136,128]{3,2,1,0:T(8,128)S(1)}, u32[]{:S(2)}, u32[]{:S(2)}) collective-permute-start(f32[4,2,136,128]{3,2,1,0:T(8,128)S(1)} %get-tuple-element.65), channel_id=1, source_target_pairs={{0,1},{1,0},{2,3},{3,2},{4,5},{5,4},{6,7},{7,6},{8,9},{9,8},{10,11... | collective-permute-start | bytes 1671176 | tf_op jit(solution)/shard_map/ppermute | solution.py:176
  69.1 1.3 copy-start.13
  70.4 8.2 %copy-start.15 = (f32[256,2048]{1,0:T(8,128)}, f32[256,2048]{1,0:T(8,128)S(1)}, u32[]{:S(2)}) copy-start(f32[256,2048]{1,0:T(8,128)S(1)} %get-tuple-element.25.dv_ref) | copy-start | bytes 6291460
  70.4 8.5 %copy-start.12 = (f32[4,2,136,128]{3,2,1,0:T(8,128)}, f32[4,2,136,128]{3,2,1,0:T(8,128)S(1)}, u32[]{:S(2)}) copy-start(f32[4,2,136,128]{3,2,1,0:T(8,128)S(1)} %get-tuple-element.26) | copy-start | bytes 1671172
  70.4 8.5 %collective-permute-start.11 = (f32[4,2,136,128]{3,2,1,0:T(8,128)S(1)}, f32[4,2,136,128]{3,2,1,0:T(8,128)S(1)}, u32[]{:S(2)}, u32[]{:S(2)}) collective-permute-start(f32[4,2,136,128]{3,2,1,0:T(8,128)S(1)} %get-tuple-element.27), channel_id=1, source_target_pairs={{0,1},{1,0},{2,3},{3,2},{4,5},{5,4},{6,7},{7,6},{8,9},{9,8},{10,11... | collective-permute-start | bytes 1671176 | tf_op jit(solution)/shard_map/ppermute | solution.py:176
  78.6 17.2 %copy-start.1 = (f32[16,64,256]{2,1,0:T(8,128)}, f32[16,64,256]{2,1,0:T(8,128)S(1)}, u32[]{:S(2)}) copy-start(f32[16,64,256]{2,1,0:T(8,128)S(1)} %get-tuple-element.30.a0_ref) | copy-start | bytes 3145732
  78.6 15.2 %collective-permute-start.22 = (f32[16,64,256]{2,1,0:T(8,128)S(1)}, f32[16,64,256]{2,1,0:T(8,128)S(1)}, u32[]{:S(2)}, u32[]{:S(2)}) collective-permute-start(f32[16,64,256]{2,1,0:T(8,128)S(1)} %get-tuple-element.31), channel_id=1, source_target_pairs={{0,1},{1,0},{2,3},{3,2},{4,5},{5,4},{6,7},{7,6},{8,9},{9,8},{10,11... | collective-permute-start | bytes 3145736 | tf_op jit(solution)/shard_map/ppermute | solution.py:176
  78.9 16.9 %copy-start.22 = (f32[4,2,136,128]{3,2,1,0:T(8,128)}, f32[4,2,136,128]{3,2,1,0:T(8,128)S(1)}, u32[]{:S(2)}) copy-start(f32[4,2,136,128]{3,2,1,0:T(8,128)S(1)} %collective-permute-done.11) | copy-start | bytes 1671172
  78.9 14.9 %copy-start.20 = (f32[4,2,136,128]{3,2,1,0:T(8,128)}, f32[4,2,136,128]{3,2,1,0:T(8,128)S(1)}, u32[]{:S(2)}) copy-start(f32[4,2,136,128]{3,2,1,0:T(8,128)S(1)} %add.263) | copy-start | bytes 1671172
  79.0 6.6 %collective-permute-start.12 = (f32[2,136,128]{2,1,0:T(8,128)S(1)}, f32[2,136,128]{2,1,0:T(8,128)S(1)}, u32[]{:S(2)}, u32[]{:S(2)}) collective-permute-start(f32[2,136,128]{2,1,0:T(8,128)S(1)} %get-tuple-element.64), channel_id=1, source_target_pairs={{0,2},{1,3},{2,0},{3,1},{4,6},{5,7},{6,4},{7,5},{8,10},{9,11},{10,... | collective-permute-start | bytes 417800 | tf_op jit(solution)/shard_map/ppermute | solution.py:176
  80.4 8.6 %collective-permute-start.13 = (f32[2,136,128]{2,1,0:T(8,128)S(1)}, f32[2,136,128]{2,1,0:T(8,128)S(1)}, u32[]{:S(2)}, u32[]{:S(2)}) collective-permute-start(f32[2,136,128]{2,1,0:T(8,128)S(1)} %get-tuple-element.63), channel_id=1, source_target_pairs={{0,4},{1,5},{2,6},{3,7},{4,0},{5,1},{6,2},{7,3},{8,12},{9,13},{10,... | collective-permute-start | bytes 417800 | tf_op jit(solution)/shard_map/ppermute | solution.py:176
  81.0 8.0 %collective-permute-start.14 = (f32[2,136,128]{2,1,0:T(8,128)S(1)}, f32[2,136,128]{2,1,0:T(8,128)S(1)}, u32[]{:S(2)}, u32[]{:S(2)}) collective-permute-start(f32[2,136,128]{2,1,0:T(8,128)S(1)} %get-tuple-element.62), channel_id=1, source_target_pairs={{0,6},{1,7},{2,4},{3,5},{4,2},{5,3},{6,0},{7,1},{8,14},{9,15},{10,... | collective-permute-start | bytes 417800 | tf_op jit(solution)/shard_map/ppermute | solution.py:176
  89.1 4.8 %copy-start.23 = (f32[2,136,128]{2,1,0:T(8,128)}, f32[2,136,128]{2,1,0:T(8,128)S(1)}, u32[]{:S(2)}) copy-start(f32[2,136,128]{2,1,0:T(8,128)S(1)} %collective-permute-done.14) | copy-start | bytes 417796
  89.8 10.3 %collective-permute-start.15 = (f32[2,136,128]{2,1,0:T(8,128)}, f32[2,136,128]{2,1,0:T(8,128)}, u32[]{:S(2)}, u32[]{:S(2)}) collective-permute-start(f32[2,136,128]{2,1,0:T(8,128)} %add_add_fusion.1), channel_id=1, source_target_pairs={{8,0},{9,1},{10,2},{11,3},{12,4},{13,5},{14,6},{15,7},{16,8},{17,9... | collective-permute-start | bytes 417800 | tf_op jit(solution)/shard_map/ppermute | solution.py:191
  91.1 18.5 %collective-permute-start.16 = (f32[2,136,128]{2,1,0:T(8,128)}, f32[2,136,128]{2,1,0:T(8,128)}, u32[]{:S(2)}, u32[]{:S(2)}) collective-permute-start(f32[2,136,128]{2,1,0:T(8,128)} %add_add_fusion.1), channel_id=1, source_target_pairs={{16,0},{17,1},{18,2},{19,3},{20,4},{21,5},{22,6},{23,7},{24,8},{25... | collective-permute-start | bytes 417800 | tf_op jit(solution)/shard_map/ppermute | solution.py:191
  92.4 17.2 %collective-permute-start.17 = (f32[2,136,128]{2,1,0:T(8,128)}, f32[2,136,128]{2,1,0:T(8,128)}, u32[]{:S(2)}, u32[]{:S(2)}) collective-permute-start(f32[2,136,128]{2,1,0:T(8,128)} %add_add_fusion.1), channel_id=1, source_target_pairs={{24,0},{25,1},{26,2},{27,3},{28,4},{29,5},{30,6},{31,7}} | collective-permute-start | bytes 417800 | tf_op jit(solution)/shard_map/ppermute | solution.py:191
  93.9 1.9 copy-start.3
  95.8 1.2 copy-start.17
  97.0 1.0 copy-start.19
  97.9 49.8 %collective-permute-start.24 = (f32[8,64,768]{2,1,0:T(8,128)}, f32[8,64,768]{2,1,0:T(8,128)}, u32[]{:S(2)}, u32[]{:S(2)}) collective-permute-start(f32[8,64,768]{2,1,0:T(8,128)} %get-tuple-element.33), channel_id=1, source_target_pairs={{0,2},{1,3},{2,0},{3,1},{4,6},{5,7},{6,4},{7,5},{8,10},{9,11},{10,... | collective-permute-start | bytes 4718600 | tf_op jit(solution)/shard_map/ppermute | solution.py:176
  98.6 52.2 %collective-permute-start.28 = (f32[8,64,768]{2,1,0:T(8,128)}, f32[8,64,768]{2,1,0:T(8,128)}, u32[]{:S(2)}, u32[]{:S(2)}) collective-permute-start(f32[8,64,768]{2,1,0:T(8,128)} %copy-done.17), channel_id=1, source_target_pairs={{0,4},{1,5},{2,6},{3,7},{4,0},{5,1},{6,2},{7,3},{8,12},{9,13},{10,... | collective-permute-start | bytes 4718600 | tf_op jit(solution)/shard_map/ppermute | solution.py:176
  100.0 45.7 %collective-permute-start.32 = (f32[8,64,512]{2,1,0:T(8,128)}, f32[8,64,512]{2,1,0:T(8,128)}, u32[]{:S(2)}, u32[]{:S(2)}) collective-permute-start(f32[8,64,512]{2,1,0:T(8,128)} %copy-done.19), channel_id=1, source_target_pairs={{0,8},{1,9},{2,10},{3,11},{4,12},{5,13},{6,14},{7,15},{8,0},{9,1},... | collective-permute-start | bytes 3145736 | tf_op jit(solution)/shard_map/ppermute | solution.py:176
  113.2 23.6 %collective-permute-start.18 = (f32[2,136,128]{2,1,0:T(8,128)S(1)}, f32[2,136,128]{2,1,0:T(8,128)S(1)}, u32[]{:S(2)}, u32[]{:S(2)}) collective-permute-start(f32[2,136,128]{2,1,0:T(8,128)S(1)} %get-tuple-element.54), channel_id=1, source_target_pairs={{0,2},{1,3},{2,0},{3,1},{4,6},{5,7},{6,4},{7,5},{8,10},{9,11},{10,... | collective-permute-start | bytes 417800 | tf_op jit(solution)/shard_map/ppermute | solution.py:176
  114.1 24.1 %collective-permute-start.19 = (f32[2,136,128]{2,1,0:T(8,128)}, f32[2,136,128]{2,1,0:T(8,128)S(1)}, u32[]{:S(2)}, u32[]{:S(2)}) collective-permute-start(f32[2,136,128]{2,1,0:T(8,128)} %get-tuple-element.56), channel_id=1, source_target_pairs={{0,4},{1,5},{2,6},{3,7},{4,0},{5,1},{6,2},{7,3},{8,12},{9,13},{10,... | collective-permute-start | bytes 417800 | tf_op jit(solution)/shard_map/ppermute | solution.py:176
  136.8 6.3 %collective-permute-start.20 = (f32[2,136,128]{2,1,0:T(8,128)}, f32[2,136,128]{2,1,0:T(8,128)}, u32[]{:S(2)}, u32[]{:S(2)}) collective-permute-start(f32[2,136,128]{2,1,0:T(8,128)} %get-tuple-element.55), channel_id=1, source_target_pairs={{0,6},{1,7},{2,4},{3,5},{4,2},{5,3},{6,0},{7,1},{8,14},{9,15},{10,... | collective-permute-start | bytes 417800 | tf_op jit(solution)/shard_map/ppermute | solution.py:176
  138.2 6.3 %copy-start.2 = (f32[16,64,256]{2,1,0:T(8,128)S(1)}, f32[16,64,256]{2,1,0:T(8,128)}, u32[]{:S(2)}) copy-start(f32[16,64,256]{2,1,0:T(8,128)} %copy-done.1) | copy-start | bytes 3145732
  138.2 6.3 %copy-start.4 = (f32[16,64,256]{2,1,0:T(8,128)S(1)}, f32[16,64,256]{2,1,0:T(8,128)}, u32[]{:S(2)}) copy-start(f32[16,64,256]{2,1,0:T(8,128)} %copy-done.3) | copy-start | bytes 3145732
  144.4 18.3 %collective-permute-start.21 = (f32[4,2,136,128]{3,2,1,0:T(8,128)S(1)}, f32[4,2,136,128]{3,2,1,0:T(8,128)S(1)}, u32[]{:S(2)}, u32[]{:S(2)}) collective-permute-start(f32[4,2,136,128]{3,2,1,0:T(8,128)S(1)} %get-tuple-element.60), channel_id=1, source_target_pairs={{0,1},{1,0},{2,3},{3,2},{4,5},{5,4},{6,7},{7,6},{8,9},{9,8},{10,11... | collective-permute-start | bytes 1671176 | tf_op jit(solution)/shard_map/ppermute | solution.py:176
  147.2 14.8 %collective-permute-start.33 = (f32[2,2,64,512]{3,2,1,0:T(8,128)S(1)}, f32[2,2,64,512]{3,2,1,0:T(8,128)S(1)}, u32[]{:S(2)}, u32[]{:S(2)}) collective-permute-start(f32[2,2,64,512]{3,2,1,0:T(8,128)S(1)} %get-tuple-element.47), channel_id=1, source_target_pairs={{0,2},{1,3},{2,0},{3,1},{4,6},{5,7},{6,4},{7,5},{8,10},{9,11},{10,... | collective-permute-start | bytes 1572872 | tf_op jit(solution)/shard_map/ppermute | solution.py:176
  149.3 32.3 %collective-permute-start.25 = (f32[2,2,64,768]{3,2,1,0:T(8,128)S(1)}, f32[2,2,64,768]{3,2,1,0:T(8,128)S(1)}, u32[]{:S(2)}, u32[]{:S(2)}) collective-permute-start(f32[2,2,64,768]{3,2,1,0:T(8,128)S(1)} %get-tuple-element.43), channel_id=1, source_target_pairs={{0,4},{1,5},{2,6},{3,7},{4,0},{5,1},{6,2},{7,3},{8,12},{9,13},{10,... | collective-permute-start | bytes 2359304 | tf_op jit(solution)/shard_map/ppermute | solution.py:176
  150.8 11.8 %copy-start.7 = (bf16[256,2048]{1,0:T(8,128)(2,1)S(1)}, bf16[256,2048]{1,0:T(8,128)(2,1)}, u32[]{:S(2)}) copy-start(bf16[256,2048]{1,0:T(8,128)(2,1)} %k_ref.7) | copy-start | bytes 3145732
  150.8 11.8 %copy-start.10 = (bf16[256,2048]{1,0:T(8,128)(2,1)S(1)}, bf16[256,2048]{1,0:T(8,128)(2,1)}, u32[]{:S(2)}) copy-start(bf16[256,2048]{1,0:T(8,128)(2,1)} %v_ref.7) | copy-start | bytes 3145732
  150.8 11.8 %copy-start.14 = (f32[256,2048]{1,0:T(8,128)S(1)}, f32[256,2048]{1,0:T(8,128)}, u32[]{:S(2)}) copy-start(f32[256,2048]{1,0:T(8,128)} %copy-done.13) | copy-start | bytes 6291460
  150.8 11.8 %copy-start.16 = (f32[256,2048]{1,0:T(8,128)S(1)}, f32[256,2048]{1,0:T(8,128)}, u32[]{:S(2)}) copy-start(f32[256,2048]{1,0:T(8,128)} %copy-done.15) | copy-start | bytes 6291460
  152.6 32.0 %collective-permute-start.29 = (f32[2,2,64,768]{3,2,1,0:T(8,128)S(1)}, f32[2,2,64,768]{3,2,1,0:T(8,128)S(1)}, u32[]{:S(2)}, u32[]{:S(2)}) collective-permute-start(f32[2,2,64,768]{3,2,1,0:T(8,128)S(1)} %get-tuple-element.45), channel_id=1, source_target_pairs={{0,2},{1,3},{2,0},{3,1},{4,6},{5,7},{6,4},{7,5},{8,10},{9,11},{10,... | collective-permute-start | bytes 2359304 | tf_op jit(solution)/shard_map/ppermute | solution.py:176
  162.0 12.6 %collective-permute-start.34 = (f32[2,64,512]{2,1,0:T(8,128)S(1)}, f32[2,64,512]{2,1,0:T(8,128)S(1)}, u32[]{:S(2)}, u32[]{:S(2)}) collective-permute-start(f32[2,64,512]{2,1,0:T(8,128)S(1)} %get-tuple-element.53), channel_id=1, source_target_pairs={{0,4},{1,5},{2,6},{3,7},{4,0},{5,1},{6,2},{7,3},{8,12},{9,13},{10,... | collective-permute-start | bytes 786440 | tf_op jit(solution)/shard_map/ppermute | solution.py:176
  174.6 12.0 %collective-permute-start.35 = (f32[64,512]{1,0:T(8,128)S(1)}, f32[64,512]{1,0:T(8,128)S(1)}, u32[]{:S(2)}, u32[]{:S(2)}) collective-permute-start(f32[64,512]{1,0:T(8,128)S(1)} %fusion.21), channel_id=1, source_target_pairs={{0,16},{1,17},{2,18},{3,19},{4,20},{5,21},{6,22},{7,23},{8,24},{9,... | collective-permute-start | bytes 393224 | tf_op jit(solution)/shard_map/ppermute | solution.py:176
  181.7 13.2 %collective-permute-start.26 = (f32[2,64,768]{2,1,0:T(8,128)S(1)}, f32[2,64,768]{2,1,0:T(8,128)S(1)}, u32[]{:S(2)}, u32[]{:S(2)}) collective-permute-start(f32[2,64,768]{2,1,0:T(8,128)S(1)} %get-tuple-element.49), channel_id=1, source_target_pairs={{0,8},{1,9},{2,10},{3,11},{4,12},{5,13},{6,14},{7,15},{8,0},{9,1},... | collective-permute-start | bytes 1179656 | tf_op jit(solution)/shard_map/ppermute | solution.py:176
  184.7 21.3 %collective-permute-start.30 = (f32[2,64,768]{2,1,0:T(8,128)S(1)}, f32[2,64,768]{2,1,0:T(8,128)S(1)}, u32[]{:S(2)}, u32[]{:S(2)}) collective-permute-start(f32[2,64,768]{2,1,0:T(8,128)S(1)} %get-tuple-element.51), channel_id=1, source_target_pairs={{0,8},{1,9},{2,10},{3,11},{4,12},{5,13},{6,14},{7,15},{8,0},{9,1},... | collective-permute-start | bytes 1179656 | tf_op jit(solution)/shard_map/ppermute | solution.py:176
  194.9 13.2 %collective-permute-start.27 = (f32[64,768]{1,0:T(8,128)S(1)}, f32[64,768]{1,0:T(8,128)S(1)}, u32[]{:S(2)}, u32[]{:S(2)}) collective-permute-start(f32[64,768]{1,0:T(8,128)S(1)} %fusion.18), channel_id=1, source_target_pairs={{0,16},{1,17},{2,18},{3,19},{4,20},{5,21},{6,22},{7,23},{8,24},{9,... | collective-permute-start | bytes 589832 | tf_op jit(solution)/shard_map/ppermute | solution.py:176
  206.1 10.6 %collective-permute-start.31 = (f32[64,768]{1,0:T(8,128)S(1)}, f32[64,768]{1,0:T(8,128)S(1)}, u32[]{:S(2)}, u32[]{:S(2)}) collective-permute-start(f32[64,768]{1,0:T(8,128)S(1)} %fusion.15), channel_id=1, source_target_pairs={{0,16},{1,17},{2,18},{3,19},{4,20},{5,21},{6,22},{7,23},{8,24},{9,... | collective-permute-start | bytes 589832 | tf_op jit(solution)/shard_map/ppermute | solution.py:176

commit v2 on v1

v2 whole, which is shorter than its diff:
```python
import functools

import jax
import jax.numpy as jnp
from jax import lax
from jax.experimental import pallas as pl
from jax.experimental.pallas import tpu as pltpu
from jax.sharding import PartitionSpec as P

HEADS = 16
HEAD = 128
HALF = HEAD // 2
ROWS = HEAD + 8
PACK = 2 * HEAD + HEADS
F32 = jnp.float32
BF16 = jnp.bfloat16
NN = (((1,), (0,)), ((), ()))
NT = (((1,), (1,)), ((), ()))
TN = (((0,), (0,)), ((), ()))
PARTS = ((0, 768, (0, 1, 2, 3)), (768, 768, (1, 0, 3, 2)), (1536, 512, (2, 3, 0, 1)))
PAIRS = HEADS // 2
PLACES = PAIRS // 2
VMEM_LIMIT = 12 * 1024 * 1024


def split(a):
    high = a.astype(BF16)
    return high, (a - high.astype(F32)).astype(BF16)


def mm(a, b, dims):
    out = lax.dot_general(a[0], b[0], dims, preferred_element_type=F32)
    if len(b) > 1:
        out = out + lax.dot_general(a[0], b[1], dims, preferred_element_type=F32)
    if len(a) > 1:
        out = out + lax.dot_general(a[1], b[0], dims, preferred_element_type=F32)
    return out


def feature(x):
    return jnp.where(x > 0, x + 1.0, jnp.exp(jnp.minimum(x, 0.0)))


def slope(x, f):
    return jnp.where(x > 0, 1.0, f)


def masked(a, query_dim):
    query = lax.broadcasted_iota(jnp.int32, a.shape, query_dim)
    return jnp.where(lax.broadcasted_iota(jnp.int32, a.shape, 1 - query_dim) <= query, a, 0.0)


def each_head(at_ref, one):
    me = at_ref[0]
    core, plane = me % 2, (me // 2) % 4

    def pair(turn, carry):
        place, r = turn // 2, turn % 2
        for side in range(2):
            head = (side ^ core) * 8 + (place ^ plane) * 2 + r
            one(side, place, r, head, pl.ds(pl.multiple_of(head * HEAD, HEAD), HEAD))
        return carry

    lax.fori_loop(0, HEADS // 2, pair, 0)


def first_of(row):
    return jnp.where(lax.broadcasted_iota(jnp.int32, (8, row.shape[1]), 0) == 0, row, 0.0)


def rows_of(r):
    return slice(r * HEAD, (r + 1) * HEAD)


def times_row(row, b, dims):
    high, low = split(row)
    width = row.shape[1]
    at_top = lax.broadcasted_iota(jnp.int32, (16, width), 0) < 8
    both = jnp.where(at_top, high.astype(F32), low.astype(F32)).astype(BF16)
    out = lax.dot_general(both, b[0], dims, preferred_element_type=F32)
    out = out[:1] + out[8:9]
    if len(b) > 1:
        out = out + lax.dot_general(both, b[1], dims, preferred_element_type=F32)[:1]
    return out


def summary_kernel(at_ref, k_ref, v_ref, keep_ref, send_ref, sum_ref):
    def one(side, place, r, head, cols):
        fk = feature(k_ref[:, cols].astype(F32))
        state = mm((v_ref[:, cols],), split(fk), TN)
        (keep_ref, send_ref)[side][place, pl.ds(r * HEAD, HEAD), :] = state
        sum_ref[pl.ds(head, 1), :] = jnp.sum(fk, axis=0, keepdims=True)

    each_head(at_ref, one)
    for place in range(PLACES):
        keep_ref[place, 2 * HEAD :, :] = sum_ref[...]
        send_ref[place, 2 * HEAD :, :] = sum_ref[...]


def inner_kernel(at_ref, q_ref, k_ref, v_ref, nd_ref):
    def one(side, place, r, head, cols):
        fqs, fks = split(feature(q_ref[:, cols].astype(F32))), split(feature(k_ref[:, cols].astype(F32)))
        scores = masked(mm(fks, fqs, NT), 1)
        nd_ref[head, :HEAD, :] = mm((v_ref[:, cols],), split(scores), TN)
        nd_ref[head, HEAD:, :] = first_of(jnp.sum(scores, axis=0, keepdims=True))

    each_head(at_ref, one)


def grad_kernel(g_ref, w_ref, some_ref, gt_ref, wide_ref):
    got = lax.dot_general(w_ref[...], g_ref[...], NT, preferred_element_type=F32)
    gt_ref[...] = got.reshape(gt_ref.shape)
    wide_ref[...] = some_ref[...].astype(F32)


def attended_grad(out_grad, out_weight):
    t, model = out_grad.shape
    step = model // PAIRS
    return pl.pallas_call(
        grad_kernel,
        grid=(PAIRS,),
        out_shape=(
            jax.ShapeDtypeStruct((HEADS, HEAD, t), F32),
            jax.ShapeDtypeStruct((t, model), F32),
        ),
        in_specs=[
            pl.BlockSpec((t, model), lambda i: (0, 0)),
            pl.BlockSpec((2 * HEAD, model), lambda i: (i, 0)),
            pl.BlockSpec((t, step), lambda i: (0, i)),
        ],
        out_specs=(
            pl.BlockSpec((2, HEAD, t), lambda i: (i, 0, 0)),
            pl.BlockSpec((t, step), lambda i: (0, i)),
        ),
        compiler_params=pltpu.CompilerParams(vmem_limit_bytes=VMEM_LIMIT),
        cost_estimate=pl.CostEstimate(flops=1000, bytes_accessed=1000, transcendentals=0),
    )(out_grad, out_weight, out_grad)


def early_kernel(at_ref, q_ref, nd_ref, gt_ref, z_ref, keep_ref, send_ref, inv_ref):
    def one(side, place, r, head, cols):
        fqs = split(feature(q_ref[:, cols].astype(F32)))
        denom = times_row(z_ref[pl.ds(head, 1), :], fqs, NT)
        inv = 1.0 / (nd_ref[head, HEAD : HEAD + 1, :] + denom)
        inv_ref[head] = first_of(inv)
        state = mm(split(gt_ref[head] * inv), fqs, NN)
        (keep_ref, send_ref)[side][place, pl.ds(r * HEAD, HEAD), :] = state

    each_head(at_ref, one)
    for place in range(PLACES):
        keep_ref[place, 2 * HEAD :, :] = jnp.zeros((HEADS, HEAD), F32)
        send_ref[place, 2 * HEAD :, :] = jnp.zeros((HEADS, HEAD), F32)


def forward_kernel(
    at_ref, q_ref, nd_ref, gt_ref, inv_ref, s0_ref, s1_ref, dkeep_ref, dmate_ref,
    keep_ref, send_ref, dd_ref, t0_ref, t1_ref, t2_ref, t3_ref, dz_ref,
):
    me = at_ref[0]
    core, chip = me % 2, me // 2

    def one(side, place, r, head, cols):
        state = (s0_ref, s1_ref)[side][place, pl.ds(r * HEAD, HEAD), :]
        fqs = split(feature(q_ref[:, cols].astype(F32)))
        inv = inv_ref[head, :1, :]
        att = (nd_ref[head, :HEAD, :] + mm(split(state), fqs, NT)) * inv
        low, high = att[:HALF], att[HALF:]
        keep_ref[head ^ chip] = jnp.where(core == 0, low, high)
        send_ref[head ^ chip] = jnp.where(core == 0, high, low)
        dd = -jnp.sum(gt_ref[head] * att, axis=0, keepdims=True) * inv
        dd_ref[head] = first_of(dd)
        dz_ref[pl.ds(head, 1), :] = times_row(dd, fqs, NN)

    each_head(at_ref, one)
    for j, t_ref in enumerate((t0_ref, t1_ref, t2_ref, t3_ref)):
        t_ref[: 2 * HEAD, :] = dkeep_ref[j, : 2 * HEAD, :] + dmate_ref[j, : 2 * HEAD, :]
        t_ref[2 * HEAD :, :] = dz_ref[...]


def backward_kernel(
    at_ref, q_ref, k_ref, v_ref, gt_ref, inv_ref, dd_ref, z_ref, s0_ref, s1_ref, qg_ref, dk_ref, dv_ref
):
    def one(side, place, r, head, cols):
        state = (s0_ref, s1_ref)[side][place, pl.ds(r * HEAD, HEAD), :]
        q, v = q_ref[:, cols].astype(F32), v_ref[:, cols]
        fq = feature(q)
        fqs, fks = split(fq), split(feature(k_ref[:, cols].astype(F32)))
        ss = split(masked(mm(fks, fqs, NT), 1))
        dn = split(gt_ref[head] * inv_ref[head, :1, :])
        dd = dd_ref[head, :1, :]
        ds = split(masked(mm((v,), dn, NN) + dd, 1))
        z = z_ref[pl.ds(head, 1), :]
        dd_rows, z_rows = (jnp.concatenate([first_of(x)] * 2, axis=0) for x in (dd, z))
        dfq = mm(ds, fks, TN) + mm(dn, split(state), TN) + 0.5 * mm(split(dd_rows), split(z_rows), TN)
        qg_ref[:, cols] = (dfq * slope(q, fq)).astype(BF16)
        dk_ref[:, cols] = mm(ds, fqs, NN)
        dv_ref[:, cols] = mm(ss, dn, NT)

    each_head(at_ref, one)


def finish_kernel(at_ref, k_ref, v_ref, dk_ref, dv_ref, dz_ref, s0_ref, s1_ref, kg_ref, vg_ref):
    def one(side, place, r, head, cols):
        states = split((s0_ref, s1_ref)[side][place, pl.ds(r * HEAD, HEAD), :])
        k = k_ref[:, cols].astype(F32)
        fk = feature(k)
        dfk = dk_ref[:, cols] + mm((v_ref[:, cols],), states, NN) + dz_ref[pl.ds(head, 1), :]
        kg_ref[:, cols] = (dfk * slope(k, fk)).astype(BF16)
        vg_ref[:, cols] = (dv_ref[:, cols] + mm(split(fk), states, NT)).astype(BF16)

    each_head(at_ref, one)


def weight_kernel(bit_set, a0_ref, a1_ref, g0_ref, g1_ref, *refs):
    outs, (a_ref, g_ref) = refs[:-2], refs[-2:]
    t = g0_ref.shape[0]
    a_ref[:, :, :t] = a0_ref[...].astype(BF16)
    a_ref[:, :, t:] = a1_ref[...].astype(BF16)
    g_ref[:t, :] = g0_ref[...]
    g_ref[t:, :] = g1_ref[...].astype(BF16)
    for out_ref, (start, width, order) in zip(outs, PARTS, strict=True):
        rels = [rel for rel in range(HEADS) if (rel >> order[0]) & 1 == bit_set]
        lhs = jnp.concatenate([a_ref[rel] for rel in rels], axis=0)
        for at in range(0, width, 256):
            got = jnp.dot(lhs, g_ref[:, start + at : start + at + 256], preferred_element_type=F32)
            out_ref[:, :, at : at + 256] = got.reshape(len(rels), HALF, 256)


def call(kernel, outs, *args, scratch=()):
    specs = [pl.BlockSpec(memory_space=pltpu.SMEM if a.size == 1 else pltpu.VMEM) for a in args]
    return pl.pallas_call(
        kernel,
        out_shape=tuple(outs),
        in_specs=specs,
        out_specs=tuple(pl.BlockSpec(memory_space=pltpu.VMEM) for _ in outs),
        scratch_shapes=list(scratch),
        compiler_params=pltpu.CompilerParams(vmem_limit_bytes=VMEM_LIMIT),
        cost_estimate=pl.CostEstimate(flops=1000, bytes_accessed=1000, transcendentals=0),
    )(*args)


def swap(x, mask):
    n = lax.axis_size("seq")
    return lax.ppermute(x, "seq", [(i, i ^ mask) for i in range(n)])


def after(first, *arrays):
    arrays, _ = lax.optimization_barrier((arrays, first))
    return arrays if len(arrays) > 1 else arrays[0]


def along(layer, later):
    n = lax.axis_size("seq")
    got = []
    for k in range(1, n // 8):
        pairs = [(i, i + 8 * k) for i in range(n - 8 * k)]
        got.append(lax.ppermute(layer, "seq", [(b, a) for a, b in pairs] if later else pairs))
    return got or [jnp.zeros_like(layer)]


def along_in_turn(layer, first, me, later, beside):
    outer, mask = jnp.zeros_like(layer), 8
    while mask < lax.axis_size("seq"):
        other = after(beside, first) if mask == 8 else swap(layer, mask)
        outer = outer + jnp.where(((me & mask) == 0) == later, other, 0.0)
        layer = layer + other
        mask *= 2
    return outer


def before(got, place, plane, later):
    out = 0.0
    for i, x in enumerate(got):
        if i != place:
            ahead = (plane ^ i) > (plane ^ place) if later else (plane ^ i) < (plane ^ place)
            out = out + jnp.where(ahead, x, 0.0)
    return out


def halves(keep, got, left, bit):
    axis = left.index(bit)
    take = lambda a, i: lax.index_in_dim(a, i, axis, keepdims=False)
    return take(keep, 1) + take(got, 1), take(keep, 0) + take(got, 0)


def body(queries, keys, values, out_weight, out_grad):
    t, model = out_grad.shape
    shape = jax.ShapeDtypeStruct
    me = lax.axis_index("seq")
    core, plane = me % 2, (me // 2) % 4
    at = me.astype(jnp.int32).reshape(1)
    packs = [shape((PLACES, PACK, HEAD), F32)] * 2
    row = shape((HEADS, 8, t), F32)
    sums = shape((HEADS, HEAD), F32)
    wide = shape((t, HEADS * HEAD), F32)
    narrow = shape((t, HEADS * HEAD), BF16)
    places = range(PLACES)
    own_sums = lambda x: x[2 * HEAD :]

    keep, send = call(summary_kernel, packs, at, keys, values, scratch=(pltpu.VMEM((HEADS, HEAD), F32),))
    mate = swap(send, 1)
    gt, grad_wide = attended_grad(out_grad, out_weight)
    (inner,) = call(inner_kernel, [shape((HEADS, ROWS, t), F32)], at, queries, keys, values)
    total = [keep[j] + mate[j] for j in places]
    got = [total[0]] + [swap(total[j], 2 * j) for j in places[1:]]
    layer, inner = lax.optimization_barrier((got[0] + got[1] + got[2] + got[3], inner))
    outer = along(layer, False)
    outer, gt, grad_wide = lax.optimization_barrier((outer, gt, grad_wide))
    outer = sum(outer[1:], outer[0])
    back = [outer + before(got, j, plane, False) for j in places]
    z_in = own_sums(back[0]) + jnp.where(core == 1, own_sums(mate[0]), 0.0)

    z_in = after(back, z_in)
    back = [swap(x, 2 * j) if j else x for j, x in enumerate(back)]
    grad_mate = swap(grad_wide, 1)
    dkeep, dsend, inv = call(early_kernel, packs + [row], at, queries, inner, gt, z_in)
    back, dsend = lax.optimization_barrier((back, dsend))
    dmate = swap(dsend, 1)
    s1 = swap(jnp.stack([x + jnp.where(core == 0, keep[j], 0.0) for j, x in enumerate(back)]), 1)
    s0 = jnp.stack([x + jnp.where(core == 1, mate[j], 0.0) for j, x in enumerate(back)])

    half = shape((HEADS, HALF, t), F32)
    a_keep, a_send, dd, *dtotal = call(
        forward_kernel,
        [half, half, row] + [shape((PACK, HEAD), F32)] * PLACES,
        at,
        queries,
        inner,
        gt,
        inv,
        s0,
        s1,
        dkeep,
        dmate,
        scratch=(pltpu.VMEM((HEADS, HEAD), F32),),
    )
    a_mate = swap(a_send, 1)
    dgot = [dtotal[0]] + [swap(dtotal[j], 2 * j) for j in places[1:]]

    weight = lambda bit: call(
        functools.partial(weight_kernel, bit),
        [shape((HEADS // 2, HALF, width), F32) for _, width, _ in PARTS],
        a_keep,
        a_mate,
        out_grad,
        grad_mate,
        scratch=(pltpu.VMEM((HEADS, HALF, 2 * t), BF16), pltpu.VMEM((2 * t, model), BF16)),
    )
    sends, dgot = lax.optimization_barrier((list(weight(1)), dgot))
    a_mate = after(sends, a_mate)
    keeps = weight(0)
    dlayer = dgot[0] + dgot[1] + dgot[2] + dgot[3]
    gots = [swap(send, 2 << order[0]) for send, (_, _, order) in zip(sends, PARTS, strict=True)]
    dfirst = swap(dlayer, 8)
    queries = after((keeps, dlayer), queries)
    query_grad, dk, dv = call(
        backward_kernel, [narrow, wide, wide], at, queries, keys, values, gt, inv, dd, z_in, s0, s1
    )
    douter = along_in_turn(dlayer, dfirst, me, True, dk)
    gots, douter = lax.optimization_barrier((gots, douter))
    dback = [douter + before(dgot, j, plane, True) for j in places]

    lefts = [sorted(order[1:], reverse=True) for _, _, order in PARTS]
    for turn in range(1, 4):
        sends, kept = [], []
        for keep_part, got, left, (_, width, order) in zip(keeps, gots, lefts, PARTS, strict=True):
            shaped = (2,) * len(left) + (HALF, width)
            send, keep_part = halves(keep_part.reshape(shaped), got.reshape(shaped), left, order[turn])
            sends.append(send)
            kept.append(keep_part)
            left.remove(order[turn])
        keeps = kept
        gots = [swap(send, 2 << order[turn]) for send, (_, _, order) in zip(sends, PARTS, strict=True)]
        if turn == 1:
            dz, dz_part = own_sums(dgot[0]), own_sums(dback[0])
            up = swap(jnp.stack(dback[2:]), 4)
            across = swap(jnp.stack([dback[1], up[1]]), 2)
            dback = [dback[0], across[0], up[0], across[1]]
            gots, dback = lax.optimization_barrier((gots, dback))
        elif turn == 2:
            other = [(x + jnp.where(core == 1, dkeep[j], 0.0))[: 2 * HEAD] for j, x in enumerate(dback)]
            other = [jnp.concatenate([x, dz_part if j == 0 else dz]) for j, x in enumerate(other)]
            l1 = swap(after(sends, jnp.stack(other)), 1)
            l0 = jnp.stack([x + jnp.where(core == 0, dmate[j], 0.0) for j, x in enumerate(dback)])
            gots, l1 = lax.optimization_barrier((gots, l1))
    l0 = after(sends, l0)
    dz_in = dz_part + own_sums(l1[0]) + jnp.where(core == 0, own_sums(l1[1]), 0.0)
    key_grad, value_grad = call(finish_kernel, [narrow, narrow], at, keys, values, dk, dv, dz_in, l0, l1)
    key_grad, gots = lax.optimization_barrier((key_grad, gots))
    parts = [keep_part + got for keep_part, got in zip(keeps, gots, strict=True)]
    weight_grad = jnp.concatenate(parts, axis=1)
    return (query_grad, key_grad, value_grad, weight_grad)


def solution(mesh):
    placed = (
        P(("groups", "seq"), None),
        P(("groups", "seq"), None),
        P(("groups", "seq"), None),
        P(),
        P(("groups", "seq"), None),
    )
    return jax.shard_map(
        body,
        mesh=mesh,
        in_specs=placed,
        out_specs=(
            P(("groups", "seq"), None),
            P(("groups", "seq"), None),
            P(("groups", "seq"), None),
            P(("groups", "seq"), None),
        ),
        check_vma=False,
    )
```

time: 218 us -> 175 us (0.80)
  waiting for transfers between devices: 93.1 us -> 59.9 us
  starting transfers between devices: 57.9 us -> 37.5 us
  Pallas kernels: 37.3 us -> 47.1 us
  local copies, waits for them, and re-layouts: 6.77 us -> 14.8 us
  matrix products: 5.89 us -> 0 us
    ppermute x30 -> x31, waiting for transfers between devices: 88.6 us -> 59.9 us  [swap(): return lax.ppermute(x, 'seq', [(i, i ^ mask) for i in range(n)])]
    ppermute x30 -> x31, starting transfers between devices: 44.6 us -> 26.5 us  [swap(): return lax.ppermute(x, 'seq', [(i, i ^ mask) for i in range(n)])]
    unnamed x48 -> x80, local copies, waits for them, and re-layouts: 6.72 us -> 14.7 us
    dot_general x1 -> x0, matrix products: 5.89 us -> none  [body(): lax.dot_general(out_grad, out_weight, NT, preferred_element_type=F32)]
    pallas_call x6 -> x8, Pallas kernels: 37.3 us -> 43.1 us  [call(): pl.pallas_call(kernel, out_shape=tuple(outs), in_specs=specs, out_specs=t...]
    ppermute x6 -> x3, waiting for transfers between devices: 4.42 us -> 0.01 us  [along(): lax.ppermute(layer, 'seq', [(b, a) for a, b in pairs] if later else pairs)]
    pallas_call x0 -> x1, Pallas kernels: none -> 4.02 us  [attended_grad(): pl.pallas_call(grad_kernel, grid=(PAIRS,), out_shape=(jax.ShapeDtypeStruc...]
    ppermute x6 -> x3, starting transfers between devices: 13.3 us -> 11 us  [along(): lax.ppermute(layer, 'seq', [(b, a) for a, b in pairs] if later else pairs)]
  transfers between devices with their start and end apart: 36 -> 34, of which waited for: 19 -> 12; matrix products, arithmetic and copies ran while one was open for 9% -> 5% of each run, Pallas kernels for 16% -> 26%
where the time goes in v2:
time: 175 us; the launch traced here: 174 us
  waiting for transfers between devices  59.9 us (34%)
  Pallas kernels  47.1 us (27%)
  starting transfers between devices  37.5 us (21%)
  local copies, waits for them, and re-layouts  14.8 us (8%)
  other arithmetic  13.9 us (8%)
    ppermute x31, waiting for transfers between devices, swap(): return lax.ppermute(x, 'seq', [(i, i ^ mask) for i in range(n)])  59.9 us
    pallas_call x8, Pallas kernels, call(): pl.pallas_call(kernel, out_shape=tuple(outs), in_specs=specs, out_specs=t...  43.1 us
    ppermute x31, starting transfers between devices, swap(): return lax.ppermute(x, 'seq', [(i, i ^ mask) for i in range(n)])  26.5 us
    unnamed x80, local copies, waits for them, and re-layouts  14.7 us
    ppermute x3, starting transfers between devices, along(): lax.ppermute(layer, 'seq', [(b, a) for a, b in pairs] if later else pairs)  11 us
    add x10, other arithmetic, halves(): return (take(keep, 1) + take(got, 1), take(keep, 0) + take(got, 0))  5.8 us
    pallas_call x1, Pallas kernels, attended_grad(): pl.pallas_call(grad_kernel, grid=(PAIRS,), out_shape=(jax.ShapeDtypeStruc...  4.02 us
  transfers between devices with their start and end apart: 34, of which 12 were waited for; matrix products, arithmetic and copies ran while one was open for 5% of the time, Pallas kernels for 26%

profile of v2, /device:TPU:0, one launch (start us, length us, event | category | flops | bytes accessed | tf_op | source)
XLA Modules:
  0.0 174.5 jit_solution(2652858393488611990)
XLA Ops:
  0.6 1.2 copy-done.4
  1.9 1.2 copy-done.7
  3.1 2.4 %shard_map.84 = (f32[4,272,128]{2,1,0:T(8,128)S(1)}, f32[4,272,128]{2,1,0:T(8,128)S(1)}) custom-call(s32[1]{0:T(128)} %bitcast.at_ref, bf16[256,2048]{1,0:T(8,128)(2,1)S(1)} %copy-done.4, bf16[256,2048]{1,0:T(8,128)(2,1)S(1)} %copy-done.7), custom_call_target="tpu_custom_call" | custom-call | flops 1000 | bytes 1000 | tf_op jit(solution)/shard_map/pallas_call | solution.py:231
  5.5 0.5 collective-permute-start
  6.0 1.6 collective-permute-done
  7.7 2.9 %collective-permute-start.1 = (f32[272,128]{1,0:T(8,128)S(1)}, f32[272,128]{1,0:T(8,128)S(1)}, u32[]{:S(2)}, u32[]{:S(2)}) collective-permute-start(f32[272,128]{1,0:T(8,128)S(1)} %get-tuple-element.154), channel_id=1, source_target_pairs={{0,2},{1,3},{2,0},{3,1},{4,6},{5,7},{6,4},{7,5},{8,10},{9,11},{10,... | collective-permute-start | bytes 417800 | tf_op jit(solution)/shard_map/ppermute | solution.py:244
  10.6 1.5 collective-permute-start.2
  12.2 7.7 %shard_map.85.nd_ref = f32[16,136,256]{2,1,0:T(8,128)S(1)} custom-call(s32[1]{0:T(128)} %bitcast.at_ref, bf16[256,2048]{1,0:T(8,128)(2,1)S(1)} %copy-done.9, bf16[256,2048]{1,0:T(8,128)(2,1)S(1)} %copy-done.5, bf16[256,2048]{1,0:T(8,128)(2,1)S(1)} %copy-done.7), custom_call_target="tpu_custom_call" | custom-call | flops 1000 | bytes 1000 | tf_op jit(solution)/shard_map/pallas_call | solution.py:231
  19.9 0.8 fusion.46
  20.7 4.6 %collective-permute-start.4 = (f32[272,128]{1,0:T(8,128)}, f32[272,128]{1,0:T(8,128)}, u32[]{:S(2)}, u32[]{:S(2)}) collective-permute-start(f32[272,128]{1,0:T(8,128)} %get-tuple-element.76), channel_id=1, source_target_pairs={{0,8},{1,9},{2,10},{3,11},{4,12},{5,13},{6,14},{7,15},{8,16},{9,17... | collective-permute-start | bytes 417800 | tf_op jit(solution)/shard_map/ppermute | solution.py:257
  25.3 4.5 %collective-permute-start.5 = (f32[272,128]{1,0:T(8,128)}, f32[272,128]{1,0:T(8,128)}, u32[]{:S(2)}, u32[]{:S(2)}) collective-permute-start(f32[272,128]{1,0:T(8,128)} %get-tuple-element.76), channel_id=1, source_target_pairs={{0,16},{1,17},{2,18},{3,19},{4,20},{5,21},{6,22},{7,23},{8,24},{9,... | collective-permute-start | bytes 417800 | tf_op jit(solution)/shard_map/ppermute | solution.py:257
  29.8 1.9 %collective-permute-start.6 = (f32[272,128]{1,0:T(8,128)}, f32[272,128]{1,0:T(8,128)}, u32[]{:S(2)}, u32[]{:S(2)}) collective-permute-start(f32[272,128]{1,0:T(8,128)} %get-tuple-element.76), channel_id=1, source_target_pairs={{0,24},{1,25},{2,26},{3,27},{4,28},{5,29},{6,30},{7,31}} | collective-permute-start | bytes 417800 | tf_op jit(solution)/shard_map/ppermute | solution.py:257
  31.7 3.4 %copy-done.13 = bf16[2048,2048]{1,0:T(8,128)(2,1)S(1)} copy-done((bf16[2048,2048]{1,0:T(8,128)(2,1)S(1)}, bf16[2048,2048]{1,0:T(8,128)(2,1)}, u32[]{:S(2)}) %copy-start.13) | copy-done | bytes 8388632
  35.1 4.0 %shard_map.86 = (f32[16,128,256]{2,1,0:T(8,128)S(1)}, f32[256,2048]{1,0:T(8,128)S(1)}) custom-call(bf16[256,2048]{1,0:T(8,128)(2,1)S(1)} %copy-done.3, bf16[2048,2048]{1,0:T(8,128)(2,1)S(1)} %copy-done.13, bf16[256,2048]{1,0:T(8,128)(2,1)S(1)} %copy-done.3), custom_call_target="tpu_custom_call" | custom-call | flops 1000 | bytes 1000 | tf_op jit(solution)/shard_map/pallas_call | solution.py:119
  39.1 1.3 copy-done
  40.4 1.3 copy-done.30
  41.8 1.3 fusion.55
  43.1 1.1 fusion.52
  44.2 1.6 collective-permute-start.7
  45.7 1.5 collective-permute-start.8
  47.3 0.5 collective-permute-start.9
  47.7 0.7 fusion.62.z_ref
  48.4 1.2 copy-done.10
  49.7 4.8 %shard_map.87 = (f32[4,272,128]{2,1,0:T(8,128)S(1)}, f32[4,272,128]{2,1,0:T(8,128)S(1)}, f32[16,8,256]{2,1,0:T(8,128)S(1)}) custom-call(s32[1]{0:T(128)} %bitcast.at_ref, bf16[256,2048]{1,0:T(8,128)(2,1)S(1)} %copy-done.10, f32[16,136,256]{2,1,0:T(8,128)S(1)} %shard_map.85.nd_ref, f32[16,128,256]{2,1,0:T(8,128)S(1)} %copy-done.1, f32[16,128]{1,0:T(8,128)S(1)} %fusion.62.z_ref), custom_call_target="tpu_custom_call" | custom-call | flops 1000 | bytes 1000 | tf_op jit(solution)/shard_map/pallas_call | solution.py:231
  54.7 0.6 collective-permute-start.10
  55.4 1.5 collective-permute-done.10.s1_ref
  56.9 0.8 collective-permute-done.11.dmate_ref
  57.7 5.7 %shard_map.88 = (f32[16,64,256]{2,1,0:T(8,128)S(1)}, f32[16,64,256]{2,1,0:T(8,128)S(1)}, f32[16,8,256]{2,1,0:T(8,128)S(1)}, f32[272,128]{1,0:T(8,128)S(1)}, f32[...) custom-call(s32[1]{0:T(128)} %bitcast.at_ref, bf16[256,2048]{1,0:T(8,128)(2,1)S(1)} %copy-done.11, ...), custom_call_target="tpu_custom_call" | custom-call | flops 1000 | bytes 1000 | tf_op jit(solution)/shard_map/pallas_call | solution.py:231
  63.9 1.5 collective-permute-start.14
  65.4 1.5 collective-permute-start.15
  67.5 2.7 %shard_map.89 = (f32[8,64,768]{2,1,0:T(8,128)}, f32[8,64,768]{2,1,0:T(8,128)}, f32[8,64,512]{2,1,0:T(8,128)}) custom-call(f32[16,64,256]{2,1,0:T(8,128)S(1)} %get-tuple-element.92.a0_ref, f32[16,64,256]{2,1,0:T(8,128)S(1)} %collective-permute-done.12.a1_ref, bf16[256,2048]{1,0:T(8,128)(2,1)S(1)} %copy-done.3, f32[256,2048]{1,0:T(8,128)S(1)} %collective-permute-done.13.g1_ref), custom_call_target="tpu_custom_call" | custom-call | flops 1000 | bytes 1000 | tf_op jit(solution)/shard_map/pallas_call | solution.py:231
  70.2 3.6 %collective-permute-done.15 = f32[272,128]{1,0:T(8,128)S(1)} collective-permute-done((f32[272,128]{1,0:T(8,128)S(1)}, f32[272,128]{1,0:T(8,128)S(1)}, u32[]{:S(2)}, u32[]{:S(2)}) %collective-permute-start.15) | collective-permute-done | bytes 139296 | tf_op jit(solution)/shard_map/ppermute | solution.py:244
  73.8 1.2 collective-permute-start.17
  75.1 0.9 collective-permute-start.18
  76.0 0.7 add_add_fusion.1
  76.7 2.0 %collective-permute-start.20 = (f32[272,128]{1,0:T(8,128)}, f32[272,128]{1,0:T(8,128)}, u32[]{:S(2)}, u32[]{:S(2)}) collective-permute-start(f32[272,128]{1,0:T(8,128)} %add_add_fusion.1), channel_id=1, source_target_pairs={{0,8},{1,9},{2,10},{3,11},{4,12},{5,13},{6,14},{7,15},{8,0},{9,1},... | collective-permute-start | bytes 417800 | tf_op jit(solution)/shard_map/ppermute | solution.py:244
  78.7 1.6 copy-done.15
  80.3 1.2 copy-done.19
  81.5 1.3 shard_map.90
  84.0 0.9 copy-done.29
  84.9 14.4 %shard_map.91 = (bf16[256,2048]{1,0:T(8,128)(2,1)}, f32[256,2048]{1,0:T(8,128)S(1)}, f32[256,2048]{1,0:T(8,128)S(1)}) custom-call(s32[1]{0:T(128)} %bitcast.at_ref, bf16[256,2048]{1,0:T(8,128)(2,1)S(1)} %copy-done.12, bf16[256,2048]{1,0:T(8,128)(2,1)S(1)} %copy-done.6, bf16[256,2048]{1,0:T(8,128)(2,1)S(1)} %copy-done.8, f32[16,128,256]{2,1,0:T(8,128)S(1)} %copy-done.2, ...), custom_call_target="tpu_custom_call" | custom-call | flops 1000 | bytes 1000 | tf_op jit(solution)/shard_map/pallas_call | solution.py:231
  99.3 3.4 %collective-permute-done.20 = f32[272,128]{1,0:T(8,128)} collective-permute-done((f32[272,128]{1,0:T(8,128)}, f32[272,128]{1,0:T(8,128)}, u32[]{:S(2)}, u32[]{:S(2)}) %collective-permute-start.20) | collective-permute-done | bytes 139296 | tf_op jit(solution)/shard_map/ppermute | solution.py:244
  102.7 1.0 add.339
  103.9 7.1 %collective-permute-done.21 = f32[272,128]{1,0:T(8,128)S(1)} collective-permute-done((f32[272,128]{1,0:T(8,128)S(1)}, f32[272,128]{1,0:T(8,128)S(1)}, u32[]{:S(2)}, u32[]{:S(2)}) %collective-permute-start.21) | collective-permute-done | bytes 139296 | tf_op jit(solution)/shard_map/ppermute | solution.py:244
  110.9 0.9 select_add_fusion
  112.1 1.6 collective-permute-start.25
  113.7 1.4 slice_add_fusion
  115.2 1.2 fusion.2
  116.5 0.5 collective-permute-start.23
  116.9 1.6 fusion.4
  118.5 1.6 collective-permute-start.22
  120.2 1.2 collective-permute-start.26
  121.4 1.2 fusion
  122.6 15.9 %collective-permute-done.26 = f32[2,272,128]{2,1,0:T(8,128)S(1)} collective-permute-done((f32[2,272,128]{2,1,0:T(8,128)S(1)}, f32[2,272,128]{2,1,0:T(8,128)S(1)}, u32[]{:S(2)}, u32[]{:S(2)}) %collective-permute-start.26) | collective-permute-done | bytes 278560 | tf_op jit(solution)/shard_map/ppermute | solution.py:244
  139.1 2.7 %collective-permute-start.28 = (f32[2,64,768]{2,1,0:T(8,128)S(1)}, f32[2,64,768]{2,1,0:T(8,128)S(1)}, u32[]{:S(2)}, u32[]{:S(2)}) collective-permute-start(f32[2,64,768]{2,1,0:T(8,128)S(1)} %get-tuple-element.151), channel_id=1, source_target_pairs={{0,16},{1,17},{2,18},{3,19},{4,20},{5,21},{6,22},{7,23},{8,24},{9,... | collective-permute-start | bytes 1179656 | tf_op jit(solution)/shard_map/ppermute | solution.py:244
  142.2 8.0 %collective-permute-done.29 = f32[2,64,512]{2,1,0:T(8,128)S(1)} collective-permute-done((f32[2,64,512]{2,1,0:T(8,128)S(1)}, f32[2,64,512]{2,1,0:T(8,128)S(1)}, u32[]{:S(2)}, u32[]{:S(2)}) %collective-permute-start.29) | collective-permute-done | bytes 262176 | tf_op jit(solution)/shard_map/ppermute | solution.py:244
  150.2 9.6 %collective-permute-done.28 = f32[2,64,768]{2,1,0:T(8,128)S(1)} collective-permute-done((f32[2,64,768]{2,1,0:T(8,128)S(1)}, f32[2,64,768]{2,1,0:T(8,128)S(1)}, u32[]{:S(2)}, u32[]{:S(2)}) %collective-permute-start.28) | collective-permute-done | bytes 393248 | tf_op jit(solution)/shard_map/ppermute | solution.py:244
  159.8 1.6 collective-permute-done.27
  161.4 0.5 collective-permute-start.33
  161.9 0.5 collective-permute-start.32
  162.5 4.1 %shard_map.92 = (bf16[256,2048]{1,0:T(8,128)(2,1)}, bf16[256,2048]{1,0:T(8,128)(2,1)}) custom-call(s32[1]{0:T(128)} %bitcast.at_ref, bf16[256,2048]{1,0:T(8,128)(2,1)S(1)} %copy-done.6, bf16[256,2048]{1,0:T(8,128)(2,1)S(1)} %copy-done.8, f32[256,2048]{1,0:T(8,128)S(1)} %get-tuple-element.116.dk_ref, f32[256,2048]{1,0:T(8,128)S(1)} %get-tuple-element.117.dv_ref, ...), custom_call_target="tpu_custom_call" | custom-call | flops 1000 | bytes 1000 | tf_op jit(solution)/shard_map/pallas_call | solution.py:231
  166.6 2.6 %collective-permute-done.32 = f32[64,768]{1,0:T(8,128)S(1)} collective-permute-done((f32[64,768]{1,0:T(8,128)S(1)}, f32[64,768]{1,0:T(8,128)S(1)}, u32[]{:S(2)}, u32[]{:S(2)}) %collective-permute-start.32) | collective-permute-done | bytes 196640 | tf_op jit(solution)/shard_map/ppermute | solution.py:244
  169.2 4.3 %collective-permute-done.31 = f32[64,768]{1,0:T(8,128)S(1)} collective-permute-done((f32[64,768]{1,0:T(8,128)S(1)}, f32[64,768]{1,0:T(8,128)S(1)}, u32[]{:S(2)}, u32[]{:S(2)}) %collective-permute-start.31) | collective-permute-done | bytes 196640 | tf_op jit(solution)/shard_map/ppermute | solution.py:244
  173.6 0.8 pad_maximum_fusion.4
  (134 shorter events, 4.2 us)
Async XLA Ops:
  3.1 9.1 %copy-start.5 = (bf16[256,2048]{1,0:T(8,128)(2,1)S(1)}, bf16[256,2048]{1,0:T(8,128)(2,1)}, u32[]{:S(2)}) copy-start(bf16[256,2048]{1,0:T(8,128)(2,1)} %k_ref.7) | copy-start | bytes 3145732
  3.1 9.1 %copy-start.9 = (bf16[256,2048]{1,0:T(8,128)(2,1)S(1)}, bf16[256,2048]{1,0:T(8,128)(2,1)}, u32[]{:S(2)}) copy-start(bf16[256,2048]{1,0:T(8,128)(2,1)} %q_ref.6) | copy-start | bytes 3145732
  5.5 14.4 %copy-start.20 = (f32[4,272,128]{2,1,0:T(8,128)}, f32[4,272,128]{2,1,0:T(8,128)S(1)}, u32[]{:S(2)}) copy-start(f32[4,272,128]{2,1,0:T(8,128)S(1)} %get-tuple-element.73) | copy-start | bytes 1671172
  5.5 2.1 %collective-permute-start = (f32[4,272,128]{2,1,0:T(8,128)S(1)}, f32[4,272,128]{2,1,0:T(8,128)S(1)}, u32[]{:S(2)}, u32[]{:S(2)}) collective-permute-start(f32[4,272,128]{2,1,0:T(8,128)S(1)} %get-tuple-element.74), channel_id=1, source_target_pairs={{0,1},{1,0},{2,3},{3,2},{4,5},{5,4},{6,7},{7,6},{8,9},{9,8},{10,11... | collective-permute-start | bytes 1671176 | tf_op jit(solution)/shard_map/ppermute | solution.py:244
  7.6 12.3 %copy-start.31 = (f32[4,272,128]{2,1,0:T(8,128)}, f32[4,272,128]{2,1,0:T(8,128)S(1)}, u32[]{:S(2)}) copy-start(f32[4,272,128]{2,1,0:T(8,128)S(1)} %collective-permute-done) | copy-start | bytes 1671172
  7.7 12.2 %collective-permute-start.1 = (f32[272,128]{1,0:T(8,128)S(1)}, f32[272,128]{1,0:T(8,128)S(1)}, u32[]{:S(2)}, u32[]{:S(2)}) collective-permute-start(f32[272,128]{1,0:T(8,128)S(1)} %get-tuple-element.154), channel_id=1, source_target_pairs={{0,2},{1,3},{2,0},{3,1},{4,6},{5,7},{6,4},{7,5},{8,10},{9,11},{10,... | collective-permute-start | bytes 417800 | tf_op jit(solution)/shard_map/ppermute | solution.py:244
  10.6 9.3 %collective-permute-start.2 = (f32[272,128]{1,0:T(8,128)S(1)}, f32[272,128]{1,0:T(8,128)S(1)}, u32[]{:S(2)}, u32[]{:S(2)}) collective-permute-start(f32[272,128]{1,0:T(8,128)S(1)} %get-tuple-element.156), channel_id=1, source_target_pairs={{0,4},{1,5},{2,6},{3,7},{4,0},{5,1},{6,2},{7,3},{8,12},{9,13},{10,... | collective-permute-start | bytes 417800 | tf_op jit(solution)/shard_map/ppermute | solution.py:244
  12.1 7.8 %collective-permute-start.3 = (f32[272,128]{1,0:T(8,128)S(1)}, f32[272,128]{1,0:T(8,128)S(1)}, u32[]{:S(2)}, u32[]{:S(2)}) collective-permute-start(f32[272,128]{1,0:T(8,128)S(1)} %get-tuple-element.155), channel_id=1, source_target_pairs={{0,6},{1,7},{2,4},{3,5},{4,2},{5,3},{6,0},{7,1},{8,14},{9,15},{10,... | collective-permute-start | bytes 417800 | tf_op jit(solution)/shard_map/ppermute | solution.py:244
  12.2 19.6 %copy-start.3 = (bf16[256,2048]{1,0:T(8,128)(2,1)S(1)}, bf16[256,2048]{1,0:T(8,128)(2,1)}, u32[]{:S(2)}) copy-start(bf16[256,2048]{1,0:T(8,128)(2,1)} %g0_ref.3) | copy-start | bytes 3145732
  19.9 9.8 %copy-start.39 = (f32[272,128]{1,0:T(8,128)}, f32[272,128]{1,0:T(8,128)S(1)}, u32[]{:S(2)}) copy-start(f32[272,128]{1,0:T(8,128)S(1)} %collective-permute-done.3) | copy-start | bytes 417796
  20.7 21.1 %collective-permute-start.4 = (f32[272,128]{1,0:T(8,128)}, f32[272,128]{1,0:T(8,128)}, u32[]{:S(2)}, u32[]{:S(2)}) collective-permute-start(f32[272,128]{1,0:T(8,128)} %get-tuple-element.76), channel_id=1, source_target_pairs={{0,8},{1,9},{2,10},{3,11},{4,12},{5,13},{6,14},{7,15},{8,16},{9,17... | collective-permute-start | bytes 417800 | tf_op jit(solution)/shard_map/ppermute | solution.py:257
  25.3 16.5 %collective-permute-start.5 = (f32[272,128]{1,0:T(8,128)}, f32[272,128]{1,0:T(8,128)}, u32[]{:S(2)}, u32[]{:S(2)}) collective-permute-start(f32[272,128]{1,0:T(8,128)} %get-tuple-element.76), channel_id=1, source_target_pairs={{0,16},{1,17},{2,18},{3,19},{4,20},{5,21},{6,22},{7,23},{8,24},{9,... | collective-permute-start | bytes 417800 | tf_op jit(solution)/shard_map/ppermute | solution.py:257
  29.8 12.0 %collective-permute-start.6 = (f32[272,128]{1,0:T(8,128)}, f32[272,128]{1,0:T(8,128)}, u32[]{:S(2)}, u32[]{:S(2)}) collective-permute-start(f32[272,128]{1,0:T(8,128)} %get-tuple-element.76), channel_id=1, source_target_pairs={{0,24},{1,25},{2,26},{3,27},{4,28},{5,29},{6,30},{7,31}} | collective-permute-start | bytes 417800 | tf_op jit(solution)/shard_map/ppermute | solution.py:257
  31.7 3.4 %copy-start.13 = (bf16[2048,2048]{1,0:T(8,128)(2,1)S(1)}, bf16[2048,2048]{1,0:T(8,128)(2,1)}, u32[]{:S(2)}) copy-start(bf16[2048,2048]{1,0:T(8,128)(2,1)} %w_ref.1) | copy-start | bytes 25165828
  41.8 6.7 %copy-start.1 = (f32[16,128,256]{2,1,0:T(8,128)S(1)}, f32[16,128,256]{2,1,0:T(8,128)}, u32[]{:S(2)}) copy-start(f32[16,128,256]{2,1,0:T(8,128)} %copy-done) | copy-start | bytes 6291460
  44.2 10.3 %collective-permute-start.7 = (f32[272,128]{1,0:T(8,128)S(1)}, f32[272,128]{1,0:T(8,128)S(1)}, u32[]{:S(2)}, u32[]{:S(2)}) collective-permute-start(f32[272,128]{1,0:T(8,128)S(1)} %get-tuple-element.184), channel_id=1, source_target_pairs={{0,2},{1,3},{2,0},{3,1},{4,6},{5,7},{6,4},{7,5},{8,10},{9,11},{10,... | collective-permute-start | bytes 417800 | tf_op jit(solution)/shard_map/ppermute | solution.py:244
  45.7 8.8 %collective-permute-start.8 = (f32[272,128]{1,0:T(8,128)S(1)}, f32[272,128]{1,0:T(8,128)S(1)}, u32[]{:S(2)}, u32[]{:S(2)}) collective-permute-start(f32[272,128]{1,0:T(8,128)S(1)} %get-tuple-element.183), channel_id=1, source_target_pairs={{0,4},{1,5},{2,6},{3,7},{4,0},{5,1},{6,2},{7,3},{8,12},{9,13},{10,... | collective-permute-start | bytes 417800 | tf_op jit(solution)/shard_map/ppermute | solution.py:244
  47.3 7.2 %collective-permute-start.9 = (f32[272,128]{1,0:T(8,128)S(1)}, f32[272,128]{1,0:T(8,128)S(1)}, u32[]{:S(2)}, u32[]{:S(2)}) collective-permute-start(f32[272,128]{1,0:T(8,128)S(1)} %get-tuple-element.142), channel_id=1, source_target_pairs={{0,6},{1,7},{2,4},{3,5},{4,2},{5,3},{6,0},{7,1},{8,14},{9,15},{10,... | collective-permute-start | bytes 417800 | tf_op jit(solution)/shard_map/ppermute | solution.py:244
  47.7 19.7 %collective-permute-start.13 = (f32[256,2048]{1,0:T(8,128)}, f32[256,2048]{1,0:T(8,128)S(1)}, u32[]{:S(2)}, u32[]{:S(2)}) collective-permute-start(f32[256,2048]{1,0:T(8,128)} %copy-done.30), channel_id=1, source_target_pairs={{0,1},{1,0},{2,3},{3,2},{4,5},{5,4},{6,7},{7,6},{8,9},{9,8},{10,11... | collective-permute-start | bytes 6291464 | tf_op jit(solution)/shard_map/ppermute | solution.py:244
  49.7 4.8 %copy-start.21 = (f32[4,272,128]{2,1,0:T(8,128)S(1)}, f32[4,272,128]{2,1,0:T(8,128)}, u32[]{:S(2)}) copy-start(f32[4,272,128]{2,1,0:T(8,128)} %copy-done.20) | copy-start | bytes 1671172
  49.7 4.9 %copy-start.32 = (f32[4,272,128]{2,1,0:T(8,128)S(1)}, f32[4,272,128]{2,1,0:T(8,128)}, u32[]{:S(2)}) copy-start(f32[4,272,128]{2,1,0:T(8,128)} %copy-done.31) | copy-start | bytes 1671172
  54.5 3.2 %copy-start.24 = (f32[4,272,128]{2,1,0:T(8,128)}, f32[4,272,128]{2,1,0:T(8,128)S(1)}, u32[]{:S(2)}) copy-start(f32[4,272,128]{2,1,0:T(8,128)S(1)} %get-tuple-element.90.dkeep_ref) | copy-start | bytes 1671172
  54.7 3.0 %copy-start.11 = (bf16[256,2048]{1,0:T(8,128)(2,1)S(1)}, bf16[256,2048]{1,0:T(8,128)(2,1)}, u32[]{:S(2)}) copy-start(bf16[256,2048]{1,0:T(8,128)(2,1)} %q_ref.6) | copy-start | bytes 3145732
  54.7 2.2 %collective-permute-start.10 = (f32[4,272,128]{2,1,0:T(8,128)S(1)}, f32[4,272,128]{2,1,0:T(8,128)S(1)}, u32[]{:S(2)}, u32[]{:S(2)}) collective-permute-start(f32[4,272,128]{2,1,0:T(8,128)S(1)} %pad_maximum_fusion.1), channel_id=1, source_target_pairs={{0,1},{1,0},{2,3},{3,2},{4,5},{5,4},{6,7},{7,6},{8,9},{9,8},{10,11... | collective-permute-start | bytes 1671176 | tf_op jit(solution)/shard_map/ppermute | solution.py:244
  55.3 2.4 %collective-permute-start.11 = (f32[4,272,128]{2,1,0:T(8,128)S(1)}, f32[4,272,128]{2,1,0:T(8,128)S(1)}, u32[]{:S(2)}, u32[]{:S(2)}) collective-permute-start(f32[4,272,128]{2,1,0:T(8,128)S(1)} %get-tuple-element.91), channel_id=1, source_target_pairs={{0,1},{1,0},{2,3},{3,2},{4,5},{5,4},{6,7},{7,6},{8,9},{9,8},{10,11... | collective-permute-start | bytes 1671176 | tf_op jit(solution)/shard_map/ppermute | solution.py:244
  55.4 8.0 %copy-start.16 = (f32[4,272,128]{2,1,0:T(8,128)}, f32[4,272,128]{2,1,0:T(8,128)S(1)}, u32[]{:S(2)}) copy-start(f32[4,272,128]{2,1,0:T(8,128)S(1)} %pad_maximum_fusion.s0_ref) | copy-start | bytes 1671172
  56.9 6.6 %copy-start.26 = (f32[4,272,128]{2,1,0:T(8,128)}, f32[4,272,128]{2,1,0:T(8,128)S(1)}, u32[]{:S(2)}) copy-start(f32[4,272,128]{2,1,0:T(8,128)S(1)} %collective-permute-done.10.s1_ref) | copy-start | bytes 1671172
  57.7 5.8 %copy-start.22 = (f32[4,272,128]{2,1,0:T(8,128)}, f32[4,272,128]{2,1,0:T(8,128)S(1)}, u32[]{:S(2)}) copy-start(f32[4,272,128]{2,1,0:T(8,128)S(1)} %collective-permute-done.11.dmate_ref) | copy-start | bytes 1671172
  63.5 6.7 %copy-start.18 = (f32[16,64,256]{2,1,0:T(8,128)}, f32[16,64,256]{2,1,0:T(8,128)S(1)}, u32[]{:S(2)}) copy-start(f32[16,64,256]{2,1,0:T(8,128)S(1)} %get-tuple-element.92.a0_ref) | copy-start | bytes 3145732
  63.5 6.7 %copy-start.28 = (f32[16,8,256]{2,1,0:T(8,128)}, f32[16,8,256]{2,1,0:T(8,128)S(1)}, u32[]{:S(2)}) copy-start(f32[16,8,256]{2,1,0:T(8,128)S(1)} %get-tuple-element.114.dd_ref) | copy-start | bytes 393220
  63.5 4.0 %collective-permute-start.12 = (f32[16,64,256]{2,1,0:T(8,128)S(1)}, f32[16,64,256]{2,1,0:T(8,128)S(1)}, u32[]{:S(2)}, u32[]{:S(2)}) collective-permute-start(f32[16,64,256]{2,1,0:T(8,128)S(1)} %get-tuple-element.93), channel_id=1, source_target_pairs={{0,1},{1,0},{2,3},{3,2},{4,5},{5,4},{6,7},{7,6},{8,9},{9,8},{10,11... | collective-permute-start | bytes 3145736 | tf_op jit(solution)/shard_map/ppermute | solution.py:244
  63.9 6.3 %collective-permute-start.14 = (f32[272,128]{1,0:T(8,128)S(1)}, f32[272,128]{1,0:T(8,128)S(1)}, u32[]{:S(2)}, u32[]{:S(2)}) collective-permute-start(f32[272,128]{1,0:T(8,128)S(1)} %get-tuple-element.99), channel_id=1, source_target_pairs={{0,2},{1,3},{2,0},{3,1},{4,6},{5,7},{6,4},{7,5},{8,10},{9,11},{10,... | collective-permute-start | bytes 417800 | tf_op jit(solution)/shard_map/ppermute | solution.py:244
  65.4 8.4 %collective-permute-start.15 = (f32[272,128]{1,0:T(8,128)S(1)}, f32[272,128]{1,0:T(8,128)S(1)}, u32[]{:S(2)}, u32[]{:S(2)}) collective-permute-start(f32[272,128]{1,0:T(8,128)S(1)} %get-tuple-element.100), channel_id=1, source_target_pairs={{0,4},{1,5},{2,6},{3,7},{4,0},{5,1},{6,2},{7,3},{8,12},{9,13},{10,... | collective-permute-start | bytes 417800 | tf_op jit(solution)/shard_map/ppermute | solution.py:244
  67.0 6.9 %collective-permute-start.16 = (f32[272,128]{1,0:T(8,128)S(1)}, f32[272,128]{1,0:T(8,128)S(1)}, u32[]{:S(2)}, u32[]{:S(2)}) collective-permute-start(f32[272,128]{1,0:T(8,128)S(1)} %get-tuple-element.101), channel_id=1, source_target_pairs={{0,6},{1,7},{2,4},{3,5},{4,2},{5,3},{6,0},{7,1},{8,14},{9,15},{10,... | collective-permute-start | bytes 417800 | tf_op jit(solution)/shard_map/ppermute | solution.py:244
  67.4 2.8 %copy-start.14 = (f32[256,2048]{1,0:T(8,128)}, f32[256,2048]{1,0:T(8,128)S(1)}, u32[]{:S(2)}) copy-start(f32[256,2048]{1,0:T(8,128)S(1)} %collective-permute-done.13.g1_ref) | copy-start | bytes 6291460
  67.4 15.3 %copy-start.27 = (f32[4,272,128]{2,1,0:T(8,128)S(1)}, f32[4,272,128]{2,1,0:T(8,128)}, u32[]{:S(2)}) copy-start(f32[4,272,128]{2,1,0:T(8,128)} %copy-done.26) | copy-start | bytes 1671172
  70.2 5.8 %copy-start.33 = (f32[272,128]{1,0:T(8,128)}, f32[272,128]{1,0:T(8,128)S(1)}, u32[]{:S(2)}) copy-start(f32[272,128]{1,0:T(8,128)S(1)} %collective-permute-done.14) | copy-start | bytes 417796
  73.8 2.8 %copy-start.35 = (f32[272,128]{1,0:T(8,128)}, f32[272,128]{1,0:T(8,128)S(1)}, u32[]{:S(2)}) copy-start(f32[272,128]{1,0:T(8,128)S(1)} %collective-permute-done.15) | copy-start | bytes 417796
  73.8 2.8 %copy-start.37 = (f32[272,128]{1,0:T(8,128)}, f32[272,128]{1,0:T(8,128)S(1)}, u32[]{:S(2)}) copy-start(f32[272,128]{1,0:T(8,128)S(1)} %collective-permute-done.16) | copy-start | bytes 417796
  73.8 38.0 %collective-permute-start.17 = (f32[8,64,768]{2,1,0:T(8,128)}, f32[8,64,768]{2,1,0:T(8,128)}, u32[]{:S(2)}, u32[]{:S(2)}) collective-permute-start(f32[8,64,768]{2,1,0:T(8,128)} %get-tuple-element.102), channel_id=1, source_target_pairs={{0,2},{1,3},{2,0},{3,1},{4,6},{5,7},{6,4},{7,5},{8,10},{9,11},{10,... | collective-permute-start | bytes 4718600 | tf_op jit(solution)/shard_map/ppermute | solution.py:244
  75.1 36.8 %collective-permute-start.18 = (f32[8,64,768]{2,1,0:T(8,128)}, f32[8,64,768]{2,1,0:T(8,128)}, u32[]{:S(2)}, u32[]{:S(2)}) collective-permute-start(f32[8,64,768]{2,1,0:T(8,128)} %get-tuple-element.103), channel_id=1, source_target_pairs={{0,4},{1,5},{2,6},{3,7},{4,0},{5,1},{6,2},{7,3},{8,12},{9,13},{10,... | collective-permute-start | bytes 4718600 | tf_op jit(solution)/shard_map/ppermute | solution.py:244
  76.0 35.9 %collective-permute-start.19 = (f32[8,64,512]{2,1,0:T(8,128)}, f32[8,64,512]{2,1,0:T(8,128)}, u32[]{:S(2)}, u32[]{:S(2)}) collective-permute-start(f32[8,64,512]{2,1,0:T(8,128)} %get-tuple-element.104), channel_id=1, source_target_pairs={{0,8},{1,9},{2,10},{3,11},{4,12},{5,13},{6,14},{7,15},{8,0},{9,1},... | collective-permute-start | bytes 3145736 | tf_op jit(solution)/shard_map/ppermute | solution.py:244
  76.0 6.8 %copy-start.17 = (f32[4,272,128]{2,1,0:T(8,128)S(1)}, f32[4,272,128]{2,1,0:T(8,128)}, u32[]{:S(2)}) copy-start(f32[4,272,128]{2,1,0:T(8,128)} %copy-done.16) | copy-start | bytes 1671172
  76.7 26.0 %collective-permute-start.20 = (f32[272,128]{1,0:T(8,128)}, f32[272,128]{1,0:T(8,128)}, u32[]{:S(2)}, u32[]{:S(2)}) collective-permute-start(f32[272,128]{1,0:T(8,128)} %add_add_fusion.1), channel_id=1, source_target_pairs={{0,8},{1,9},{2,10},{3,11},{4,12},{5,13},{6,14},{7,15},{8,0},{9,1},... | collective-permute-start | bytes 417800 | tf_op jit(solution)/shard_map/ppermute | solution.py:244
  81.5 2.2 %copy-start.8 = (bf16[256,2048]{1,0:T(8,128)(2,1)S(1)}, bf16[256,2048]{1,0:T(8,128)(2,1)}, u32[]{:S(2)}) copy-start(bf16[256,2048]{1,0:T(8,128)(2,1)} %v_ref.7) | copy-start | bytes 3145732
  81.5 2.5 %copy-start.12 = (bf16[256,2048]{1,0:T(8,128)(2,1)S(1)}, bf16[256,2048]{1,0:T(8,128)(2,1)}, u32[]{:S(2)}) copy-start(bf16[256,2048]{1,0:T(8,128)(2,1)} %q_ref.6) | copy-start | bytes 3145732
  84.9 18.9 %copy-start.25 = (f32[4,272,128]{2,1,0:T(8,128)S(1)}, f32[4,272,128]{2,1,0:T(8,128)}, u32[]{:S(2)}) copy-start(f32[4,272,128]{2,1,0:T(8,128)} %copy-done.24) | copy-start | bytes 1671172
  99.3 12.6 %copy-start.34 = (f32[272,128]{1,0:T(8,128)S(1)}, f32[272,128]{1,0:T(8,128)}, u32[]{:S(2)}) copy-start(f32[272,128]{1,0:T(8,128)} %copy-done.33) | copy-start | bytes 417796
  99.3 12.6 %copy-start.36 = (f32[272,128]{1,0:T(8,128)S(1)}, f32[272,128]{1,0:T(8,128)}, u32[]{:S(2)}) copy-start(f32[272,128]{1,0:T(8,128)} %copy-done.35) | copy-start | bytes 417796
  99.3 12.6 %copy-start.38 = (f32[272,128]{1,0:T(8,128)S(1)}, f32[272,128]{1,0:T(8,128)}, u32[]{:S(2)}) copy-start(f32[272,128]{1,0:T(8,128)} %copy-done.37) | copy-start | bytes 417796
  103.7 7.2 %collective-permute-start.21 = (f32[272,128]{1,0:T(8,128)S(1)}, f32[272,128]{1,0:T(8,128)S(1)}, u32[]{:S(2)}, u32[]{:S(2)}) collective-permute-start(f32[272,128]{1,0:T(8,128)S(1)} %add.339), channel_id=1, source_target_pairs={{0,16},{1,17},{2,18},{3,19},{4,20},{5,21},{6,22},{7,23},{8,24},{9,... | collective-permute-start | bytes 417800 | tf_op jit(solution)/shard_map/ppermute | solution.py:244
  112.1 8.1 %collective-permute-start.25 = (f32[2,272,128]{2,1,0:T(8,128)S(1)}, f32[2,272,128]{2,1,0:T(8,128)S(1)}, u32[]{:S(2)}, u32[]{:S(2)}) collective-permute-start(f32[2,272,128]{2,1,0:T(8,128)S(1)} %pad_maximum_fusion.5), channel_id=1, source_target_pairs={{0,4},{1,5},{2,6},{3,7},{4,0},{5,1},{6,2},{7,3},{8,12},{9,13},{10,... | collective-permute-start | bytes 835592 | tf_op jit(solution)/shard_map/ppermute | solution.py:244
  115.1 23.4 %collective-permute-start.24 = (f32[2,2,64,512]{3,2,1,0:T(8,128)S(1)}, f32[2,2,64,512]{3,2,1,0:T(8,128)S(1)}, u32[]{:S(2)}, u32[]{:S(2)}) collective-permute-start(f32[2,2,64,512]{3,2,1,0:T(8,128)S(1)} %bitcast.282), channel_id=1, source_target_pairs={{0,16},{1,17},{2,18},{3,19},{4,20},{5,21},{6,22},{7,23},{8,24},{9,... | collective-permute-start | bytes 1572872 | tf_op jit(solution)/shard_map/ppermute | solution.py:244
  116.5 22.1 %collective-permute-start.23 = (f32[2,2,64,768]{3,2,1,0:T(8,128)S(1)}, f32[2,2,64,768]{3,2,1,0:T(8,128)S(1)}, u32[]{:S(2)}, u32[]{:S(2)}) collective-permute-start(f32[2,2,64,768]{3,2,1,0:T(8,128)S(1)} %fusion.2), channel_id=1, source_target_pairs={{0,2},{1,3},{2,0},{3,1},{4,6},{5,7},{6,4},{7,5},{8,10},{9,11},{10,... | collective-permute-start | bytes 2359304 | tf_op jit(solution)/shard_map/ppermute | solution.py:244
  118.5 20.0 %collective-permute-start.22 = (f32[2,2,64,768]{3,2,1,0:T(8,128)S(1)}, f32[2,2,64,768]{3,2,1,0:T(8,128)S(1)}, u32[]{:S(2)}, u32[]{:S(2)}) collective-permute-start(f32[2,2,64,768]{3,2,1,0:T(8,128)S(1)} %get-tuple-element.146), channel_id=1, source_target_pairs={{0,4},{1,5},{2,6},{3,7},{4,0},{5,1},{6,2},{7,3},{8,12},{9,13},{10,... | collective-permute-start | bytes 2359304 | tf_op jit(solution)/shard_map/ppermute | solution.py:244
  120.2 18.3 %collective-permute-start.26 = (f32[2,272,128]{2,1,0:T(8,128)S(1)}, f32[2,272,128]{2,1,0:T(8,128)S(1)}, u32[]{:S(2)}, u32[]{:S(2)}) collective-permute-start(f32[2,272,128]{2,1,0:T(8,128)S(1)} %pad_maximum_fusion.6), channel_id=1, source_target_pairs={{0,2},{1,3},{2,0},{3,1},{4,6},{5,7},{6,4},{7,5},{8,10},{9,11},{10,... | collective-permute-start | bytes 835592 | tf_op jit(solution)/shard_map/ppermute | solution.py:244
  138.9 3.2 %copy-start.23 = (f32[4,272,128]{2,1,0:T(8,128)S(1)}, f32[4,272,128]{2,1,0:T(8,128)}, u32[]{:S(2)}) copy-start(f32[4,272,128]{2,1,0:T(8,128)} %copy-done.22) | copy-start | bytes 1671172
  139.0 22.3 %collective-permute-start.30 = (f32[4,272,128]{2,1,0:T(8,128)S(1)}, f32[4,272,128]{2,1,0:T(8,128)S(1)}, u32[]{:S(2)}, u32[]{:S(2)}) collective-permute-start(f32[4,272,128]{2,1,0:T(8,128)S(1)} %pad_maximum_fusion.2), channel_id=1, source_target_pairs={{0,1},{1,0},{2,3},{3,2},{4,5},{5,4},{6,7},{7,6},{8,9},{9,8},{10,11... | collective-permute-start | bytes 1671176 | tf_op jit(solution)/shard_map/ppermute | solution.py:244
  139.1 20.6 %collective-permute-start.28 = (f32[2,64,768]{2,1,0:T(8,128)S(1)}, f32[2,64,768]{2,1,0:T(8,128)S(1)}, u32[]{:S(2)}, u32[]{:S(2)}) collective-permute-start(f32[2,64,768]{2,1,0:T(8,128)S(1)} %get-tuple-element.151), channel_id=1, source_target_pairs={{0,16},{1,17},{2,18},{3,19},{4,20},{5,21},{6,22},{7,23},{8,24},{9,... | collective-permute-start | bytes 1179656 | tf_op jit(solution)/shard_map/ppermute | solution.py:244
  141.8 19.5 %collective-permute-start.27 = (f32[2,64,768]{2,1,0:T(8,128)S(1)}, f32[2,64,768]{2,1,0:T(8,128)S(1)}, u32[]{:S(2)}, u32[]{:S(2)}) collective-permute-start(f32[2,64,768]{2,1,0:T(8,128)S(1)} %get-tuple-element.153), channel_id=1, source_target_pairs={{0,8},{1,9},{2,10},{3,11},{4,12},{5,13},{6,14},{7,15},{8,0},{9,1},... | collective-permute-start | bytes 1179656 | tf_op jit(solution)/shard_map/ppermute | solution.py:244
  141.8 8.4 %collective-permute-start.29 = (f32[2,64,512]{2,1,0:T(8,128)S(1)}, f32[2,64,512]{2,1,0:T(8,128)S(1)}, u32[]{:S(2)}, u32[]{:S(2)}) collective-permute-start(f32[2,64,512]{2,1,0:T(8,128)S(1)} %get-tuple-element.158), channel_id=1, source_target_pairs={{0,2},{1,3},{2,0},{3,1},{4,6},{5,7},{6,4},{7,5},{8,10},{9,11},{10,... | collective-permute-start | bytes 786440 | tf_op jit(solution)/shard_map/ppermute | solution.py:244
  161.4 5.2 %collective-permute-start.33 = (f32[64,512]{1,0:T(8,128)S(1)}, f32[64,512]{1,0:T(8,128)S(1)}, u32[]{:S(2)}, u32[]{:S(2)}) collective-permute-start(f32[64,512]{1,0:T(8,128)S(1)} %fusion.60), channel_id=1, source_target_pairs={{0,4},{1,5},{2,6},{3,7},{4,0},{5,1},{6,2},{7,3},{8,12},{9,13},{10,... | collective-permute-start | bytes 393224 | tf_op jit(solution)/shard_map/ppermute | solution.py:244
  161.9 7.3 %collective-permute-start.32 = (f32[64,768]{1,0:T(8,128)S(1)}, f32[64,768]{1,0:T(8,128)S(1)}, u32[]{:S(2)}, u32[]{:S(2)}) collective-permute-start(f32[64,768]{1,0:T(8,128)S(1)} %fusion.19), channel_id=1, source_target_pairs={{0,8},{1,9},{2,10},{3,11},{4,12},{5,13},{6,14},{7,15},{8,0},{9,1},... | collective-permute-start | bytes 589832 | tf_op jit(solution)/shard_map/ppermute | solution.py:244
  162.4 11.1 %collective-permute-start.31 = (f32[64,768]{1,0:T(8,128)S(1)}, f32[64,768]{1,0:T(8,128)S(1)}, u32[]{:S(2)}, u32[]{:S(2)}) collective-permute-start(f32[64,768]{1,0:T(8,128)S(1)} %fusion.21), channel_id=1, source_target_pairs={{0,16},{1,17},{2,18},{3,19},{4,20},{5,21},{6,22},{7,23},{8,24},{9,... | collective-permute-start | bytes 589832 | tf_op jit(solution)/shard_map/ppermute | solution.py:244
  (10 other events, 13.5 us)

commit v3 on v2

--- a/solution.py
+++ b/solution.py
@@ -17,7 +17,7 @@
 NN = (((1,), (0,)), ((), ()))
 NT = (((1,), (1,)), ((), ()))
 TN = (((0,), (0,)), ((), ()))
-PARTS = ((0, 768, (0, 1, 2, 3)), (768, 768, (1, 0, 3, 2)), (1536, 512, (2, 3, 0, 1)))
+PARTS = ((0, 768, (0, 1, 2, 3)), (768, 768, (1, 2, 3, 0)), (1536, 512, (2, 0, 1, 3)))
 PAIRS = HEADS // 2
 PLACES = PAIRS // 2
 VMEM_LIMIT = 12 * 1024 * 1024
@@ -152,29 +152,34 @@
         send_ref[place, 2 * HEAD :, :] = jnp.zeros((HEADS, HEAD), F32)
 
 
-def forward_kernel(
-    at_ref, q_ref, nd_ref, gt_ref, inv_ref, s0_ref, s1_ref, dkeep_ref, dmate_ref,
-    keep_ref, send_ref, dd_ref, t0_ref, t1_ref, t2_ref, t3_ref, dz_ref,
-):
+def attended_of(q_ref, nd_ref, inv_ref, s_ref, place, r, head, cols):
+    state = s_ref[place, pl.ds(r * HEAD, HEAD), :]
+    fqs = split(feature(q_ref[:, cols].astype(F32)))
+    inv = inv_ref[head, :1, :]
+    return (nd_ref[head, :HEAD, :] + mm(split(state), fqs, NT)) * inv, inv, fqs
+
+
+def forward_kernel(at_ref, q_ref, nd_ref, inv_ref, s0_ref, s1_ref, keep_ref, send_ref):
     me = at_ref[0]
     core, chip = me % 2, me // 2
 
     def one(side, place, r, head, cols):
-        state = (s0_ref, s1_ref)[side][place, pl.ds(r * HEAD, HEAD), :]
-        fqs = split(feature(q_ref[:, cols].astype(F32)))
-        inv = inv_ref[head, :1, :]
-        att = (nd_ref[head, :HEAD, :] + mm(split(state), fqs, NT)) * inv
+        att, _, _ = attended_of(q_ref, nd_ref, inv_ref, (s0_ref, s1_ref)[side], place, r, head, cols)
         low, high = att[:HALF], att[HALF:]
         keep_ref[head ^ chip] = jnp.where(core == 0, low, high)
         send_ref[head ^ chip] = jnp.where(core == 0, high, low)
+
+    each_head(at_ref, one)
+
+
+def denominator_kernel(at_ref, q_ref, nd_ref, gt_ref, inv_ref, s0_ref, s1_ref, dd_ref, dz_ref):
+    def one(side, place, r, head, cols):
+        att, inv, fqs = attended_of(q_ref, nd_ref, inv_ref, (s0_ref, s1_ref)[side], place, r, head, cols)
         dd = -jnp.sum(gt_ref[head] * att, axis=0, keepdims=True) * inv
         dd_ref[head] = first_of(dd)
         dz_ref[pl.ds(head, 1), :] = times_row(dd, fqs, NN)
 
     each_head(at_ref, one)
-    for j, t_ref in enumerate((t0_ref, t1_ref, t2_ref, t3_ref)):
-        t_ref[: 2 * HEAD, :] = dkeep_ref[j, : 2 * HEAD, :] + dmate_ref[j, : 2 * HEAD, :]
-        t_ref[2 * HEAD :, :] = dz_ref[...]
 
 
 def backward_kernel(
@@ -277,10 +282,8 @@
     return out
 
 
-def halves(keep, got, left, bit):
-    axis = left.index(bit)
-    take = lambda a, i: lax.index_in_dim(a, i, axis, keepdims=False)
-    return take(keep, 1) + take(got, 1), take(keep, 0) + take(got, 0)
+def half(a, left, bit, which):
+    return lax.index_in_dim(a.reshape((2,) * len(left) + a.shape[-2:]), which, left.index(bit), keepdims=False)
 
 
 def body(queries, keys, values, out_weight, out_grad):
@@ -296,6 +299,7 @@
     narrow = shape((t, HEADS * HEAD), BF16)
     places = range(PLACES)
     own_sums = lambda x: x[2 * HEAD :]
+    with_sums = lambda x, tail: jnp.concatenate([x[: 2 * HEAD], tail])
 
     keep, send = call(summary_kernel, packs, at, keys, values, scratch=(pltpu.VMEM((HEADS, HEAD), F32),))
     mate = swap(send, 1)
@@ -319,23 +323,13 @@
     s1 = swap(jnp.stack([x + jnp.where(core == 0, keep[j], 0.0) for j, x in enumerate(back)]), 1)
     s0 = jnp.stack([x + jnp.where(core == 1, mate[j], 0.0) for j, x in enumerate(back)])
 
-    half = shape((HEADS, HALF, t), F32)
-    a_keep, a_send, dd, *dtotal = call(
-        forward_kernel,
-        [half, half, row] + [shape((PACK, HEAD), F32)] * PLACES,
-        at,
-        queries,
-        inner,
-        gt,
-        inv,
-        s0,
-        s1,
-        dkeep,
-        dmate,
-        scratch=(pltpu.VMEM((HEADS, HEAD), F32),),
+    tall = shape((HEADS, HALF, t), F32)
+    dtotal = [dkeep[j] + dmate[j] for j in places]
+    dgot = [dtotal[0]] + [swap(dtotal[j], 2 * j) for j in places[1:]]
+    a_keep, a_send = call(
+        forward_kernel, [tall, tall], at, after(dtotal, queries), inner, inv, s0, s1
     )
     a_mate = swap(a_send, 1)
-    dgot = [dtotal[0]] + [swap(dtotal[j], 2 * j) for j in places[1:]]
 
     weight = lambda bit: call(
         functools.partial(weight_kernel, bit),
@@ -349,10 +343,13 @@
     sends, dgot = lax.optimization_barrier((list(weight(1)), dgot))
     a_mate = after(sends, a_mate)
     keeps = weight(0)
-    dlayer = dgot[0] + dgot[1] + dgot[2] + dgot[3]
     gots = [swap(send, 2 << order[0]) for send, (_, _, order) in zip(sends, PARTS, strict=True)]
+    dd, dz = call(
+        denominator_kernel, [row, sums], at, after(sends, queries), inner, gt, inv, s0, s1
+    )
+    dlayer = with_sums(dgot[0] + dgot[1] + dgot[2] + dgot[3], dz)
     dfirst = swap(dlayer, 8)
-    queries = after((keeps, dlayer), queries)
+    queries = after(dlayer, queries)
     query_grad, dk, dv = call(
         backward_kernel, [narrow, wide, wide], at, queries, keys, values, gt, inv, dd, z_in, s0, s1
     )
@@ -360,29 +357,33 @@
     gots, douter = lax.optimization_barrier((gots, douter))
     dback = [douter + before(dgot, j, plane, True) for j in places]
 
+    behind = own_sums(douter)
     lefts = [sorted(order[1:], reverse=True) for _, _, order in PARTS]
     for turn in range(1, 4):
-        sends, kept = [], []
-        for keep_part, got, left, (_, width, order) in zip(keeps, gots, lefts, PARTS, strict=True):
-            shaped = (2,) * len(left) + (HALF, width)
-            send, keep_part = halves(keep_part.reshape(shaped), got.reshape(shaped), left, order[turn])
-            sends.append(send)
-            kept.append(keep_part)
-            left.remove(order[turn])
-        keeps = kept
-        gots = [swap(send, 2 << order[turn]) for send, (_, _, order) in zip(sends, PARTS, strict=True)]
-        if turn == 1:
-            dz, dz_part = own_sums(dgot[0]), own_sums(dback[0])
-            up = swap(jnp.stack(dback[2:]), 4)
-            across = swap(jnp.stack([dback[1], up[1]]), 2)
-            dback = [dback[0], across[0], up[0], across[1]]
-            gots, dback = lax.optimization_barrier((gots, dback))
-        elif turn == 2:
-            other = [(x + jnp.where(core == 1, dkeep[j], 0.0))[: 2 * HEAD] for j, x in enumerate(dback)]
-            other = [jnp.concatenate([x, dz_part if j == 0 else dz]) for j, x in enumerate(other)]
-            l1 = swap(after(sends, jnp.stack(other)), 1)
+        bits = [order[turn] for _, _, order in PARTS]
+        lists = list(zip(keeps, gots, lefts, bits, strict=True))
+        sends = [half(k, left, bit, 1) + half(g, left, bit, 1) for k, g, left, bit in lists]
+        keeps, gots = after(sends, keeps, gots)
+        lists = list(zip(keeps, gots, lefts, bits, strict=True))
+        keeps = [half(k, left, bit, 0) + half(g, left, bit, 0) for k, g, left, bit in lists]
+        lefts = [[b for b in left if b != bit] for left, bit in zip(lefts, bits, strict=True)]
+        gots = [swap(send, 2 << bit) for send, bit in zip(sends, bits, strict=True)]
+        if turn == 2:
+            behind, dz_beside = behind + own_sums(across[0]), own_sums(across[1])
+            up = jnp.stack([with_sums(dback[2], behind), with_sums(across[1], dz + dz_beside)])
+            up = swap(after(sends, up), 4)
+            dz_part = behind + own_sums(up[0]) + jnp.where((plane ^ 1) > plane, dz_beside, 0.0)
+            dz_part = dz_part + jnp.where((plane ^ 2) > plane, own_sums(up[1]), 0.0)
+            dback = [dback[0], across[0], up[0], up[1]]
+            other = [x + jnp.where(core == 1, dkeep[j], 0.0) for j, x in enumerate(dback)]
+            other = [with_sums(x, dz_part if j == 0 else dz) for j, x in enumerate(other)]
+            l1 = swap(jnp.stack(other), 1)
             l0 = jnp.stack([x + jnp.where(core == 0, dmate[j], 0.0) for j, x in enumerate(dback)])
-            gots, l1 = lax.optimization_barrier((gots, l1))
+            gots, l0, l1 = lax.optimization_barrier((gots, l0, l1))
+        elif turn == 1:
+            across = jnp.stack([with_sums(dback[1], behind), with_sums(dback[3], dz)])
+            across = swap(after(sends, across), 2)
+            gots, across = lax.optimization_barrier((gots, across))
     l0 = after(sends, l0)
     dz_in = dz_part + own_sums(l1[0]) + jnp.where(core == 0, own_sums(l1[1]), 0.0)
     key_grad, value_grad = call(finish_kernel, [narrow, narrow], at, keys, values, dk, dv, dz_in, l0, l1)

time: 175 us -> 165 us (0.943)
  waiting for transfers between devices: 59.9 us -> 43.6 us
  starting transfers between devices: 37.5 us -> 40.8 us
  Pallas kernels: 47.1 us -> 50.1 us
    ppermute x31, waiting for transfers between devices: 59.9 us -> 43.6 us  [swap(): return lax.ppermute(x, 'seq', [(i, i ^ mask) for i in range(n)])]
    ppermute x31, starting transfers between devices: 26.5 us -> 29.8 us  [swap(): return lax.ppermute(x, 'seq', [(i, i ^ mask) for i in range(n)])]
    pallas_call x8 -> x9, Pallas kernels: 43.1 us -> 46.1 us  [call(): pl.pallas_call(kernel, out_shape=tuple(outs), in_specs=specs, out_specs=t...]
    add x11 -> x22, other arithmetic: 6.5 us -> 8.8 us  [the longest x9 3.88 us: body(): half(k, left, bit, 1) + half(g, left, bit, 1)]
    unnamed x80 -> x88, local copies, waits for them, and re-layouts: 14.7 us -> 14.8 us
  transfers between devices with their start and end apart: 34 -> 34, of which waited for: 12 -> 14; matrix products, arithmetic and copies ran while one was open for 5% -> 5% of each run, Pallas kernels for 26% -> 29%
where the time goes in v3:
time: 165 us
  Pallas kernels  50.1 us (30%)
  waiting for transfers between devices  43.6 us (26%)
  starting transfers between devices  40.8 us (25%)
  local copies, waits for them, and re-layouts  14.9 us (9%)
  other arithmetic  14.2 us (9%)
    pallas_call x9, Pallas kernels, call(): pl.pallas_call(kernel, out_shape=tuple(outs), in_specs=specs, out_specs=t...  46.1 us
    ppermute x31, waiting for transfers between devices, swap(): return lax.ppermute(x, 'seq', [(i, i ^ mask) for i in range(n)])  43.6 us
    ppermute x31, starting transfers between devices, swap(): return lax.ppermute(x, 'seq', [(i, i ^ mask) for i in range(n)])  29.8 us
    unnamed x88, local copies, waits for them, and re-layouts  14.8 us
    ppermute x3, starting transfers between devices, along(): lax.ppermute(layer, 'seq', [(b, a) for a, b in pairs] if later else pairs)  11 us
    pallas_call x1, Pallas kernels, attended_grad(): pl.pallas_call(grad_kernel, grid=(PAIRS,), out_shape=(jax.ShapeDtypeStruc...  4.01 us
    add x9, other arithmetic, body(): half(k, left, bit, 1) + half(g, left, bit, 1)  3.88 us
    add x6, other arithmetic, body(): half(k, left, bit, 0) + half(g, left, bit, 0)  3.81 us
  transfers between devices with their start and end apart: 34, of which 14 were waited for; matrix products, arithmetic and copies ran while one was open for 5% of the time, Pallas kernels for 29%

profile of v3, /device:TPU:0, one launch (start us, length us, event | category | flops | bytes accessed | tf_op | source)
XLA Modules:
  0.0 164.8 jit_solution(5603738657879697791)
XLA Ops:
  0.6 1.2 copy-done.6
  1.9 1.2 copy-done.10
  3.1 2.4 %shard_map.84 = (f32[4,272,128]{2,1,0:T(8,128)S(1)}, f32[4,272,128]{2,1,0:T(8,128)S(1)}) custom-call(s32[1]{0:T(128)} %bitcast.at_ref, bf16[256,2048]{1,0:T(8,128)(2,1)S(1)} %copy-done.6, bf16[256,2048]{1,0:T(8,128)(2,1)S(1)} %copy-done.10), custom_call_target="tpu_custom_call" | custom-call | flops 1000 | bytes 1000 | tf_op jit(solution)/shard_map/pallas_call | solution.py:236
  6.0 1.6 collective-permute-done
  7.7 2.9 %collective-permute-start.1 = (f32[272,128]{1,0:T(8,128)S(1)}, f32[272,128]{1,0:T(8,128)S(1)}, u32[]{:S(2)}, u32[]{:S(2)}) collective-permute-start(f32[272,128]{1,0:T(8,128)S(1)} %get-tuple-element.184), channel_id=1, source_target_pairs={{0,2},{1,3},{2,0},{3,1},{4,6},{5,7},{6,4},{7,5},{8,10},{9,11},{10,... | collective-permute-start | bytes 417800 | tf_op jit(solution)/shard_map/ppermute | solution.py:249
  10.6 1.5 collective-permute-start.2
  12.2 7.7 %shard_map.85.nd_ref = f32[16,136,256]{2,1,0:T(8,128)S(1)} custom-call(s32[1]{0:T(128)} %bitcast.at_ref, bf16[256,2048]{1,0:T(8,128)(2,1)S(1)} %copy-done, bf16[256,2048]{1,0:T(8,128)(2,1)S(1)} %copy-done.7, bf16[256,2048]{1,0:T(8,128)(2,1)S(1)} %copy-done.10), custom_call_target="tpu_custom_call" | custom-call | flops 1000 | bytes 1000 | tf_op jit(solution)/shard_map/pallas_call | solution.py:236
  19.9 0.8 fusion.28
  20.7 4.6 %collective-permute-start.4 = (f32[272,128]{1,0:T(8,128)}, f32[272,128]{1,0:T(8,128)}, u32[]{:S(2)}, u32[]{:S(2)}) collective-permute-start(f32[272,128]{1,0:T(8,128)} %get-tuple-element.92), channel_id=1, source_target_pairs={{0,8},{1,9},{2,10},{3,11},{4,12},{5,13},{6,14},{7,15},{8,16},{9,17... | collective-permute-start | bytes 417800 | tf_op jit(solution)/shard_map/ppermute | solution.py:262
  25.3 4.5 %collective-permute-start.5 = (f32[272,128]{1,0:T(8,128)}, f32[272,128]{1,0:T(8,128)}, u32[]{:S(2)}, u32[]{:S(2)}) collective-permute-start(f32[272,128]{1,0:T(8,128)} %get-tuple-element.92), channel_id=1, source_target_pairs={{0,16},{1,17},{2,18},{3,19},{4,20},{5,21},{6,22},{7,23},{8,24},{9,... | collective-permute-start | bytes 417800 | tf_op jit(solution)/shard_map/ppermute | solution.py:262
  29.8 1.9 %collective-permute-start.6 = (f32[272,128]{1,0:T(8,128)}, f32[272,128]{1,0:T(8,128)}, u32[]{:S(2)}, u32[]{:S(2)}) collective-permute-start(f32[272,128]{1,0:T(8,128)} %get-tuple-element.92), channel_id=1, source_target_pairs={{0,24},{1,25},{2,26},{3,27},{4,28},{5,29},{6,30},{7,31}} | collective-permute-start | bytes 417800 | tf_op jit(solution)/shard_map/ppermute | solution.py:262
  31.7 3.4 %copy-done.13 = bf16[2048,2048]{1,0:T(8,128)(2,1)S(1)} copy-done((bf16[2048,2048]{1,0:T(8,128)(2,1)S(1)}, bf16[2048,2048]{1,0:T(8,128)(2,1)}, u32[]{:S(2)}) %copy-start.13) | copy-done | bytes 8388632
  35.1 4.0 %shard_map.86 = (f32[16,128,256]{2,1,0:T(8,128)S(1)}, f32[256,2048]{1,0:T(8,128)S(1)}) custom-call(bf16[256,2048]{1,0:T(8,128)(2,1)S(1)} %copy-done.3, bf16[2048,2048]{1,0:T(8,128)(2,1)S(1)} %copy-done.13, bf16[256,2048]{1,0:T(8,128)(2,1)S(1)} %copy-done.3), custom_call_target="tpu_custom_call" | custom-call | flops 1000 | bytes 1000 | tf_op jit(solution)/shard_map/pallas_call | solution.py:119
  39.1 1.3 copy-done.1
  40.5 1.3 copy-done.26
  41.8 1.3 fusion.37
  43.1 1.1 fusion.34
  44.2 1.6 collective-permute-start.7
  45.7 1.5 collective-permute-start.8
  47.7 0.7 fusion.48.z_ref
  48.4 4.8 %shard_map.87 = (f32[4,272,128]{2,1,0:T(8,128)S(1)}, f32[4,272,128]{2,1,0:T(8,128)S(1)}, f32[16,8,256]{2,1,0:T(8,128)S(1)}) custom-call(s32[1]{0:T(128)} %bitcast.at_ref, bf16[256,2048]{1,0:T(8,128)(2,1)S(1)} %copy-done, f32[16,136,256]{2,1,0:T(8,128)S(1)} %shard_map.85.nd_ref, f32[16,128,256]{2,1,0:T(8,128)S(1)} %copy-done.2, f32[16,128]{1,0:T(8,128)S(1)} %fusion.48.z_ref), custom_call_target="tpu_custom_call" | custom-call | flops 1000 | bytes 1000 | tf_op jit(solution)/shard_map/pallas_call | solution.py:236
  54.4 1.2 collective-permute-done.10
  55.6 0.9 add_bitcast_fusion
  56.6 2.8 %shard_map.88 = (f32[16,64,256]{2,1,0:T(8,128)S(1)}, f32[16,64,256]{2,1,0:T(8,128)S(1)}) custom-call(s32[1]{0:T(128)} %bitcast.at_ref, bf16[256,2048]{1,0:T(8,128)(2,1)S(1)} %copy-done, f32[16,136,256]{2,1,0:T(8,128)S(1)} %shard_map.85.nd_ref, f32[16,8,256]{2,1,0:T(8,128)S(1)} %get-tuple-element.104.inv_ref, f32[4,272,128]{2,1,0:T(8,128)S(1)} %pad_maximum_fusion.s0_ref, ...), custom_call_target="tpu_custom_call" | custom-call | flops 1000 | bytes 1000 | tf_op jit(solution)/shard_map/pallas_call | solution.py:236
  59.7 1.5 collective-permute-start.14
  61.2 1.5 collective-permute-start.15
  63.2 3.0 %shard_map.89 = (f32[8,64,768]{2,1,0:T(8,128)}, f32[8,64,768]{2,1,0:T(8,128)}, f32[8,64,512]{2,1,0:T(8,128)}) custom-call(f32[16,64,256]{2,1,0:T(8,128)S(1)} %get-tuple-element.109.a0_ref, f32[16,64,256]{2,1,0:T(8,128)S(1)} %collective-permute-done.12.a1_ref, bf16[256,2048]{1,0:T(8,128)(2,1)S(1)} %copy-done.4, f32[256,2048]{1,0:T(8,128)S(1)} %collective-permute-done.13.g1_ref), custom_call_target="tpu_custom_call" | custom-call | flops 1000 | bytes 1000 | tf_op jit(solution)/shard_map/pallas_call | solution.py:236
  66.2 3.4 %collective-permute-done.15 = f32[272,128]{1,0:T(8,128)S(1)} collective-permute-done((f32[272,128]{1,0:T(8,128)S(1)}, f32[272,128]{1,0:T(8,128)S(1)}, u32[]{:S(2)}, u32[]{:S(2)}) %collective-permute-start.15) | collective-permute-done | bytes 139296 | tf_op jit(solution)/shard_map/ppermute | solution.py:249
  69.6 1.2 collective-permute-start.17
  70.8 0.9 collective-permute-start.18
  71.7 5.7 %shard_map.90 = (f32[16,8,256]{2,1,0:T(8,128)S(1)}, f32[16,128]{1,0:T(8,128)S(1)}) custom-call(s32[1]{0:T(128)} %bitcast.at_ref, bf16[256,2048]{1,0:T(8,128)(2,1)S(1)} %copy-done, f32[16,136,256]{2,1,0:T(8,128)S(1)} %shard_map.85.nd_ref, f32[16,128,256]{2,1,0:T(8,128)S(1)} %copy-done.2, f32[16,8,256]{2,1,0:T(8,128)S(1)} %get-tuple-element.104.inv_ref, ...), custom_call_target="tpu_custom_call" | custom-call | flops 1000 | bytes 1000 | tf_op jit(solution)/shard_map/pallas_call | solution.py:236
  77.5 2.1 %collective-permute-start.20 = (f32[272,128]{1,0:T(8,128)S(1)}, f32[272,128]{1,0:T(8,128)S(1)}, u32[]{:S(2)}, u32[]{:S(2)}) collective-permute-start(f32[272,128]{1,0:T(8,128)S(1)} %pad_maximum_fusion.9), channel_id=1, source_target_pairs={{0,8},{1,9},{2,10},{3,11},{4,12},{5,13},{6,14},{7,15},{8,0},{9,1},... | collective-permute-start | bytes 417800 | tf_op jit(solution)/shard_map/ppermute | solution.py:249
  79.6 14.4 %shard_map.91 = (bf16[256,2048]{1,0:T(8,128)(2,1)}, f32[256,2048]{1,0:T(8,128)S(1)}, f32[256,2048]{1,0:T(8,128)S(1)}) custom-call(s32[1]{0:T(128)} %bitcast.at_ref, bf16[256,2048]{1,0:T(8,128)(2,1)S(1)} %copy-done, bf16[256,2048]{1,0:T(8,128)(2,1)S(1)} %copy-done.8, bf16[256,2048]{1,0:T(8,128)(2,1)S(1)} %copy-done.11, f32[16,128,256]{2,1,0:T(8,128)S(1)} %copy-done.2, ...), custom_call_target="tpu_custom_call" | custom-call | flops 1000 | bytes 1000 | tf_op jit(solution)/shard_map/pallas_call | solution.py:236
  94.0 1.3 copy-done.22
  95.3 1.4 copy-done.24
  96.7 1.7 %collective-permute-done.20 = f32[272,128]{1,0:T(8,128)S(1)} collective-permute-done((f32[272,128]{1,0:T(8,128)S(1)}, f32[272,128]{1,0:T(8,128)S(1)}, u32[]{:S(2)}, u32[]{:S(2)}) %collective-permute-start.20) | collective-permute-done | bytes 139296 | tf_op jit(solution)/shard_map/ppermute | solution.py:249
  98.4 0.6 copy-done.37
  99.1 1.6 copy-done.15
  100.7 1.2 copy-done.19
  101.9 1.3 shard_map.92
  103.1 3.1 %collective-permute-done.21 = f32[272,128]{1,0:T(8,128)S(1)} collective-permute-done((f32[272,128]{1,0:T(8,128)S(1)}, f32[272,128]{1,0:T(8,128)S(1)}, u32[]{:S(2)}, u32[]{:S(2)}) %collective-permute-start.21) | collective-permute-done | bytes 139296 | tf_op jit(solution)/shard_map/ppermute | solution.py:249
  106.5 1.1 fusion.5
  107.6 0.6 collective-permute-start.24
  108.2 1.2 fusion.1
  109.5 1.3 fusion.3
  110.8 1.3 collective-permute-start.22
  112.3 1.8 %collective-permute-start.25 = (f32[2,272,128]{2,1,0:T(8,128)S(1)}, f32[2,272,128]{2,1,0:T(8,128)S(1)}, u32[]{:S(2)}, u32[]{:S(2)}) collective-permute-start(f32[2,272,128]{2,1,0:T(8,128)S(1)} %pad_maximum_fusion.10), channel_id=1, source_target_pairs={{0,2},{1,3},{2,0},{3,1},{4,6},{5,7},{6,4},{7,5},{8,10},{9,11},{10,... | collective-permute-start | bytes 835592 | tf_op jit(solution)/shard_map/ppermute | solution.py:249
  114.2 1.3 slice_add_fusion
  115.5 1.2 fusion.4
  116.7 1.2 fusion.2
  118.0 7.6 %collective-permute-done.25 = f32[2,272,128]{2,1,0:T(8,128)S(1)} collective-permute-done((f32[2,272,128]{2,1,0:T(8,128)S(1)}, f32[2,272,128]{2,1,0:T(8,128)S(1)}, u32[]{:S(2)}, u32[]{:S(2)}) %collective-permute-start.25) | collective-permute-done | bytes 278560 | tf_op jit(solution)/shard_map/ppermute | solution.py:249
  125.6 1.2 collective-permute-done.23
  126.8 1.5 collective-permute-done.22
  128.4 1.8 %collective-permute-start.29 = (f32[2,64,512]{2,1,0:T(8,128)S(1)}, f32[2,64,512]{2,1,0:T(8,128)S(1)}, u32[]{:S(2)}, u32[]{:S(2)}) collective-permute-start(f32[2,64,512]{2,1,0:T(8,128)S(1)} %fusion.9), channel_id=1, source_target_pairs={{0,4},{1,5},{2,6},{3,7},{4,0},{5,1},{6,2},{7,3},{8,12},{9,13},{10,... | collective-permute-start | bytes 786440 | tf_op jit(solution)/shard_map/ppermute | solution.py:249
  130.6 1.4 collective-permute-start.27
  132.6 7.7 %collective-permute-done.26 = f32[2,272,128]{2,1,0:T(8,128)S(1)} collective-permute-done((f32[2,272,128]{2,1,0:T(8,128)S(1)}, f32[2,272,128]{2,1,0:T(8,128)S(1)}, u32[]{:S(2)}, u32[]{:S(2)}) %collective-permute-start.26) | collective-permute-done | bytes 278560 | tf_op jit(solution)/shard_map/ppermute | solution.py:249
  140.8 7.1 %collective-permute-done.28 = f32[2,64,768]{2,1,0:T(8,128)S(1)} collective-permute-done((f32[2,64,768]{2,1,0:T(8,128)S(1)}, f32[2,64,768]{2,1,0:T(8,128)S(1)}, u32[]{:S(2)}, u32[]{:S(2)}) %collective-permute-start.28) | collective-permute-done | bytes 393248 | tf_op jit(solution)/shard_map/ppermute | solution.py:249
  147.9 1.5 collective-permute-start.33
  149.4 1.8 %collective-permute-start.32 = (f32[64,768]{1,0:T(8,128)S(1)}, f32[64,768]{1,0:T(8,128)S(1)}, u32[]{:S(2)}, u32[]{:S(2)}) collective-permute-start(f32[64,768]{1,0:T(8,128)S(1)} %fusion.11), channel_id=1, source_target_pairs={{0,2},{1,3},{2,0},{3,1},{4,6},{5,7},{6,4},{7,5},{8,10},{9,11},{10,... | collective-permute-start | bytes 589832 | tf_op jit(solution)/shard_map/ppermute | solution.py:249
  151.2 1.6 collective-permute-start.31
  152.8 4.1 %shard_map.93 = (bf16[256,2048]{1,0:T(8,128)(2,1)}, bf16[256,2048]{1,0:T(8,128)(2,1)}) custom-call(s32[1]{0:T(128)} %bitcast.at_ref, bf16[256,2048]{1,0:T(8,128)(2,1)S(1)} %copy-done.9, bf16[256,2048]{1,0:T(8,128)(2,1)S(1)} %copy-done.12, f32[256,2048]{1,0:T(8,128)S(1)} %copy-done.23, f32[256,2048]{1,0:T(8,128)S(1)} %copy-done.25, ...), custom_call_target="tpu_custom_call" | custom-call | flops 1000 | bytes 1000 | tf_op jit(solution)/shard_map/pallas_call | solution.py:236
  156.9 3.6 %collective-permute-done.33 = f32[64,512]{1,0:T(8,128)S(1)} collective-permute-done((f32[64,512]{1,0:T(8,128)S(1)}, f32[64,512]{1,0:T(8,128)S(1)}, u32[]{:S(2)}, u32[]{:S(2)}) %collective-permute-start.33) | collective-permute-done | bytes 131104 | tf_op jit(solution)/shard_map/ppermute | solution.py:249
  160.5 3.4 %collective-permute-done.31 = f32[64,768]{1,0:T(8,128)S(1)} collective-permute-done((f32[64,768]{1,0:T(8,128)S(1)}, f32[64,768]{1,0:T(8,128)S(1)}, u32[]{:S(2)}, u32[]{:S(2)}) %collective-permute-start.31) | collective-permute-done | bytes 196640 | tf_op jit(solution)/shard_map/ppermute | solution.py:249
  164.0 0.8 pad_maximum_fusion.4
  (157 shorter events, 5.4 us)
Async XLA Ops:
  3.1 9.1 %copy-start = (bf16[256,2048]{1,0:T(8,128)(2,1)S(1)}, bf16[256,2048]{1,0:T(8,128)(2,1)}, u32[]{:S(2)}) copy-start(bf16[256,2048]{1,0:T(8,128)(2,1)} %q_ref.6) | copy-start | bytes 3145732
  3.1 9.1 %copy-start.7 = (bf16[256,2048]{1,0:T(8,128)(2,1)S(1)}, bf16[256,2048]{1,0:T(8,128)(2,1)}, u32[]{:S(2)}) copy-start(bf16[256,2048]{1,0:T(8,128)(2,1)} %k_ref.7) | copy-start | bytes 3145732
  5.5 14.4 %copy-start.20 = (f32[4,272,128]{2,1,0:T(8,128)}, f32[4,272,128]{2,1,0:T(8,128)S(1)}, u32[]{:S(2)}) copy-start(f32[4,272,128]{2,1,0:T(8,128)S(1)} %get-tuple-element.89) | copy-start | bytes 1671172
  5.5 2.1 %collective-permute-start = (f32[4,272,128]{2,1,0:T(8,128)S(1)}, f32[4,272,128]{2,1,0:T(8,128)S(1)}, u32[]{:S(2)}, u32[]{:S(2)}) collective-permute-start(f32[4,272,128]{2,1,0:T(8,128)S(1)} %get-tuple-element.90), channel_id=1, source_target_pairs={{0,1},{1,0},{2,3},{3,2},{4,5},{5,4},{6,7},{7,6},{8,9},{9,8},{10,11... | collective-permute-start | bytes 1671176 | tf_op jit(solution)/shard_map/ppermute | solution.py:249
  7.6 12.3 %copy-start.27 = (f32[4,272,128]{2,1,0:T(8,128)}, f32[4,272,128]{2,1,0:T(8,128)S(1)}, u32[]{:S(2)}) copy-start(f32[4,272,128]{2,1,0:T(8,128)S(1)} %collective-permute-done) | copy-start | bytes 1671172
  7.7 12.2 %collective-permute-start.1 = (f32[272,128]{1,0:T(8,128)S(1)}, f32[272,128]{1,0:T(8,128)S(1)}, u32[]{:S(2)}, u32[]{:S(2)}) collective-permute-start(f32[272,128]{1,0:T(8,128)S(1)} %get-tuple-element.184), channel_id=1, source_target_pairs={{0,2},{1,3},{2,0},{3,1},{4,6},{5,7},{6,4},{7,5},{8,10},{9,11},{10,... | collective-permute-start | bytes 417800 | tf_op jit(solution)/shard_map/ppermute | solution.py:249
  10.6 9.3 %collective-permute-start.2 = (f32[272,128]{1,0:T(8,128)S(1)}, f32[272,128]{1,0:T(8,128)S(1)}, u32[]{:S(2)}, u32[]{:S(2)}) collective-permute-start(f32[272,128]{1,0:T(8,128)S(1)} %get-tuple-element.186), channel_id=1, source_target_pairs={{0,4},{1,5},{2,6},{3,7},{4,0},{5,1},{6,2},{7,3},{8,12},{9,13},{10,... | collective-permute-start | bytes 417800 | tf_op jit(solution)/shard_map/ppermute | solution.py:249
  12.1 7.8 %collective-permute-start.3 = (f32[272,128]{1,0:T(8,128)S(1)}, f32[272,128]{1,0:T(8,128)S(1)}, u32[]{:S(2)}, u32[]{:S(2)}) collective-permute-start(f32[272,128]{1,0:T(8,128)S(1)} %get-tuple-element.185), channel_id=1, source_target_pairs={{0,6},{1,7},{2,4},{3,5},{4,2},{5,3},{6,0},{7,1},{8,14},{9,15},{10,... | collective-permute-start | bytes 417800 | tf_op jit(solution)/shard_map/ppermute | solution.py:249
  12.2 19.5 %copy-start.3 = (bf16[256,2048]{1,0:T(8,128)(2,1)S(1)}, bf16[256,2048]{1,0:T(8,128)(2,1)}, u32[]{:S(2)}) copy-start(bf16[256,2048]{1,0:T(8,128)(2,1)} %g0_ref.3) | copy-start | bytes 3145732
  19.9 9.8 %copy-start.39 = (f32[272,128]{1,0:T(8,128)}, f32[272,128]{1,0:T(8,128)S(1)}, u32[]{:S(2)}) copy-start(f32[272,128]{1,0:T(8,128)S(1)} %collective-permute-done.3) | copy-start | bytes 417796
  20.7 21.1 %collective-permute-start.4 = (f32[272,128]{1,0:T(8,128)}, f32[272,128]{1,0:T(8,128)}, u32[]{:S(2)}, u32[]{:S(2)}) collective-permute-start(f32[272,128]{1,0:T(8,128)} %get-tuple-element.92), channel_id=1, source_target_pairs={{0,8},{1,9},{2,10},{3,11},{4,12},{5,13},{6,14},{7,15},{8,16},{9,17... | collective-permute-start | bytes 417800 | tf_op jit(solution)/shard_map/ppermute | solution.py:262
  25.3 16.5 %collective-permute-start.5 = (f32[272,128]{1,0:T(8,128)}, f32[272,128]{1,0:T(8,128)}, u32[]{:S(2)}, u32[]{:S(2)}) collective-permute-start(f32[272,128]{1,0:T(8,128)} %get-tuple-element.92), channel_id=1, source_target_pairs={{0,16},{1,17},{2,18},{3,19},{4,20},{5,21},{6,22},{7,23},{8,24},{9,... | collective-permute-start | bytes 417800 | tf_op jit(solution)/shard_map/ppermute | solution.py:262
  29.8 12.0 %collective-permute-start.6 = (f32[272,128]{1,0:T(8,128)}, f32[272,128]{1,0:T(8,128)}, u32[]{:S(2)}, u32[]{:S(2)}) collective-permute-start(f32[272,128]{1,0:T(8,128)} %get-tuple-element.92), channel_id=1, source_target_pairs={{0,24},{1,25},{2,26},{3,27},{4,28},{5,29},{6,30},{7,31}} | collective-permute-start | bytes 417800 | tf_op jit(solution)/shard_map/ppermute | solution.py:262
  31.7 3.4 %copy-start.13 = (bf16[2048,2048]{1,0:T(8,128)(2,1)S(1)}, bf16[2048,2048]{1,0:T(8,128)(2,1)}, u32[]{:S(2)}) copy-start(bf16[2048,2048]{1,0:T(8,128)(2,1)} %w_ref.1) | copy-start | bytes 25165828
  41.8 6.7 %copy-start.2 = (f32[16,128,256]{2,1,0:T(8,128)S(1)}, f32[16,128,256]{2,1,0:T(8,128)}, u32[]{:S(2)}) copy-start(f32[16,128,256]{2,1,0:T(8,128)} %copy-done.1) | copy-start | bytes 6291460
  44.2 9.1 %collective-permute-start.7 = (f32[272,128]{1,0:T(8,128)S(1)}, f32[272,128]{1,0:T(8,128)S(1)}, u32[]{:S(2)}, u32[]{:S(2)}) collective-permute-start(f32[272,128]{1,0:T(8,128)S(1)} %get-tuple-element.209), channel_id=1, source_target_pairs={{0,2},{1,3},{2,0},{3,1},{4,6},{5,7},{6,4},{7,5},{8,10},{9,11},{10,... | collective-permute-start | bytes 417800 | tf_op jit(solution)/shard_map/ppermute | solution.py:249
  45.7 7.9 %collective-permute-start.8 = (f32[272,128]{1,0:T(8,128)S(1)}, f32[272,128]{1,0:T(8,128)S(1)}, u32[]{:S(2)}, u32[]{:S(2)}) collective-permute-start(f32[272,128]{1,0:T(8,128)S(1)} %get-tuple-element.208), channel_id=1, source_target_pairs={{0,4},{1,5},{2,6},{3,7},{4,0},{5,1},{6,2},{7,3},{8,12},{9,13},{10,... | collective-permute-start | bytes 417800 | tf_op jit(solution)/shard_map/ppermute | solution.py:249
  47.3 6.3 %collective-permute-start.9 = (f32[272,128]{1,0:T(8,128)S(1)}, f32[272,128]{1,0:T(8,128)S(1)}, u32[]{:S(2)}, u32[]{:S(2)}) collective-permute-start(f32[272,128]{1,0:T(8,128)S(1)} %get-tuple-element.176), channel_id=1, source_target_pairs={{0,6},{1,7},{2,4},{3,5},{4,2},{5,3},{6,0},{7,1},{8,14},{9,15},{10,... | collective-permute-start | bytes 417800 | tf_op jit(solution)/shard_map/ppermute | solution.py:249
  47.7 15.5 %collective-permute-start.13 = (f32[256,2048]{1,0:T(8,128)}, f32[256,2048]{1,0:T(8,128)S(1)}, u32[]{:S(2)}, u32[]{:S(2)}) collective-permute-start(f32[256,2048]{1,0:T(8,128)} %copy-done.26), channel_id=1, source_target_pairs={{0,1},{1,0},{2,3},{3,2},{4,5},{5,4},{6,7},{7,6},{8,9},{9,8},{10,11... | collective-permute-start | bytes 6291464 | tf_op jit(solution)/shard_map/ppermute | solution.py:249
  48.4 5.4 %copy-start.21 = (f32[4,272,128]{2,1,0:T(8,128)S(1)}, f32[4,272,128]{2,1,0:T(8,128)}, u32[]{:S(2)}) copy-start(f32[4,272,128]{2,1,0:T(8,128)} %copy-done.20) | copy-start | bytes 1671172
  48.4 5.4 %copy-start.28 = (f32[4,272,128]{2,1,0:T(8,128)S(1)}, f32[4,272,128]{2,1,0:T(8,128)}, u32[]{:S(2)}) copy-start(f32[4,272,128]{2,1,0:T(8,128)} %copy-done.27) | copy-start | bytes 1671172
  53.6 2.0 %collective-permute-start.10 = (f32[4,272,128]{2,1,0:T(8,128)S(1)}, f32[4,272,128]{2,1,0:T(8,128)S(1)}, u32[]{:S(2)}, u32[]{:S(2)}) collective-permute-start(f32[4,272,128]{2,1,0:T(8,128)S(1)} %get-tuple-element.102), channel_id=1, source_target_pairs={{0,1},{1,0},{2,3},{3,2},{4,5},{5,4},{6,7},{7,6},{8,9},{9,8},{10,11... | collective-permute-start | bytes 1671176 | tf_op jit(solution)/shard_map/ppermute | solution.py:249
  54.0 2.4 %collective-permute-start.11 = (f32[4,272,128]{2,1,0:T(8,128)S(1)}, f32[4,272,128]{2,1,0:T(8,128)S(1)}, u32[]{:S(2)}, u32[]{:S(2)}) collective-permute-start(f32[4,272,128]{2,1,0:T(8,128)S(1)} %pad_maximum_fusion.1), channel_id=1, source_target_pairs={{0,1},{1,0},{2,3},{3,2},{4,5},{5,4},{6,7},{7,6},{8,9},{9,8},{10,11... | collective-permute-start | bytes 1671176 | tf_op jit(solution)/shard_map/ppermute | solution.py:249
  56.6 6.6 %copy-start.4 = (bf16[256,2048]{1,0:T(8,128)(2,1)S(1)}, bf16[256,2048]{1,0:T(8,128)(2,1)}, u32[]{:S(2)}) copy-start(bf16[256,2048]{1,0:T(8,128)(2,1)} %g0_ref.3) | copy-start | bytes 3145732
  59.3 6.9 %copy-start.16 = (f32[16,64,256]{2,1,0:T(8,128)}, f32[16,64,256]{2,1,0:T(8,128)S(1)}, u32[]{:S(2)}) copy-start(f32[16,64,256]{2,1,0:T(8,128)S(1)} %get-tuple-element.109.a0_ref) | copy-start | bytes 3145732
  59.3 3.8 %collective-permute-start.12 = (f32[16,64,256]{2,1,0:T(8,128)S(1)}, f32[16,64,256]{2,1,0:T(8,128)S(1)}, u32[]{:S(2)}, u32[]{:S(2)}) collective-permute-start(f32[16,64,256]{2,1,0:T(8,128)S(1)} %get-tuple-element.110), channel_id=1, source_target_pairs={{0,1},{1,0},{2,3},{3,2},{4,5},{5,4},{6,7},{7,6},{8,9},{9,8},{10,11... | collective-permute-start | bytes 3145736 | tf_op jit(solution)/shard_map/ppermute | solution.py:249
  59.7 6.5 %collective-permute-start.14 = (f32[272,128]{1,0:T(8,128)S(1)}, f32[272,128]{1,0:T(8,128)S(1)}, u32[]{:S(2)}, u32[]{:S(2)}) collective-permute-start(f32[272,128]{1,0:T(8,128)S(1)} %get-tuple-element.182), channel_id=1, source_target_pairs={{0,2},{1,3},{2,0},{3,1},{4,6},{5,7},{6,4},{7,5},{8,10},{9,11},{10,... | collective-permute-start | bytes 417800 | tf_op jit(solution)/shard_map/ppermute | solution.py:249
  61.2 8.4 %collective-permute-start.15 = (f32[272,128]{1,0:T(8,128)S(1)}, f32[272,128]{1,0:T(8,128)S(1)}, u32[]{:S(2)}, u32[]{:S(2)}) collective-permute-start(f32[272,128]{1,0:T(8,128)S(1)} %get-tuple-element.181), channel_id=1, source_target_pairs={{0,4},{1,5},{2,6},{3,7},{4,0},{5,1},{6,2},{7,3},{8,12},{9,13},{10,... | collective-permute-start | bytes 417800 | tf_op jit(solution)/shard_map/ppermute | solution.py:249
  62.7 6.9 %collective-permute-start.16 = (f32[272,128]{1,0:T(8,128)S(1)}, f32[272,128]{1,0:T(8,128)S(1)}, u32[]{:S(2)}, u32[]{:S(2)}) collective-permute-start(f32[272,128]{1,0:T(8,128)S(1)} %get-tuple-element.180), channel_id=1, source_target_pairs={{0,6},{1,7},{2,4},{3,5},{4,2},{5,3},{6,0},{7,1},{8,14},{9,15},{10,... | collective-permute-start | bytes 417800 | tf_op jit(solution)/shard_map/ppermute | solution.py:249
  63.2 3.0 %copy-start.18 = (f32[16,64,256]{2,1,0:T(8,128)}, f32[16,64,256]{2,1,0:T(8,128)S(1)}, u32[]{:S(2)}) copy-start(f32[16,64,256]{2,1,0:T(8,128)S(1)} %collective-permute-done.12.a1_ref) | copy-start | bytes 3145732
  63.2 3.0 %copy-start.14 = (f32[256,2048]{1,0:T(8,128)}, f32[256,2048]{1,0:T(8,128)S(1)}, u32[]{:S(2)}) copy-start(f32[256,2048]{1,0:T(8,128)S(1)} %collective-permute-done.13.g1_ref) | copy-start | bytes 6291460
  66.2 11.2 %copy-start.35 = (f32[272,128]{1,0:T(8,128)}, f32[272,128]{1,0:T(8,128)S(1)}, u32[]{:S(2)}) copy-start(f32[272,128]{1,0:T(8,128)S(1)} %collective-permute-done.14) | copy-start | bytes 417796
  69.6 7.8 %copy-start.31 = (f32[272,128]{1,0:T(8,128)}, f32[272,128]{1,0:T(8,128)S(1)}, u32[]{:S(2)}) copy-start(f32[272,128]{1,0:T(8,128)S(1)} %collective-permute-done.15) | copy-start | bytes 417796
  69.6 7.8 %copy-start.33 = (f32[272,128]{1,0:T(8,128)}, f32[272,128]{1,0:T(8,128)S(1)}, u32[]{:S(2)}) copy-start(f32[272,128]{1,0:T(8,128)S(1)} %collective-permute-done.16) | copy-start | bytes 417796
  69.6 36.7 %collective-permute-start.17 = (f32[8,64,768]{2,1,0:T(8,128)}, f32[8,64,768]{2,1,0:T(8,128)}, u32[]{:S(2)}, u32[]{:S(2)}) collective-permute-start(f32[8,64,768]{2,1,0:T(8,128)} %get-tuple-element.119), channel_id=1, source_target_pairs={{0,2},{1,3},{2,0},{3,1},{4,6},{5,7},{6,4},{7,5},{8,10},{9,11},{10,... | collective-permute-start | bytes 4718600 | tf_op jit(solution)/shard_map/ppermute | solution.py:249
  70.8 35.6 %collective-permute-start.18 = (f32[8,64,768]{2,1,0:T(8,128)}, f32[8,64,768]{2,1,0:T(8,128)}, u32[]{:S(2)}, u32[]{:S(2)}) collective-permute-start(f32[8,64,768]{2,1,0:T(8,128)} %get-tuple-element.120), channel_id=1, source_target_pairs={{0,4},{1,5},{2,6},{3,7},{4,0},{5,1},{6,2},{7,3},{8,12},{9,13},{10,... | collective-permute-start | bytes 4718600 | tf_op jit(solution)/shard_map/ppermute | solution.py:249
  71.7 34.5 %collective-permute-start.19 = (f32[8,64,512]{2,1,0:T(8,128)}, f32[8,64,512]{2,1,0:T(8,128)}, u32[]{:S(2)}, u32[]{:S(2)}) collective-permute-start(f32[8,64,512]{2,1,0:T(8,128)} %get-tuple-element.121), channel_id=1, source_target_pairs={{0,8},{1,9},{2,10},{3,11},{4,12},{5,13},{6,14},{7,15},{8,0},{9,1},... | collective-permute-start | bytes 3145736 | tf_op jit(solution)/shard_map/ppermute | solution.py:249
  71.7 7.9 %copy-start.8 = (bf16[256,2048]{1,0:T(8,128)(2,1)S(1)}, bf16[256,2048]{1,0:T(8,128)(2,1)}, u32[]{:S(2)}) copy-start(bf16[256,2048]{1,0:T(8,128)(2,1)} %k_ref.7) | copy-start | bytes 3145732
  71.7 7.9 %copy-start.11 = (bf16[256,2048]{1,0:T(8,128)(2,1)S(1)}, bf16[256,2048]{1,0:T(8,128)(2,1)}, u32[]{:S(2)}) copy-start(bf16[256,2048]{1,0:T(8,128)(2,1)} %v_ref.7) | copy-start | bytes 3145732
  77.5 20.9 %collective-permute-start.20 = (f32[272,128]{1,0:T(8,128)S(1)}, f32[272,128]{1,0:T(8,128)S(1)}, u32[]{:S(2)}, u32[]{:S(2)}) collective-permute-start(f32[272,128]{1,0:T(8,128)S(1)} %pad_maximum_fusion.9), channel_id=1, source_target_pairs={{0,8},{1,9},{2,10},{3,11},{4,12},{5,13},{6,14},{7,15},{8,0},{9,1},... | collective-permute-start | bytes 417800 | tf_op jit(solution)/shard_map/ppermute | solution.py:249
  79.6 19.5 %copy-start.5 = (bf16[256,2048]{1,0:T(8,128)(2,1)S(1)}, bf16[256,2048]{1,0:T(8,128)(2,1)}, u32[]{:S(2)}) copy-start(bf16[256,2048]{1,0:T(8,128)(2,1)} %g0_ref.3) | copy-start | bytes 3145732
  79.6 19.5 %copy-start.17 = (f32[16,64,256]{2,1,0:T(8,128)S(1)}, f32[16,64,256]{2,1,0:T(8,128)}, u32[]{:S(2)}) copy-start(f32[16,64,256]{2,1,0:T(8,128)} %copy-done.16) | copy-start | bytes 3145732
  99.0 7.2 %collective-permute-start.21 = (f32[272,128]{1,0:T(8,128)S(1)}, f32[272,128]{1,0:T(8,128)S(1)}, u32[]{:S(2)}, u32[]{:S(2)}) collective-permute-start(f32[272,128]{1,0:T(8,128)S(1)} %fusion.49), channel_id=1, source_target_pairs={{0,16},{1,17},{2,18},{3,19},{4,20},{5,21},{6,22},{7,23},{8,24},{9,... | collective-permute-start | bytes 417800 | tf_op jit(solution)/shard_map/ppermute | solution.py:249
  101.9 4.3 %copy-start.38 = (f32[272,128]{1,0:T(8,128)S(1)}, f32[272,128]{1,0:T(8,128)}, u32[]{:S(2)}) copy-start(f32[272,128]{1,0:T(8,128)} %copy-done.37) | copy-start | bytes 417796
  107.6 18.0 %collective-permute-start.24 = (f32[2,2,64,512]{3,2,0,1:T(8,128)S(1)}, f32[2,2,64,512]{3,2,0,1:T(8,128)S(1)}, u32[]{:S(2)}, u32[]{:S(2)}) collective-permute-start(f32[2,2,64,512]{3,2,0,1:T(8,128)S(1)} %fusion.5), channel_id=1, source_target_pairs={{0,2},{1,3},{2,0},{3,1},{4,6},{5,7},{6,4},{7,5},{8,10},{9,11},{10,... | collective-permute-start | bytes 1572872 | tf_op jit(solution)/shard_map/ppermute | solution.py:249
  109.4 2.8 %copy-start.32 = (f32[272,128]{1,0:T(8,128)S(1)}, f32[272,128]{1,0:T(8,128)}, u32[]{:S(2)}) copy-start(f32[272,128]{1,0:T(8,128)} %copy-done.31) | copy-start | bytes 417796
  109.4 17.4 %collective-permute-start.23 = (f32[2,2,64,768]{3,2,1,0:T(8,128)S(1)}, f32[2,2,64,768]{3,2,1,0:T(8,128)S(1)}, u32[]{:S(2)}, u32[]{:S(2)}) collective-permute-start(f32[2,2,64,768]{3,2,1,0:T(8,128)S(1)} %fusion.1), channel_id=1, source_target_pairs={{0,8},{1,9},{2,10},{3,11},{4,12},{5,13},{6,14},{7,15},{8,0},{9,1},... | collective-permute-start | bytes 2359304 | tf_op jit(solution)/shard_map/ppermute | solution.py:249
  110.8 17.5 %collective-permute-start.22 = (f32[2,2,64,768]{3,2,0,1:T(8,128)S(1)}, f32[2,2,64,768]{3,2,0,1:T(8,128)S(1)}, u32[]{:S(2)}, u32[]{:S(2)}) collective-permute-start(f32[2,2,64,768]{3,2,0,1:T(8,128)S(1)} %fusion.3), channel_id=1, source_target_pairs={{0,4},{1,5},{2,6},{3,7},{4,0},{5,1},{6,2},{7,3},{8,12},{9,13},{10,... | collective-permute-start | bytes 2359304 | tf_op jit(solution)/shard_map/ppermute | solution.py:249
  112.3 13.2 %collective-permute-start.25 = (f32[2,272,128]{2,1,0:T(8,128)S(1)}, f32[2,272,128]{2,1,0:T(8,128)S(1)}, u32[]{:S(2)}, u32[]{:S(2)}) collective-permute-start(f32[2,272,128]{2,1,0:T(8,128)S(1)} %pad_maximum_fusion.10), channel_id=1, source_target_pairs={{0,2},{1,3},{2,0},{3,1},{4,6},{5,7},{6,4},{7,5},{8,10},{9,11},{10,... | collective-permute-start | bytes 835592 | tf_op jit(solution)/shard_map/ppermute | solution.py:249
  128.4 4.1 %copy-start.41 = (f32[1,272,128]{2,1,0:T(8,128)S(1)}, f32[1,272,128]{2,1,0:T(8,128)}, u32[]{:S(2)}) copy-start(f32[1,272,128]{2,1,0:T(8,128)} %get-tuple-element.190) | copy-start | bytes 417796
  128.4 12.4 %collective-permute-start.29 = (f32[2,64,512]{2,1,0:T(8,128)S(1)}, f32[2,64,512]{2,1,0:T(8,128)S(1)}, u32[]{:S(2)}, u32[]{:S(2)}) collective-permute-start(f32[2,64,512]{2,1,0:T(8,128)S(1)} %fusion.9), channel_id=1, source_target_pairs={{0,4},{1,5},{2,6},{3,7},{4,0},{5,1},{6,2},{7,3},{8,12},{9,13},{10,... | collective-permute-start | bytes 786440 | tf_op jit(solution)/shard_map/ppermute | solution.py:249
  130.2 17.6 %collective-permute-start.28 = (f32[2,64,768]{2,1,0:T(8,128)S(1)}, f32[2,64,768]{2,1,0:T(8,128)S(1)}, u32[]{:S(2)}, u32[]{:S(2)}) collective-permute-start(f32[2,64,768]{2,1,0:T(8,128)S(1)} %fusion.7), channel_id=1, source_target_pairs={{0,16},{1,17},{2,18},{3,19},{4,20},{5,21},{6,22},{7,23},{8,24},{9,... | collective-permute-start | bytes 1179656 | tf_op jit(solution)/shard_map/ppermute | solution.py:249
  130.6 17.2 %collective-permute-start.27 = (f32[2,64,768]{2,1,0:T(8,128)S(1)}, f32[2,64,768]{2,1,0:T(8,128)S(1)}, u32[]{:S(2)}, u32[]{:S(2)}) collective-permute-start(f32[2,64,768]{2,1,0:T(8,128)S(1)} %fusion.8), channel_id=1, source_target_pairs={{0,8},{1,9},{2,10},{3,11},{4,12},{5,13},{6,14},{7,15},{8,0},{9,1},... | collective-permute-start | bytes 1179656 | tf_op jit(solution)/shard_map/ppermute | solution.py:249
  132.1 8.1 %collective-permute-start.26 = (f32[2,272,128]{2,1,0:T(8,128)S(1)}, f32[2,272,128]{2,1,0:T(8,128)S(1)}, u32[]{:S(2)}, u32[]{:S(2)}) collective-permute-start(f32[2,272,128]{2,1,0:T(8,128)S(1)} %pad_maximum_fusion.11), channel_id=1, source_target_pairs={{0,4},{1,5},{2,6},{3,7},{4,0},{5,1},{6,2},{7,3},{8,12},{9,13},{10,... | collective-permute-start | bytes 835592 | tf_op jit(solution)/shard_map/ppermute | solution.py:249
  132.5 7.8 %copy-start.42 = (f32[1,272,128]{2,1,0:T(8,128)S(1)}, f32[1,272,128]{2,1,0:T(8,128)}, u32[]{:S(2)}) copy-start(f32[1,272,128]{2,1,0:T(8,128)} %get-tuple-element.191) | copy-start | bytes 417796
  132.5 7.8 %copy-start.43 = (f32[1,272,128]{2,1,0:T(8,128)S(1)}, f32[1,272,128]{2,1,0:T(8,128)}, u32[]{:S(2)}) copy-start(f32[1,272,128]{2,1,0:T(8,128)} %get-tuple-element.192) | copy-start | bytes 417796
  140.4 12.4 %copy-start.25 = (f32[256,2048]{1,0:T(8,128)S(1)}, f32[256,2048]{1,0:T(8,128)}, u32[]{:S(2)}) copy-start(f32[256,2048]{1,0:T(8,128)} %copy-done.24) | copy-start | bytes 6291460
  140.5 7.4 %collective-permute-start.30 = (f32[4,272,128]{2,1,0:T(8,128)S(1)}, f32[4,272,128]{2,1,0:T(8,128)S(1)}, u32[]{:S(2)}, u32[]{:S(2)}) collective-permute-start(f32[4,272,128]{2,1,0:T(8,128)S(1)} %pad_maximum_fusion.3), channel_id=1, source_target_pairs={{0,1},{1,0},{2,3},{3,2},{4,5},{5,4},{6,7},{7,6},{8,9},{9,8},{10,11... | collective-permute-start | bytes 1671176 | tf_op jit(solution)/shard_map/ppermute | solution.py:249
  140.6 12.2 %copy-start.23 = (f32[256,2048]{1,0:T(8,128)S(1)}, f32[256,2048]{1,0:T(8,128)}, u32[]{:S(2)}) copy-start(f32[256,2048]{1,0:T(8,128)} %copy-done.22) | copy-start | bytes 6291460
  140.6 12.2 %copy-start.9 = (bf16[256,2048]{1,0:T(8,128)(2,1)S(1)}, bf16[256,2048]{1,0:T(8,128)(2,1)}, u32[]{:S(2)}) copy-start(bf16[256,2048]{1,0:T(8,128)(2,1)} %k_ref.7) | copy-start | bytes 3145732
  140.6 12.2 %copy-start.12 = (bf16[256,2048]{1,0:T(8,128)(2,1)S(1)}, bf16[256,2048]{1,0:T(8,128)(2,1)}, u32[]{:S(2)}) copy-start(bf16[256,2048]{1,0:T(8,128)(2,1)} %v_ref.7) | copy-start | bytes 3145732
  147.9 12.6 %collective-permute-start.33 = (f32[64,512]{1,0:T(8,128)S(1)}, f32[64,512]{1,0:T(8,128)S(1)}, u32[]{:S(2)}, u32[]{:S(2)}) collective-permute-start(f32[64,512]{1,0:T(8,128)S(1)} %fusion.39), channel_id=1, source_target_pairs={{0,16},{1,17},{2,18},{3,19},{4,20},{5,21},{6,22},{7,23},{8,24},{9,... | collective-permute-start | bytes 393224 | tf_op jit(solution)/shard_map/ppermute | solution.py:249
  149.4 11.1 %collective-permute-start.32 = (f32[64,768]{1,0:T(8,128)S(1)}, f32[64,768]{1,0:T(8,128)S(1)}, u32[]{:S(2)}, u32[]{:S(2)}) collective-permute-start(f32[64,768]{1,0:T(8,128)S(1)} %fusion.11), channel_id=1, source_target_pairs={{0,2},{1,3},{2,0},{3,1},{4,6},{5,7},{6,4},{7,5},{8,10},{9,11},{10,... | collective-permute-start | bytes 589832 | tf_op jit(solution)/shard_map/ppermute | solution.py:249
  151.2 12.7 %collective-permute-start.31 = (f32[64,768]{1,0:T(8,128)S(1)}, f32[64,768]{1,0:T(8,128)S(1)}, u32[]{:S(2)}, u32[]{:S(2)}) collective-permute-start(f32[64,768]{1,0:T(8,128)S(1)} %fusion.13), channel_id=1, source_target_pairs={{0,16},{1,17},{2,18},{3,19},{4,20},{5,21},{6,22},{7,23},{8,24},{9,... | collective-permute-start | bytes 589832 | tf_op jit(solution)/shard_map/ppermute | solution.py:249
  (14 other events, 21.5 us)

commit v4 on v3

--- a/solution.py
+++ b/solution.py
@@ -17,7 +17,7 @@
 NN = (((1,), (0,)), ((), ()))
 NT = (((1,), (1,)), ((), ()))
 TN = (((0,), (0,)), ((), ()))
-PARTS = ((0, 768, (0, 1, 2, 3)), (768, 768, (1, 2, 3, 0)), (1536, 512, (2, 0, 1, 3)))
+PARTS = ((0, 768, (1, 2, 3, 0)), (768, 768, (0, 1, 2, 3)), (1536, 512, (2, 0, 1, 3)))
 PAIRS = HEADS // 2
 PLACES = PAIRS // 2
 VMEM_LIMIT = 12 * 1024 * 1024
@@ -107,34 +107,53 @@
     each_head(at_ref, one)
 
 
-def grad_kernel(g_ref, w_ref, some_ref, gt_ref, wide_ref):
+def grad_kernel(g_ref, w_ref, own_ref, mate_ref, gt_ref, both_ref):
     got = lax.dot_general(w_ref[...], g_ref[...], NT, preferred_element_type=F32)
     gt_ref[...] = got.reshape(gt_ref.shape)
-    wide_ref[...] = some_ref[...].astype(F32)
-
-
-def attended_grad(out_grad, out_weight):
+    t = g_ref.shape[0]
+    both_ref[:t, :] = own_ref[...]
+    both_ref[t:, :] = mate_ref[...].astype(BF16)
+
+
+def attended_grad(out_grad, out_weight, grad_mate):
     t, model = out_grad.shape
-    step = model // PAIRS
+    some = 4
+    steps = HEADS // some
+    columns = lambda rows: pl.BlockSpec((rows, model // steps), lambda i: (0, i))
     return pl.pallas_call(
         grad_kernel,
-        grid=(PAIRS,),
+        grid=(steps,),
         out_shape=(
             jax.ShapeDtypeStruct((HEADS, HEAD, t), F32),
-            jax.ShapeDtypeStruct((t, model), F32),
+            jax.ShapeDtypeStruct((2 * t, model), BF16),
         ),
         in_specs=[
             pl.BlockSpec((t, model), lambda i: (0, 0)),
-            pl.BlockSpec((2 * HEAD, model), lambda i: (i, 0)),
-            pl.BlockSpec((t, step), lambda i: (0, i)),
+            pl.BlockSpec((some * HEAD, model), lambda i: (i, 0)),
+            columns(t),
+            columns(t),
         ],
-        out_specs=(
-            pl.BlockSpec((2, HEAD, t), lambda i: (i, 0, 0)),
-            pl.BlockSpec((t, step), lambda i: (0, i)),
-        ),
+        out_specs=(pl.BlockSpec((some, HEAD, t), lambda i: (i, 0, 0)), columns(2 * t)),
         compiler_params=pltpu.CompilerParams(vmem_limit_bytes=VMEM_LIMIT),
         cost_estimate=pl.CostEstimate(flops=1000, bytes_accessed=1000, transcendentals=0),
-    )(out_grad, out_weight, out_grad)
+    )(out_grad, out_weight, out_grad, grad_mate)
+
+
+def back_kernel(at_ref, mate_ref, *refs):
+    me = at_ref[0]
+    core, plane = me % 2, (me // 2) % 4
+    got, outer, outs = refs[:PLACES], refs[PLACES : -PLACES - 1], refs[-PLACES - 1 :]
+    total = outer[0][...]
+    for ref in outer[1:]:
+        total = total + ref[...]
+    for j in range(PLACES):
+        x = total
+        for i in range(PLACES):
+            if i != j:
+                x = x + jnp.where((plane ^ i) < (plane ^ j), got[i][...], 0.0)
+        outs[j][...] = x
+        if j == 0:
+            outs[-1][...] = x[2 * HEAD :] + jnp.where(core == 1, mate_ref[0, 2 * HEAD :, :], 0.0)
 
 
 def early_kernel(at_ref, q_ref, nd_ref, gt_ref, z_ref, keep_ref, send_ref, inv_ref):
@@ -216,13 +235,11 @@
     each_head(at_ref, one)
 
 
-def weight_kernel(bit_set, a0_ref, a1_ref, g0_ref, g1_ref, *refs):
-    outs, (a_ref, g_ref) = refs[:-2], refs[-2:]
-    t = g0_ref.shape[0]
+def weight_kernel(bit_set, a0_ref, a1_ref, g_ref, *refs):
+    outs, a_ref = refs[:-1], refs[-1]
+    t = a0_ref.shape[2]
     a_ref[:, :, :t] = a0_ref[...].astype(BF16)
     a_ref[:, :, t:] = a1_ref[...].astype(BF16)
-    g_ref[:t, :] = g0_ref[...]
-    g_ref[t:, :] = g1_ref[...].astype(BF16)
     for out_ref, (start, width, order) in zip(outs, PARTS, strict=True):
         rels = [rel for rel in range(HEADS) if (rel >> order[0]) & 1 == bit_set]
         lhs = jnp.concatenate([a_ref[rel] for rel in rels], axis=0)
@@ -284,6 +301,20 @@
 
 def half(a, left, bit, which):
     return lax.index_in_dim(a.reshape((2,) * len(left) + a.shape[-2:]), which, left.index(bit), keepdims=False)
+
+
+def one_turn(keep, got, left, bit):
+    send = half(keep, left, bit, 1) + half(got, left, bit, 1)
+    keep, got = after(send, keep, got)
+    return half(keep, left, bit, 0) + half(got, left, bit, 0), swap(send, 2 << bit)
+
+
+def sums_of(order, keep, got):
+    left = sorted(order[1:], reverse=True)
+    for bit in order[1:]:
+        keep, got = one_turn(keep, got, left, bit)
+        left = [b for b in left if b != bit]
+        got = after((yield keep, got), got)
 
 
 def body(queries, keys, values, out_weight, out_grad):
@@ -303,20 +334,20 @@
 
     keep, send = call(summary_kernel, packs, at, keys, values, scratch=(pltpu.VMEM((HEADS, HEAD), F32),))
     mate = swap(send, 1)
-    gt, grad_wide = attended_grad(out_grad, out_weight)
-    (inner,) = call(inner_kernel, [shape((HEADS, ROWS, t), F32)], at, queries, keys, values)
+    grad_mate = swap(out_grad.astype(F32), 1)
+    (inner,) = call(
+        inner_kernel, [shape((HEADS, ROWS, t), F32)], at, queries, keys, values
+    )
     total = [keep[j] + mate[j] for j in places]
     got = [total[0]] + [swap(total[j], 2 * j) for j in places[1:]]
-    layer, inner = lax.optimization_barrier((got[0] + got[1] + got[2] + got[3], inner))
+    layer, inner, grad_mate = lax.optimization_barrier((got[0] + got[1] + got[2] + got[3], inner, grad_mate))
     outer = along(layer, False)
-    outer, gt, grad_wide = lax.optimization_barrier((outer, gt, grad_wide))
-    outer = sum(outer[1:], outer[0])
-    back = [outer + before(got, j, plane, False) for j in places]
-    z_in = own_sums(back[0]) + jnp.where(core == 1, own_sums(mate[0]), 0.0)
-
-    z_in = after(back, z_in)
+    gt, grads = attended_grad(out_grad, out_weight, grad_mate)
+    outer, gt, grads = lax.optimization_barrier((outer, gt, grads))
+    pack = shape((PACK, HEAD), F32)
+    *back, z_in = call(back_kernel, [pack] * PLACES + [sums], at, mate, *got, *outer)
+
     back = [swap(x, 2 * j) if j else x for j, x in enumerate(back)]
-    grad_mate = swap(grad_wide, 1)
     dkeep, dsend, inv = call(early_kernel, packs + [row], at, queries, inner, gt, z_in)
     back, dsend = lax.optimization_barrier((back, dsend))
     dmate = swap(dsend, 1)
@@ -336,9 +367,8 @@
         [shape((HEADS // 2, HALF, width), F32) for _, width, _ in PARTS],
         a_keep,
         a_mate,
-        out_grad,
-        grad_mate,
-        scratch=(pltpu.VMEM((HEADS, HALF, 2 * t), BF16), pltpu.VMEM((2 * t, model), BF16)),
+        grads,
+        scratch=(pltpu.VMEM((HEADS, HALF, 2 * t), BF16),),
     )
     sends, dgot = lax.optimization_barrier((list(weight(1)), dgot))
     a_mate = after(sends, a_mate)
@@ -354,13 +384,16 @@
         backward_kernel, [narrow, wide, wide], at, queries, keys, values, gt, inv, dd, z_in, s0, s1
     )
     douter = along_in_turn(dlayer, dfirst, me, True, dk)
+    free = sums_of(PARTS[-1][2], keeps[-1], after(dk, gots[-1]))
+    next(free)
+    keeps, gots = keeps[:-1], gots[:-1]
     gots, douter = lax.optimization_barrier((gots, douter))
     dback = [douter + before(dgot, j, plane, True) for j in places]
 
     behind = own_sums(douter)
-    lefts = [sorted(order[1:], reverse=True) for _, _, order in PARTS]
-    for turn in range(1, 4):
-        bits = [order[turn] for _, _, order in PARTS]
+    lefts = [sorted(order[1:], reverse=True) for _, _, order in PARTS[:-1]]
+    for turn in (1, 2):
+        bits = [order[turn] for _, _, order in PARTS[:-1]]
         lists = list(zip(keeps, gots, lefts, bits, strict=True))
         sends = [half(k, left, bit, 1) + half(g, left, bit, 1) for k, g, left, bit in lists]
         keeps, gots = after(sends, keeps, gots)
@@ -369,6 +402,7 @@
         lefts = [[b for b in left if b != bit] for left, bit in zip(lefts, bits, strict=True)]
         gots = [swap(send, 2 << bit) for send, bit in zip(sends, bits, strict=True)]
         if turn == 2:
+            free.send(sends)
             behind, dz_beside = behind + own_sums(across[0]), own_sums(across[1])
             up = jnp.stack([with_sums(dback[2], behind), with_sums(across[1], dz + dz_beside)])
             up = swap(after(sends, up), 4)
@@ -377,18 +411,20 @@
             dback = [dback[0], across[0], up[0], up[1]]
             other = [x + jnp.where(core == 1, dkeep[j], 0.0) for j, x in enumerate(dback)]
             other = [with_sums(x, dz_part if j == 0 else dz) for j, x in enumerate(other)]
-            l1 = swap(jnp.stack(other), 1)
+            other = jnp.stack(other)
+            l1 = swap(other, 1)
             l0 = jnp.stack([x + jnp.where(core == 0, dmate[j], 0.0) for j, x in enumerate(dback)])
-            gots, l0, l1 = lax.optimization_barrier((gots, l0, l1))
+            result = free.send(other)
+            ends = [one_turn(keeps[1], after(other, gots[1]), lefts[1], PARTS[1][2][3])]
         elif turn == 1:
             across = jnp.stack([with_sums(dback[1], behind), with_sums(dback[3], dz)])
             across = swap(after(sends, across), 2)
             gots, across = lax.optimization_barrier((gots, across))
-    l0 = after(sends, l0)
     dz_in = dz_part + own_sums(l1[0]) + jnp.where(core == 0, own_sums(l1[1]), 0.0)
     key_grad, value_grad = call(finish_kernel, [narrow, narrow], at, keys, values, dk, dv, dz_in, l0, l1)
-    key_grad, gots = lax.optimization_barrier((key_grad, gots))
-    parts = [keep_part + got for keep_part, got in zip(keeps, gots, strict=True)]
+    ends.insert(0, one_turn(keeps[0], after(key_grad, gots[0]), lefts[0], PARTS[0][2][3]))
+    key_grad, ends = lax.optimization_barrier((key_grad, [*ends, result]))
+    parts = [keep_part + got for keep_part, got in ends]
     weight_grad = jnp.concatenate(parts, axis=1)
     return (query_grad, key_grad, value_grad, weight_grad)
 

time: 165 us -> 162 us (0.982)
  waiting for transfers between devices: 43.6 us -> 36.7 us
  starting transfers between devices: 40.8 us -> 43.4 us
    ppermute x31, waiting for transfers between devices: 43.6 us -> 36.7 us  [swap(): return lax.ppermute(x, 'seq', [(i, i ^ mask) for i in range(n)])]
    ppermute x31, starting transfers between devices: 29.8 us -> 33.7 us  [swap(): return lax.ppermute(x, 'seq', [(i, i ^ mask) for i in range(n)])]
    convert_element_type x0 -> x1, other arithmetic: none -> 2.93 us  [body(): grad_mate = swap(out_grad.astype(F32), 1)]
    unnamed x88 -> x94, local copies, waits for them, and re-layouts: 14.8 us -> 13.5 us
    add x6 -> x4, other arithmetic: 3.81 us -> 2.55 us  [body(): half(k, left, bit, 0) + half(g, left, bit, 0)]
    add x9 -> x4, other arithmetic: 3.88 us -> 2.69 us  [body(): half(k, left, bit, 1) + half(g, left, bit, 1)]
    pallas_call x9 -> x10, Pallas kernels: 46.1 us -> 46.7 us  [call(): pl.pallas_call(kernel, out_shape=tuple(outs), in_specs=specs, out_specs=t...]
  transfers between devices with their start and end apart: 34 -> 34, of which waited for: 14 -> 12; matrix products, arithmetic and copies ran while one was open for 5% -> 7% of each run, Pallas kernels for 29% -> 30%
where the time goes in v4:
time: 162 us; the launch traced here: 161 us
  Pallas kernels  51.4 us (32%)
  starting transfers between devices  43.4 us (27%)
  waiting for transfers between devices  36.7 us (23%)
  other arithmetic  14.4 us (9%)
  local copies, waits for them, and re-layouts  13.9 us (9%)
    pallas_call x10, Pallas kernels, call(): pl.pallas_call(kernel, out_shape=tuple(outs), in_specs=specs, out_specs=t...  46.7 us
    ppermute x31, waiting for transfers between devices, swap(): return lax.ppermute(x, 'seq', [(i, i ^ mask) for i in range(n)])  36.7 us
    ppermute x31, starting transfers between devices, swap(): return lax.ppermute(x, 'seq', [(i, i ^ mask) for i in range(n)])  33.7 us
    unnamed x94, local copies, waits for them, and re-layouts  13.5 us
    ppermute x3, starting transfers between devices, along(): lax.ppermute(layer, 'seq', [(b, a) for a, b in pairs] if later else pairs)  9.68 us
    pallas_call x1, Pallas kernels, attended_grad(): pl.pallas_call(grad_kernel, grid=(steps,), out_shape=(jax.ShapeDtypeStruc...  4.63 us
  transfers between devices with their start and end apart: 34, of which 12 were waited for; matrix products, arithmetic and copies ran while one was open for 7% of the time, Pallas kernels for 30%

profile of v4, /device:TPU:0, one launch (start us, length us, event | category | flops | bytes accessed | tf_op | source)
XLA Modules:
  0.0 161.2 jit_solution(18422363890848864354)
XLA Ops:
  0.7 2.9 %convert_element_type.3 = f32[256,2048]{1,0:T(8,128)} convert(bf16[256,2048]{1,0:T(8,128)(2,1)} %own_ref.1) | non-fusion elementwise | flops 524288 | bytes 3145728 | tf_op jit(solution)/shard_map/convert_element_type | solution.py:337
  4.1 2.4 %shard_map.84 = (f32[4,272,128]{2,1,0:T(8,128)S(1)}, f32[4,272,128]{2,1,0:T(8,128)S(1)}) custom-call(s32[1]{0:T(128)} %bitcast.at_ref, bf16[256,2048]{1,0:T(8,128)(2,1)S(1)} %copy-done.4, bf16[256,2048]{1,0:T(8,128)(2,1)S(1)} %copy-done.8), custom_call_target="tpu_custom_call" | custom-call | flops 1000 | bytes 1000 | tf_op jit(solution)/shard_map/pallas_call | solution.py:253
  6.6 2.0 %collective-permute-done.mate_ref = f32[4,272,128]{2,1,0:T(8,128)S(1)} collective-permute-done((f32[4,272,128]{2,1,0:T(8,128)S(1)}, f32[4,272,128]{2,1,0:T(8,128)S(1)}, u32[]{:S(2)}, u32[]{:S(2)}) %collective-permute-start) | collective-permute-done | bytes 557088 | tf_op jit(solution)/shard_map/ppermute | solution.py:266
  8.7 3.9 %collective-permute-start.3 = (f32[272,128]{1,0:T(8,128)S(1)}, f32[272,128]{1,0:T(8,128)S(1)}, u32[]{:S(2)}, u32[]{:S(2)}) collective-permute-start(f32[272,128]{1,0:T(8,128)S(1)} %get-tuple-element.193), channel_id=1, source_target_pairs={{0,6},{1,7},{2,4},{3,5},{4,2},{5,3},{6,0},{7,1},{8,14},{9,15},{10,... | collective-permute-start | bytes 417800 | tf_op jit(solution)/shard_map/ppermute | solution.py:266
  12.6 0.5 collective-permute-start.2
  13.2 7.7 %shard_map.85.nd_ref = f32[16,136,256]{2,1,0:T(8,128)S(1)} custom-call(s32[1]{0:T(128)} %bitcast.at_ref, bf16[256,2048]{1,0:T(8,128)(2,1)S(1)} %copy-done, bf16[256,2048]{1,0:T(8,128)(2,1)S(1)} %copy-done.5, bf16[256,2048]{1,0:T(8,128)(2,1)S(1)} %copy-done.9), custom_call_target="tpu_custom_call" | custom-call | flops 1000 | bytes 1000 | tf_op jit(solution)/shard_map/pallas_call | solution.py:253
  21.0 3.9 %collective-permute-start.5 = (f32[272,128]{1,0:T(8,128)S(1)}, f32[272,128]{1,0:T(8,128)S(1)}, u32[]{:S(2)}, u32[]{:S(2)}) collective-permute-start(f32[272,128]{1,0:T(8,128)S(1)} %get-tuple-element.97), channel_id=1, source_target_pairs={{0,8},{1,9},{2,10},{3,11},{4,12},{5,13},{6,14},{7,15},{8,16},{9,17... | collective-permute-start | bytes 417800 | tf_op jit(solution)/shard_map/ppermute | solution.py:279
  24.9 4.5 %collective-permute-start.6 = (f32[272,128]{1,0:T(8,128)S(1)}, f32[272,128]{1,0:T(8,128)S(1)}, u32[]{:S(2)}, u32[]{:S(2)}) collective-permute-start(f32[272,128]{1,0:T(8,128)S(1)} %get-tuple-element.97), channel_id=1, source_target_pairs={{0,16},{1,17},{2,18},{3,19},{4,20},{5,21},{6,22},{7,23},{8,24},{9,... | collective-permute-start | bytes 417800 | tf_op jit(solution)/shard_map/ppermute | solution.py:279
  29.4 1.3 collective-permute-start.7
  30.8 3.4 %copy-done.13 = bf16[2048,2048]{1,0:T(8,128)(2,1)S(1)} copy-done((bf16[2048,2048]{1,0:T(8,128)(2,1)S(1)}, bf16[2048,2048]{1,0:T(8,128)(2,1)}, u32[]{:S(2)}) %copy-start.13) | copy-done | bytes 8388632
  34.1 4.6 %shard_map.86 = (f32[16,128,256]{2,1,0:T(8,128)S(1)}, bf16[512,2048]{1,0:T(8,128)(2,1)S(1)}) custom-call(bf16[256,2048]{1,0:T(8,128)(2,1)S(1)} %copy-done.12, bf16[2048,2048]{1,0:T(8,128)(2,1)S(1)} %copy-done.13, bf16[256,2048]{1,0:T(8,128)(2,1)S(1)} %copy-done.12, f32[256,2048]{1,0:T(8,128)} %collective-permute-done.4.mate_ref), custom_call_target="tpu_custom_call" | custom-call | flops 1000 | bytes 1000 | tf_op jit(solution)/shard_map/pallas_call | solution.py:123
  38.8 1.3 copy-done.1
  40.1 1.3 copy-done.14
  41.4 0.8 shard_map.87
  42.3 1.5 collective-permute-start.8
  43.8 1.5 collective-permute-start.9
  45.3 0.5 collective-permute-start.10
  45.8 1.6 copy-done.2
  47.4 4.8 %shard_map.88 = (f32[4,272,128]{2,1,0:T(8,128)S(1)}, f32[4,272,128]{2,1,0:T(8,128)S(1)}, f32[16,8,256]{2,1,0:T(8,128)S(1)}) custom-call(s32[1]{0:T(128)} %bitcast.at_ref, bf16[256,2048]{1,0:T(8,128)(2,1)S(1)} %copy-done, f32[16,136,256]{2,1,0:T(8,128)S(1)} %shard_map.85.nd_ref, f32[16,128,256]{2,1,0:T(8,128)S(1)} %copy-done.2, ...), custom_call_target="tpu_custom_call" | custom-call | flops 1000 | bytes 1000 | tf_op jit(solution)/shard_map/pallas_call | solution.py:253
  52.3 1.1 fusion.26
  53.5 0.5 collective-permute-start.12
  54.2 0.9 add_bitcast_fusion.2
  55.1 0.5 collective-permute-done.12.s1_ref
  55.6 2.8 %shard_map.89 = (f32[16,64,256]{2,1,0:T(8,128)S(1)}, f32[16,64,256]{2,1,0:T(8,128)S(1)}) custom-call(s32[1]{0:T(128)} %bitcast.at_ref, bf16[256,2048]{1,0:T(8,128)(2,1)S(1)} %copy-done, f32[16,136,256]{2,1,0:T(8,128)S(1)} %shard_map.85.nd_ref, f32[16,8,256]{2,1,0:T(8,128)S(1)} %get-tuple-element.114.inv_ref, f32[4,272,128]{2,1,0:T(8,128)S(1)} %pad_maximum_fusion.s0_ref, ...), custom_call_target="tpu_custom_call" | custom-call | flops 1000 | bytes 1000 | tf_op jit(solution)/shard_map/pallas_call | solution.py:253
  58.8 1.5 collective-permute-start.14
  60.3 1.5 collective-permute-start.15
  61.9 0.5 collective-permute-start.16
  62.4 2.8 %shard_map.90 = (f32[8,64,768]{2,1,0:T(8,128)}, f32[8,64,768]{2,1,0:T(8,128)}, f32[8,64,512]{2,1,0:T(8,128)}) custom-call(f32[16,64,256]{2,1,0:T(8,128)S(1)} %get-tuple-element.119.a0_ref, f32[16,64,256]{2,1,0:T(8,128)S(1)} %collective-permute-done.13.a1_ref, bf16[512,2048]{1,0:T(8,128)(2,1)S(1)} %copy-done.15), custom_call_target="tpu_custom_call" | custom-call | flops 1000 | bytes 1000 | tf_op jit(solution)/shard_map/pallas_call | solution.py:253
  65.1 3.6 %collective-permute-done.15 = f32[272,128]{1,0:T(8,128)S(1)} collective-permute-done((f32[272,128]{1,0:T(8,128)S(1)}, f32[272,128]{1,0:T(8,128)S(1)}, u32[]{:S(2)}, u32[]{:S(2)}) %collective-permute-start.15) | collective-permute-done | bytes 139296 | tf_op jit(solution)/shard_map/ppermute | solution.py:266
  68.8 1.6 collective-permute-start.17
  70.3 0.5 collective-permute-start.18
  70.9 5.7 %shard_map.91 = (f32[16,8,256]{2,1,0:T(8,128)S(1)}, f32[16,128]{1,0:T(8,128)S(1)}) custom-call(s32[1]{0:T(128)} %bitcast.at_ref, bf16[256,2048]{1,0:T(8,128)(2,1)S(1)} %copy-done, f32[16,136,256]{2,1,0:T(8,128)S(1)} %shard_map.85.nd_ref, f32[16,128,256]{2,1,0:T(8,128)S(1)} %copy-done.3, f32[16,8,256]{2,1,0:T(8,128)S(1)} %get-tuple-element.114.inv_ref, ...), custom_call_target="tpu_custom_call" | custom-call | flops 1000 | bytes 1000 | tf_op jit(solution)/shard_map/pallas_call | solution.py:253
  76.7 2.1 %collective-permute-start.19 = (f32[272,128]{1,0:T(8,128)S(1)}, f32[272,128]{1,0:T(8,128)S(1)}, u32[]{:S(2)}, u32[]{:S(2)}) collective-permute-start(f32[272,128]{1,0:T(8,128)S(1)} %pad_maximum_fusion.9), channel_id=1, source_target_pairs={{0,8},{1,9},{2,10},{3,11},{4,12},{5,13},{6,14},{7,15},{8,0},{9,1},... | collective-permute-start | bytes 417800 | tf_op jit(solution)/shard_map/ppermute | solution.py:266
  78.8 14.4 %shard_map.92 = (bf16[256,2048]{1,0:T(8,128)(2,1)}, f32[256,2048]{1,0:T(8,128)S(1)}, f32[256,2048]{1,0:T(8,128)S(1)}) custom-call(s32[1]{0:T(128)} %bitcast.at_ref, bf16[256,2048]{1,0:T(8,128)(2,1)S(1)} %copy-done, bf16[256,2048]{1,0:T(8,128)(2,1)S(1)} %copy-done.6, bf16[256,2048]{1,0:T(8,128)(2,1)S(1)} %copy-done.10, f32[16,128,256]{2,1,0:T(8,128)S(1)} %copy-done.3, ...), custom_call_target="tpu_custom_call" | custom-call | flops 1000 | bytes 1000 | tf_op jit(solution)/shard_map/pallas_call | solution.py:253
  93.2 1.3 copy-done.25
  94.5 1.3 copy-done.27
  95.9 1.7 %collective-permute-done.19 = f32[272,128]{1,0:T(8,128)S(1)} collective-permute-done((f32[272,128]{1,0:T(8,128)S(1)}, f32[272,128]{1,0:T(8,128)S(1)}, u32[]{:S(2)}, u32[]{:S(2)}) %collective-permute-start.19) | collective-permute-done | bytes 139296 | tf_op jit(solution)/shard_map/ppermute | solution.py:266
  97.6 0.6 copy-done.41
  98.2 1.2 copy-done.20
  99.5 1.2 copy-done.22
  100.7 1.3 shard_map.93
  101.9 3.5 %collective-permute-done.20 = f32[272,128]{1,0:T(8,128)S(1)} collective-permute-done((f32[272,128]{1,0:T(8,128)S(1)}, f32[272,128]{1,0:T(8,128)S(1)}, u32[]{:S(2)}, u32[]{:S(2)}) %collective-permute-start.20) | collective-permute-done | bytes 139296 | tf_op jit(solution)/shard_map/ppermute | solution.py:266
  105.4 1.1 fusion.5
  106.6 1.6 collective-permute-start.31
  108.1 1.1 fusion.4
  109.3 1.2 fusion.1
  110.6 1.4 fusion.3
  112.0 0.6 collective-permute-start.22
  112.8 1.8 %collective-permute-start.23 = (f32[2,272,128]{2,1,0:T(8,128)S(1)}, f32[2,272,128]{2,1,0:T(8,128)S(1)}, u32[]{:S(2)}, u32[]{:S(2)}) collective-permute-start(f32[2,272,128]{2,1,0:T(8,128)S(1)} %pad_maximum_fusion.10), channel_id=1, source_target_pairs={{0,2},{1,3},{2,0},{3,1},{4,6},{5,7},{6,4},{7,5},{8,10},{9,11},{10,... | collective-permute-start | bytes 835592 | tf_op jit(solution)/shard_map/ppermute | solution.py:266
  114.7 1.2 slice_add_fusion
  115.9 1.2 fusion.2
  117.1 6.0 %collective-permute-done.23 = f32[2,272,128]{2,1,0:T(8,128)S(1)} collective-permute-done((f32[2,272,128]{2,1,0:T(8,128)S(1)}, f32[2,272,128]{2,1,0:T(8,128)S(1)}, u32[]{:S(2)}, u32[]{:S(2)}) %collective-permute-start.23) | collective-permute-done | bytes 278560 | tf_op jit(solution)/shard_map/ppermute | solution.py:266
  123.2 3.4 %collective-permute-done.21 = f32[2,2,64,768]{3,2,1,0:T(8,128)S(1)} collective-permute-done((f32[2,2,64,768]{3,2,1,0:T(8,128)S(1)}, f32[2,2,64,768]{3,2,1,0:T(8,128)S(1)}, u32[]{:S(2)}, u32[]{:S(2)}) %collective-permute-start.21) | collective-permute-done | bytes 786464 | tf_op jit(solution)/shard_map/ppermute | solution.py:266
  126.5 2.2 %collective-permute-done.22 = f32[2,2,64,768]{3,2,0,1:T(8,128)S(1)} collective-permute-done((f32[2,2,64,768]{3,2,0,1:T(8,128)S(1)}, f32[2,2,64,768]{3,2,0,1:T(8,128)S(1)}, u32[]{:S(2)}, u32[]{:S(2)}) %collective-permute-start.22) | collective-permute-done | bytes 786464 | tf_op jit(solution)/shard_map/ppermute | solution.py:266
  129.0 1.5 collective-permute-start.28
  130.6 1.8 %collective-permute-start.32 = (f32[2,64,512]{2,1,0:T(8,128)S(1)}, f32[2,64,512]{2,1,0:T(8,128)S(1)}, u32[]{:S(2)}, u32[]{:S(2)}) collective-permute-start(f32[2,64,512]{2,1,0:T(8,128)S(1)} %fusion.9), channel_id=1, source_target_pairs={{0,4},{1,5},{2,6},{3,7},{4,0},{5,1},{6,2},{7,3},{8,12},{9,13},{10,... | collective-permute-start | bytes 786440 | tf_op jit(solution)/shard_map/ppermute | solution.py:266
  133.4 8.4 %collective-permute-done.24 = f32[2,272,128]{2,1,0:T(8,128)S(1)} collective-permute-done((f32[2,272,128]{2,1,0:T(8,128)S(1)}, f32[2,272,128]{2,1,0:T(8,128)S(1)}, u32[]{:S(2)}, u32[]{:S(2)}) %collective-permute-start.24) | collective-permute-done | bytes 278560 | tf_op jit(solution)/shard_map/ppermute | solution.py:266
  142.2 2.7 %collective-permute-start.33 = (f32[64,512]{1,0:T(8,128)S(1)}, f32[64,512]{1,0:T(8,128)S(1)}, u32[]{:S(2)}, u32[]{:S(2)}) collective-permute-start(f32[64,512]{1,0:T(8,128)S(1)} %fusion.28), channel_id=1, source_target_pairs={{0,16},{1,17},{2,18},{3,19},{4,20},{5,21},{6,22},{7,23},{8,24},{9,... | collective-permute-start | bytes 393224 | tf_op jit(solution)/shard_map/ppermute | solution.py:266
  145.0 2.5 %collective-permute-start.29 = (f32[64,768]{1,0:T(8,128)S(1)}, f32[64,768]{1,0:T(8,128)S(1)}, u32[]{:S(2)}, u32[]{:S(2)}) collective-permute-start(f32[64,768]{1,0:T(8,128)S(1)} %fusion.11), channel_id=1, source_target_pairs={{0,16},{1,17},{2,18},{3,19},{4,20},{5,21},{6,22},{7,23},{8,24},{9,... | collective-permute-start | bytes 589832 | tf_op jit(solution)/shard_map/ppermute | solution.py:266
  147.6 4.1 %shard_map.94 = (bf16[256,2048]{1,0:T(8,128)(2,1)}, bf16[256,2048]{1,0:T(8,128)(2,1)}) custom-call(s32[1]{0:T(128)} %bitcast.at_ref, bf16[256,2048]{1,0:T(8,128)(2,1)S(1)} %copy-done.7, bf16[256,2048]{1,0:T(8,128)(2,1)S(1)} %copy-done.11, f32[256,2048]{1,0:T(8,128)S(1)} %copy-done.26, f32[256,2048]{1,0:T(8,128)S(1)} %copy-done.28, ...), custom_call_target="tpu_custom_call" | custom-call | flops 1000 | bytes 1000 | tf_op jit(solution)/shard_map/pallas_call | solution.py:253
  151.7 3.2 %collective-permute-start.27 = (f32[64,768]{1,0:T(8,128)S(1)}, f32[64,768]{1,0:T(8,128)S(1)}, u32[]{:S(2)}, u32[]{:S(2)}) collective-permute-start(f32[64,768]{1,0:T(8,128)S(1)} %fusion.13), channel_id=1, source_target_pairs={{0,2},{1,3},{2,0},{3,1},{4,6},{5,7},{6,4},{7,5},{8,10},{9,11},{10,... | collective-permute-start | bytes 589832 | tf_op jit(solution)/shard_map/ppermute | solution.py:266
  155.0 1.4 collective-permute-done.33
  156.3 3.9 %collective-permute-done.29 = f32[64,768]{1,0:T(8,128)S(1)} collective-permute-done((f32[64,768]{1,0:T(8,128)S(1)}, f32[64,768]{1,0:T(8,128)S(1)}, u32[]{:S(2)}, u32[]{:S(2)}) %collective-permute-start.29) | collective-permute-done | bytes 196640 | tf_op jit(solution)/shard_map/ppermute | solution.py:266
  160.4 0.8 pad_maximum_fusion.4
  (166 shorter events, 4.1 us)
Async XLA Ops:
  0.6 3.4 %copy-start.4 = (bf16[256,2048]{1,0:T(8,128)(2,1)S(1)}, bf16[256,2048]{1,0:T(8,128)(2,1)}, u32[]{:S(2)}) copy-start(bf16[256,2048]{1,0:T(8,128)(2,1)} %k_ref.7) | copy-start | bytes 3145732
  0.6 3.4 %copy-start.8 = (bf16[256,2048]{1,0:T(8,128)(2,1)S(1)}, bf16[256,2048]{1,0:T(8,128)(2,1)}, u32[]{:S(2)}) copy-start(bf16[256,2048]{1,0:T(8,128)(2,1)} %v_ref.7) | copy-start | bytes 3145732
  3.6 17.4 %collective-permute-start.4 = (f32[256,2048]{1,0:T(8,128)}, f32[256,2048]{1,0:T(8,128)}, u32[]{:S(2)}, u32[]{:S(2)}) collective-permute-start(f32[256,2048]{1,0:T(8,128)} %convert_element_type.3), channel_id=1, source_target_pairs={{0,1},{1,0},{2,3},{3,2},{4,5},{5,4},{6,7},{7,6},{8,9},{9,8},{10,11... | collective-permute-start | bytes 6291464 | tf_op jit(solution)/shard_map/ppermute | solution.py:266
  4.0 9.2 %copy-start = (bf16[256,2048]{1,0:T(8,128)(2,1)S(1)}, bf16[256,2048]{1,0:T(8,128)(2,1)}, u32[]{:S(2)}) copy-start(bf16[256,2048]{1,0:T(8,128)(2,1)} %q_ref.6) | copy-start | bytes 3145732
  4.0 9.2 %copy-start.5 = (bf16[256,2048]{1,0:T(8,128)(2,1)S(1)}, bf16[256,2048]{1,0:T(8,128)(2,1)}, u32[]{:S(2)}) copy-start(bf16[256,2048]{1,0:T(8,128)(2,1)} %k_ref.7) | copy-start | bytes 3145732
  4.0 9.2 %copy-start.9 = (bf16[256,2048]{1,0:T(8,128)(2,1)S(1)}, bf16[256,2048]{1,0:T(8,128)(2,1)}, u32[]{:S(2)}) copy-start(bf16[256,2048]{1,0:T(8,128)(2,1)} %v_ref.7) | copy-start | bytes 3145732
  6.5 14.5 %copy-start.23 = (f32[4,272,128]{2,1,0:T(8,128)}, f32[4,272,128]{2,1,0:T(8,128)S(1)}, u32[]{:S(2)}) copy-start(f32[4,272,128]{2,1,0:T(8,128)S(1)} %get-tuple-element.94) | copy-start | bytes 1671172
  6.5 2.1 %collective-permute-start = (f32[4,272,128]{2,1,0:T(8,128)S(1)}, f32[4,272,128]{2,1,0:T(8,128)S(1)}, u32[]{:S(2)}, u32[]{:S(2)}) collective-permute-start(f32[4,272,128]{2,1,0:T(8,128)S(1)} %get-tuple-element.95), channel_id=1, source_target_pairs={{0,1},{1,0},{2,3},{3,2},{4,5},{5,4},{6,7},{7,6},{8,9},{9,8},{10,11... | collective-permute-start | bytes 1671176 | tf_op jit(solution)/shard_map/ppermute | solution.py:266
  8.6 32.8 %copy-start.17 = (f32[4,272,128]{2,1,0:T(8,128)}, f32[4,272,128]{2,1,0:T(8,128)S(1)}, u32[]{:S(2)}) copy-start(f32[4,272,128]{2,1,0:T(8,128)S(1)} %collective-permute-done.mate_ref) | copy-start | bytes 1671172
  8.7 12.3 %collective-permute-start.3 = (f32[272,128]{1,0:T(8,128)S(1)}, f32[272,128]{1,0:T(8,128)S(1)}, u32[]{:S(2)}, u32[]{:S(2)}) collective-permute-start(f32[272,128]{1,0:T(8,128)S(1)} %get-tuple-element.193), channel_id=1, source_target_pairs={{0,6},{1,7},{2,4},{3,5},{4,2},{5,3},{6,0},{7,1},{8,14},{9,15},{10,... | collective-permute-start | bytes 417800 | tf_op jit(solution)/shard_map/ppermute | solution.py:266
  12.6 8.4 %collective-permute-start.2 = (f32[272,128]{1,0:T(8,128)S(1)}, f32[272,128]{1,0:T(8,128)S(1)}, u32[]{:S(2)}, u32[]{:S(2)}) collective-permute-start(f32[272,128]{1,0:T(8,128)S(1)} %get-tuple-element.194), channel_id=1, source_target_pairs={{0,4},{1,5},{2,6},{3,7},{4,0},{5,1},{6,2},{7,3},{8,12},{9,13},{10,... | collective-permute-start | bytes 417800 | tf_op jit(solution)/shard_map/ppermute | solution.py:266
  13.1 7.9 %collective-permute-start.1 = (f32[272,128]{1,0:T(8,128)S(1)}, f32[272,128]{1,0:T(8,128)S(1)}, u32[]{:S(2)}, u32[]{:S(2)}) collective-permute-start(f32[272,128]{1,0:T(8,128)S(1)} %get-tuple-element.192), channel_id=1, source_target_pairs={{0,2},{1,3},{2,0},{3,1},{4,6},{5,7},{6,4},{7,5},{8,10},{9,11},{10,... | collective-permute-start | bytes 417800 | tf_op jit(solution)/shard_map/ppermute | solution.py:266
  13.2 17.5 %copy-start.12 = (bf16[256,2048]{1,0:T(8,128)(2,1)S(1)}, bf16[256,2048]{1,0:T(8,128)(2,1)}, u32[]{:S(2)}) copy-start(bf16[256,2048]{1,0:T(8,128)(2,1)} %own_ref.1) | copy-start | bytes 3145732
  21.0 20.4 %collective-permute-start.5 = (f32[272,128]{1,0:T(8,128)S(1)}, f32[272,128]{1,0:T(8,128)S(1)}, u32[]{:S(2)}, u32[]{:S(2)}) collective-permute-start(f32[272,128]{1,0:T(8,128)S(1)} %get-tuple-element.97), channel_id=1, source_target_pairs={{0,8},{1,9},{2,10},{3,11},{4,12},{5,13},{6,14},{7,15},{8,16},{9,17... | collective-permute-start | bytes 417800 | tf_op jit(solution)/shard_map/ppermute | solution.py:279
  24.9 16.5 %collective-permute-start.6 = (f32[272,128]{1,0:T(8,128)S(1)}, f32[272,128]{1,0:T(8,128)S(1)}, u32[]{:S(2)}, u32[]{:S(2)}) collective-permute-start(f32[272,128]{1,0:T(8,128)S(1)} %get-tuple-element.97), channel_id=1, source_target_pairs={{0,16},{1,17},{2,18},{3,19},{4,20},{5,21},{6,22},{7,23},{8,24},{9,... | collective-permute-start | bytes 417800 | tf_op jit(solution)/shard_map/ppermute | solution.py:279
  29.4 12.0 %collective-permute-start.7 = (f32[272,128]{1,0:T(8,128)S(1)}, f32[272,128]{1,0:T(8,128)S(1)}, u32[]{:S(2)}, u32[]{:S(2)}) collective-permute-start(f32[272,128]{1,0:T(8,128)S(1)} %get-tuple-element.97), channel_id=1, source_target_pairs={{0,24},{1,25},{2,26},{3,27},{4,28},{5,29},{6,30},{7,31}} | collective-permute-start | bytes 417800 | tf_op jit(solution)/shard_map/ppermute | solution.py:279
  42.3 9.9 %collective-permute-start.8 = (f32[272,128]{1,0:T(8,128)}, f32[272,128]{1,0:T(8,128)}, u32[]{:S(2)}, u32[]{:S(2)}) collective-permute-start(f32[272,128]{1,0:T(8,128)} %get-tuple-element.108), channel_id=1, source_target_pairs={{0,2},{1,3},{2,0},{3,1},{4,6},{5,7},{6,4},{7,5},{8,10},{9,11},{10,... | collective-permute-start | bytes 417800 | tf_op jit(solution)/shard_map/ppermute | solution.py:266
  43.8 8.4 %collective-permute-start.9 = (f32[272,128]{1,0:T(8,128)}, f32[272,128]{1,0:T(8,128)}, u32[]{:S(2)}, u32[]{:S(2)}) collective-permute-start(f32[272,128]{1,0:T(8,128)} %get-tuple-element.109), channel_id=1, source_target_pairs={{0,4},{1,5},{2,6},{3,7},{4,0},{5,1},{6,2},{7,3},{8,12},{9,13},{10,... | collective-permute-start | bytes 417800 | tf_op jit(solution)/shard_map/ppermute | solution.py:266
  45.3 6.9 %collective-permute-start.10 = (f32[272,128]{1,0:T(8,128)}, f32[272,128]{1,0:T(8,128)}, u32[]{:S(2)}, u32[]{:S(2)}) collective-permute-start(f32[272,128]{1,0:T(8,128)} %get-tuple-element.110), channel_id=1, source_target_pairs={{0,6},{1,7},{2,4},{3,5},{4,2},{5,3},{6,0},{7,1},{8,14},{9,15},{10,... | collective-permute-start | bytes 417800 | tf_op jit(solution)/shard_map/ppermute | solution.py:266
  47.4 4.9 %copy-start.18 = (f32[4,272,128]{2,1,0:T(8,128)S(1)}, f32[4,272,128]{2,1,0:T(8,128)}, u32[]{:S(2)}) copy-start(f32[4,272,128]{2,1,0:T(8,128)} %copy-done.17) | copy-start | bytes 1671172
  47.4 4.9 %copy-start.24 = (f32[4,272,128]{2,1,0:T(8,128)S(1)}, f32[4,272,128]{2,1,0:T(8,128)}, u32[]{:S(2)}) copy-start(f32[4,272,128]{2,1,0:T(8,128)} %copy-done.23) | copy-start | bytes 1671172
  52.2 2.0 %collective-permute-start.11 = (f32[4,272,128]{2,1,0:T(8,128)S(1)}, f32[4,272,128]{2,1,0:T(8,128)S(1)}, u32[]{:S(2)}, u32[]{:S(2)}) collective-permute-start(f32[4,272,128]{2,1,0:T(8,128)S(1)} %get-tuple-element.112), channel_id=1, source_target_pairs={{0,1},{1,0},{2,3},{3,2},{4,5},{5,4},{6,7},{7,6},{8,9},{9,8},{10,11... | collective-permute-start | bytes 1671176 | tf_op jit(solution)/shard_map/ppermute | solution.py:266
  53.5 2.1 %collective-permute-start.12 = (f32[4,272,128]{2,1,0:T(8,128)S(1)}, f32[4,272,128]{2,1,0:T(8,128)S(1)}, u32[]{:S(2)}, u32[]{:S(2)}) collective-permute-start(f32[4,272,128]{2,1,0:T(8,128)S(1)} %pad_maximum_fusion.1), channel_id=1, source_target_pairs={{0,1},{1,0},{2,3},{3,2},{4,5},{5,4},{6,7},{7,6},{8,9},{9,8},{10,11... | collective-permute-start | bytes 1671176 | tf_op jit(solution)/shard_map/ppermute | solution.py:266
  54.2 4.2 %copy-start.29 = (f32[4,272,128]{2,1,0:T(8,128)}, f32[4,272,128]{2,1,0:T(8,128)S(1)}, u32[]{:S(2)}) copy-start(f32[4,272,128]{2,1,0:T(8,128)S(1)} %collective-permute-done.11) | copy-start | bytes 1671172
  55.1 21.5 %copy-start.31 = (f32[272,128]{1,0:T(8,128)}, f32[272,128]{1,0:T(8,128)S(1)}, u32[]{:S(2)}) copy-start(f32[272,128]{1,0:T(8,128)S(1)} %get-tuple-element.125) | copy-start | bytes 417796
  55.6 6.7 %copy-start.15 = (bf16[512,2048]{1,0:T(8,128)(2,1)S(1)}, bf16[512,2048]{1,0:T(8,128)(2,1)}, u32[]{:S(2)}) copy-start(bf16[512,2048]{1,0:T(8,128)(2,1)} %copy-done.14) | copy-start | bytes 6291460
  58.4 6.7 %copy-start.19 = (f32[16,64,256]{2,1,0:T(8,128)}, f32[16,64,256]{2,1,0:T(8,128)S(1)}, u32[]{:S(2)}) copy-start(f32[16,64,256]{2,1,0:T(8,128)S(1)} %get-tuple-element.119.a0_ref) | copy-start | bytes 3145732
  58.4 3.9 %collective-permute-start.13 = (f32[16,64,256]{2,1,0:T(8,128)S(1)}, f32[16,64,256]{2,1,0:T(8,128)S(1)}, u32[]{:S(2)}, u32[]{:S(2)}) collective-permute-start(f32[16,64,256]{2,1,0:T(8,128)S(1)} %get-tuple-element.120), channel_id=1, source_target_pairs={{0,1},{1,0},{2,3},{3,2},{4,5},{5,4},{6,7},{7,6},{8,9},{9,8},{10,11... | collective-permute-start | bytes 3145736 | tf_op jit(solution)/shard_map/ppermute | solution.py:266
  58.8 6.3 %collective-permute-start.14 = (f32[272,128]{1,0:T(8,128)S(1)}, f32[272,128]{1,0:T(8,128)S(1)}, u32[]{:S(2)}, u32[]{:S(2)}) collective-permute-start(f32[272,128]{1,0:T(8,128)S(1)} %get-tuple-element.190), channel_id=1, source_target_pairs={{0,2},{1,3},{2,0},{3,1},{4,6},{5,7},{6,4},{7,5},{8,10},{9,11},{10,... | collective-permute-start | bytes 417800 | tf_op jit(solution)/shard_map/ppermute | solution.py:266
  60.3 8.4 %collective-permute-start.15 = (f32[272,128]{1,0:T(8,128)S(1)}, f32[272,128]{1,0:T(8,128)S(1)}, u32[]{:S(2)}, u32[]{:S(2)}) collective-permute-start(f32[272,128]{1,0:T(8,128)S(1)} %get-tuple-element.189), channel_id=1, source_target_pairs={{0,4},{1,5},{2,6},{3,7},{4,0},{5,1},{6,2},{7,3},{8,12},{9,13},{10,... | collective-permute-start | bytes 417800 | tf_op jit(solution)/shard_map/ppermute | solution.py:266
  61.9 6.9 %collective-permute-start.16 = (f32[272,128]{1,0:T(8,128)S(1)}, f32[272,128]{1,0:T(8,128)S(1)}, u32[]{:S(2)}, u32[]{:S(2)}) collective-permute-start(f32[272,128]{1,0:T(8,128)S(1)} %get-tuple-element.188), channel_id=1, source_target_pairs={{0,6},{1,7},{2,4},{3,5},{4,2},{5,3},{6,0},{7,1},{8,14},{9,15},{10,... | collective-permute-start | bytes 417800 | tf_op jit(solution)/shard_map/ppermute | solution.py:266
  62.3 8.5 %copy-start.3 = (f32[16,128,256]{2,1,0:T(8,128)S(1)}, f32[16,128,256]{2,1,0:T(8,128)}, u32[]{:S(2)}) copy-start(f32[16,128,256]{2,1,0:T(8,128)} %copy-done.1) | copy-start | bytes 6291460
  65.1 11.5 %copy-start.37 = (f32[272,128]{1,0:T(8,128)}, f32[272,128]{1,0:T(8,128)S(1)}, u32[]{:S(2)}) copy-start(f32[272,128]{1,0:T(8,128)S(1)} %collective-permute-done.14) | copy-start | bytes 417796
  68.8 7.9 %copy-start.33 = (f32[272,128]{1,0:T(8,128)}, f32[272,128]{1,0:T(8,128)S(1)}, u32[]{:S(2)}) copy-start(f32[272,128]{1,0:T(8,128)S(1)} %collective-permute-done.15) | copy-start | bytes 417796
  68.8 7.9 %copy-start.35 = (f32[272,128]{1,0:T(8,128)}, f32[272,128]{1,0:T(8,128)S(1)}, u32[]{:S(2)}) copy-start(f32[272,128]{1,0:T(8,128)S(1)} %collective-permute-done.16) | copy-start | bytes 417796
  68.8 40.5 %collective-permute-start.17 = (f32[8,64,768]{2,1,0:T(8,128)}, f32[8,64,768]{2,1,0:T(8,128)}, u32[]{:S(2)}, u32[]{:S(2)}) collective-permute-start(f32[8,64,768]{2,1,0:T(8,128)} %get-tuple-element.129), channel_id=1, source_target_pairs={{0,4},{1,5},{2,6},{3,7},{4,0},{5,1},{6,2},{7,3},{8,12},{9,13},{10,... | collective-permute-start | bytes 4718600 | tf_op jit(solution)/shard_map/ppermute | solution.py:266
  70.3 38.9 %collective-permute-start.18 = (f32[8,64,768]{2,1,0:T(8,128)}, f32[8,64,768]{2,1,0:T(8,128)}, u32[]{:S(2)}, u32[]{:S(2)}) collective-permute-start(f32[8,64,768]{2,1,0:T(8,128)} %get-tuple-element.130), channel_id=1, source_target_pairs={{0,2},{1,3},{2,0},{3,1},{4,6},{5,7},{6,4},{7,5},{8,10},{9,11},{10,... | collective-permute-start | bytes 4718600 | tf_op jit(solution)/shard_map/ppermute | solution.py:266
  70.9 34.5 %collective-permute-start.30 = (f32[8,64,512]{2,1,0:T(8,128)}, f32[8,64,512]{2,1,0:T(8,128)}, u32[]{:S(2)}, u32[]{:S(2)}) collective-permute-start(f32[8,64,512]{2,1,0:T(8,128)} %get-tuple-element.131), channel_id=1, source_target_pairs={{0,8},{1,9},{2,10},{3,11},{4,12},{5,13},{6,14},{7,15},{8,0},{9,1},... | collective-permute-start | bytes 3145736 | tf_op jit(solution)/shard_map/ppermute | solution.py:266
  70.9 7.9 %copy-start.6 = (bf16[256,2048]{1,0:T(8,128)(2,1)S(1)}, bf16[256,2048]{1,0:T(8,128)(2,1)}, u32[]{:S(2)}) copy-start(bf16[256,2048]{1,0:T(8,128)(2,1)} %k_ref.7) | copy-start | bytes 3145732
  70.9 7.9 %copy-start.10 = (bf16[256,2048]{1,0:T(8,128)(2,1)S(1)}, bf16[256,2048]{1,0:T(8,128)(2,1)}, u32[]{:S(2)}) copy-start(bf16[256,2048]{1,0:T(8,128)(2,1)} %v_ref.7) | copy-start | bytes 3145732
  76.7 20.8 %collective-permute-start.19 = (f32[272,128]{1,0:T(8,128)S(1)}, f32[272,128]{1,0:T(8,128)S(1)}, u32[]{:S(2)}, u32[]{:S(2)}) collective-permute-start(f32[272,128]{1,0:T(8,128)S(1)} %pad_maximum_fusion.9), channel_id=1, source_target_pairs={{0,8},{1,9},{2,10},{3,11},{4,12},{5,13},{6,14},{7,15},{8,0},{9,1},... | collective-permute-start | bytes 417800 | tf_op jit(solution)/shard_map/ppermute | solution.py:266
  78.8 19.4 %copy-start.16 = (bf16[512,2048]{1,0:T(8,128)(2,1)S(1)}, bf16[512,2048]{1,0:T(8,128)(2,1)}, u32[]{:S(2)}) copy-start(bf16[512,2048]{1,0:T(8,128)(2,1)} %copy-done.14) | copy-start | bytes 6291460
  98.2 7.2 %collective-permute-start.20 = (f32[272,128]{1,0:T(8,128)S(1)}, f32[272,128]{1,0:T(8,128)S(1)}, u32[]{:S(2)}, u32[]{:S(2)}) collective-permute-start(f32[272,128]{1,0:T(8,128)S(1)} %fusion.39), channel_id=1, source_target_pairs={{0,16},{1,17},{2,18},{3,19},{4,20},{5,21},{6,22},{7,23},{8,24},{9,... | collective-permute-start | bytes 417800 | tf_op jit(solution)/shard_map/ppermute | solution.py:266
  100.7 4.7 %copy-start.42 = (f32[272,128]{1,0:T(8,128)S(1)}, f32[272,128]{1,0:T(8,128)}, u32[]{:S(2)}) copy-start(f32[272,128]{1,0:T(8,128)} %copy-done.41) | copy-start | bytes 417796
  106.6 24.0 %collective-permute-start.31 = (f32[2,2,64,512]{3,2,0,1:T(8,128)S(1)}, f32[2,2,64,512]{3,2,0,1:T(8,128)S(1)}, u32[]{:S(2)}, u32[]{:S(2)}) collective-permute-start(f32[2,2,64,512]{3,2,0,1:T(8,128)S(1)} %fusion.5), channel_id=1, source_target_pairs={{0,2},{1,3},{2,0},{3,1},{4,6},{5,7},{6,4},{7,5},{8,10},{9,11},{10,... | collective-permute-start | bytes 1572872 | tf_op jit(solution)/shard_map/ppermute | solution.py:266
  110.5 16.0 %collective-permute-start.21 = (f32[2,2,64,768]{3,2,1,0:T(8,128)S(1)}, f32[2,2,64,768]{3,2,1,0:T(8,128)S(1)}, u32[]{:S(2)}, u32[]{:S(2)}) collective-permute-start(f32[2,2,64,768]{3,2,1,0:T(8,128)S(1)} %fusion.1), channel_id=1, source_target_pairs={{0,8},{1,9},{2,10},{3,11},{4,12},{5,13},{6,14},{7,15},{8,0},{9,1},... | collective-permute-start | bytes 2359304 | tf_op jit(solution)/shard_map/ppermute | solution.py:266
  112.0 16.7 %collective-permute-start.22 = (f32[2,2,64,768]{3,2,0,1:T(8,128)S(1)}, f32[2,2,64,768]{3,2,0,1:T(8,128)S(1)}, u32[]{:S(2)}, u32[]{:S(2)}) collective-permute-start(f32[2,2,64,768]{3,2,0,1:T(8,128)S(1)} %fusion.3), channel_id=1, source_target_pairs={{0,4},{1,5},{2,6},{3,7},{4,0},{5,1},{6,2},{7,3},{8,12},{9,13},{10,... | collective-permute-start | bytes 2359304 | tf_op jit(solution)/shard_map/ppermute | solution.py:266
  112.8 10.4 %collective-permute-start.23 = (f32[2,272,128]{2,1,0:T(8,128)S(1)}, f32[2,272,128]{2,1,0:T(8,128)S(1)}, u32[]{:S(2)}, u32[]{:S(2)}) collective-permute-start(f32[2,272,128]{2,1,0:T(8,128)S(1)} %pad_maximum_fusion.10), channel_id=1, source_target_pairs={{0,2},{1,3},{2,0},{3,1},{4,6},{5,7},{6,4},{7,5},{8,10},{9,11},{10,... | collective-permute-start | bytes 835592 | tf_op jit(solution)/shard_map/ppermute | solution.py:266
  123.2 7.4 %copy-start.39 = (f32[2,272,128]{2,1,0:T(8,128)}, f32[2,272,128]{2,1,0:T(8,128)S(1)}, u32[]{:S(2)}) copy-start(f32[2,272,128]{2,1,0:T(8,128)S(1)} %collective-permute-done.23) | copy-start | bytes 835588
  128.7 23.0 %collective-permute-start.26 = (f32[2,64,768]{2,1,0:T(8,128)S(1)}, f32[2,64,768]{2,1,0:T(8,128)S(1)}, u32[]{:S(2)}, u32[]{:S(2)}) collective-permute-start(f32[2,64,768]{2,1,0:T(8,128)S(1)} %fusion.8), channel_id=1, source_target_pairs={{0,16},{1,17},{2,18},{3,19},{4,20},{5,21},{6,22},{7,23},{8,24},{9,... | collective-permute-start | bytes 1179656 | tf_op jit(solution)/shard_map/ppermute | solution.py:266
  129.0 16.0 %collective-permute-start.28 = (f32[2,64,768]{2,1,0:T(8,128)S(1)}, f32[2,64,768]{2,1,0:T(8,128)S(1)}, u32[]{:S(2)}, u32[]{:S(2)}) collective-permute-start(f32[2,64,768]{2,1,0:T(8,128)S(1)} %fusion.6), channel_id=1, source_target_pairs={{0,8},{1,9},{2,10},{3,11},{4,12},{5,13},{6,14},{7,15},{8,0},{9,1},... | collective-permute-start | bytes 1179656 | tf_op jit(solution)/shard_map/ppermute | solution.py:266
  130.6 11.6 %collective-permute-start.32 = (f32[2,64,512]{2,1,0:T(8,128)S(1)}, f32[2,64,512]{2,1,0:T(8,128)S(1)}, u32[]{:S(2)}, u32[]{:S(2)}) collective-permute-start(f32[2,64,512]{2,1,0:T(8,128)S(1)} %fusion.9), channel_id=1, source_target_pairs={{0,4},{1,5},{2,6},{3,7},{4,0},{5,1},{6,2},{7,3},{8,12},{9,13},{10,... | collective-permute-start | bytes 786440 | tf_op jit(solution)/shard_map/ppermute | solution.py:266
  132.5 9.3 %collective-permute-start.24 = (f32[2,272,128]{2,1,0:T(8,128)S(1)}, f32[2,272,128]{2,1,0:T(8,128)S(1)}, u32[]{:S(2)}, u32[]{:S(2)}) collective-permute-start(f32[2,272,128]{2,1,0:T(8,128)S(1)} %pad_maximum_fusion.11), channel_id=1, source_target_pairs={{0,4},{1,5},{2,6},{3,7},{4,0},{5,1},{6,2},{7,3},{8,12},{9,13},{10,... | collective-permute-start | bytes 835592 | tf_op jit(solution)/shard_map/ppermute | solution.py:266
  132.8 9.0 %copy-start.40 = (f32[2,272,128]{2,1,0:T(8,128)S(1)}, f32[2,272,128]{2,1,0:T(8,128)}, u32[]{:S(2)}) copy-start(f32[2,272,128]{2,1,0:T(8,128)} %copy-done.39) | copy-start | bytes 835588
  132.9 8.9 %copy-start.45 = (f32[1,272,128]{2,1,0:T(8,128)S(1)}, f32[1,272,128]{2,1,0:T(8,128)}, u32[]{:S(2)}) copy-start(f32[1,272,128]{2,1,0:T(8,128)} %get-tuple-element.200) | copy-start | bytes 417796
  132.9 8.9 %copy-start.46 = (f32[1,272,128]{2,1,0:T(8,128)S(1)}, f32[1,272,128]{2,1,0:T(8,128)}, u32[]{:S(2)}) copy-start(f32[1,272,128]{2,1,0:T(8,128)} %get-tuple-element.201) | copy-start | bytes 417796
  141.8 5.8 %copy-start.28 = (f32[256,2048]{1,0:T(8,128)S(1)}, f32[256,2048]{1,0:T(8,128)}, u32[]{:S(2)}) copy-start(f32[256,2048]{1,0:T(8,128)} %copy-done.27) | copy-start | bytes 6291460
  142.0 5.6 %copy-start.26 = (f32[256,2048]{1,0:T(8,128)S(1)}, f32[256,2048]{1,0:T(8,128)}, u32[]{:S(2)}) copy-start(f32[256,2048]{1,0:T(8,128)} %copy-done.25) | copy-start | bytes 6291460
  142.0 5.6 %copy-start.7 = (bf16[256,2048]{1,0:T(8,128)(2,1)S(1)}, bf16[256,2048]{1,0:T(8,128)(2,1)}, u32[]{:S(2)}) copy-start(bf16[256,2048]{1,0:T(8,128)(2,1)} %k_ref.7) | copy-start | bytes 3145732
  142.1 5.6 %copy-start.11 = (bf16[256,2048]{1,0:T(8,128)(2,1)S(1)}, bf16[256,2048]{1,0:T(8,128)(2,1)}, u32[]{:S(2)}) copy-start(bf16[256,2048]{1,0:T(8,128)(2,1)} %v_ref.7) | copy-start | bytes 3145732
  142.1 5.5 %collective-permute-start.25 = (f32[4,272,128]{2,1,0:T(8,128)S(1)}, f32[4,272,128]{2,1,0:T(8,128)S(1)}, u32[]{:S(2)}, u32[]{:S(2)}) collective-permute-start(f32[4,272,128]{2,1,0:T(8,128)S(1)} %pad_maximum_fusion.2), channel_id=1, source_target_pairs={{0,1},{1,0},{2,3},{3,2},{4,5},{5,4},{6,7},{7,6},{8,9},{9,8},{10,11... | collective-permute-start | bytes 1671176 | tf_op jit(solution)/shard_map/ppermute | solution.py:266
  142.2 14.1 %collective-permute-start.33 = (f32[64,512]{1,0:T(8,128)S(1)}, f32[64,512]{1,0:T(8,128)S(1)}, u32[]{:S(2)}, u32[]{:S(2)}) collective-permute-start(f32[64,512]{1,0:T(8,128)S(1)} %fusion.28), channel_id=1, source_target_pairs={{0,16},{1,17},{2,18},{3,19},{4,20},{5,21},{6,22},{7,23},{8,24},{9,... | collective-permute-start | bytes 393224 | tf_op jit(solution)/shard_map/ppermute | solution.py:266
  145.0 15.3 %collective-permute-start.29 = (f32[64,768]{1,0:T(8,128)S(1)}, f32[64,768]{1,0:T(8,128)S(1)}, u32[]{:S(2)}, u32[]{:S(2)}) collective-permute-start(f32[64,768]{1,0:T(8,128)S(1)} %fusion.11), channel_id=1, source_target_pairs={{0,16},{1,17},{2,18},{3,19},{4,20},{5,21},{6,22},{7,23},{8,24},{9,... | collective-permute-start | bytes 589832 | tf_op jit(solution)/shard_map/ppermute | solution.py:266
  151.7 8.5 %collective-permute-start.27 = (f32[64,768]{1,0:T(8,128)S(1)}, f32[64,768]{1,0:T(8,128)S(1)}, u32[]{:S(2)}, u32[]{:S(2)}) collective-permute-start(f32[64,768]{1,0:T(8,128)S(1)} %fusion.13), channel_id=1, source_target_pairs={{0,2},{1,3},{2,0},{3,1},{4,6},{5,7},{6,4},{7,5},{8,10},{9,11},{10,... | collective-permute-start | bytes 589832 | tf_op jit(solution)/shard_map/ppermute | solution.py:266
  (18 other events, 32.2 us)

commit v5 on v4

--- a/solution.py
+++ b/solution.py
@@ -334,7 +334,7 @@
 
     keep, send = call(summary_kernel, packs, at, keys, values, scratch=(pltpu.VMEM((HEADS, HEAD), F32),))
     mate = swap(send, 1)
-    grad_mate = swap(out_grad.astype(F32), 1)
+    grad_mate = swap(after(mate, out_grad).astype(F32), 1)
     (inner,) = call(
         inner_kernel, [shape((HEADS, ROWS, t), F32)], at, queries, keys, values
     )

time: 162 us -> 160 us (0.988)
  other arithmetic: 14.4 us -> 11.7 us
  local copies, waits for them, and re-layouts: 13.9 us -> 16.3 us
    convert_element_type x1, other arithmetic: 2.93 us -> 0.23 us  [body(): grad_mate = swap(after(mate, out_grad).astype(F32), 1)]
    unnamed x94, local copies, waits for them, and re-layouts: 13.5 us -> 16 us
  transfers between devices with their start and end apart: 34 -> 34, of which waited for: 12 -> 12; matrix products, arithmetic and copies ran while one was open for 7% -> 7% of each run, Pallas kernels for 30% -> 28%
where the time goes in v5:
time: 160 us; the launch traced here: 159 us
  Pallas kernels  50 us (31%)
  starting transfers between devices  43.5 us (27%)
  waiting for transfers between devices  36.3 us (23%)
  local copies, waits for them, and re-layouts  16.3 us (10%)
  other arithmetic  11.7 us (7%)
    pallas_call x10, Pallas kernels, call(): pl.pallas_call(kernel, out_shape=tuple(outs), in_specs=specs, out_specs=t...  46.7 us
    ppermute x31, waiting for transfers between devices, swap(): return lax.ppermute(x, 'seq', [(i, i ^ mask) for i in range(n)])  36.2 us
    ppermute x31, starting transfers between devices, swap(): return lax.ppermute(x, 'seq', [(i, i ^ mask) for i in range(n)])  33.8 us
    unnamed x94, local copies, waits for them, and re-layouts  16 us
    ppermute x3, starting transfers between devices, along(): lax.ppermute(layer, 'seq', [(b, a) for a, b in pairs] if later else pairs)  9.68 us
    pallas_call x1, Pallas kernels, attended_grad(): pl.pallas_call(grad_kernel, grid=(steps,), out_shape=(jax.ShapeDtypeStruc...  3.33 us
  transfers between devices with their start and end apart: 34, of which 12 were waited for; matrix products, arithmetic and copies ran while one was open for 7% of the time, Pallas kernels for 28%

profile of v5, /device:TPU:0, one launch (start us, length us, event | category | flops | bytes accessed | tf_op | source)
XLA Modules:
  0.0 159.3 jit_solution(8405313273623299624)
XLA Ops:
  0.6 1.2 copy-done.4
  1.9 1.2 copy-done.8
  3.1 2.4 %shard_map.84 = (f32[4,272,128]{2,1,0:T(8,128)S(1)}, f32[4,272,128]{2,1,0:T(8,128)S(1)}) custom-call(s32[1]{0:T(128)} %bitcast.at_ref, bf16[256,2048]{1,0:T(8,128)(2,1)S(1)} %copy-done.4, bf16[256,2048]{1,0:T(8,128)(2,1)S(1)} %copy-done.8), custom_call_target="tpu_custom_call" | custom-call | flops 1000 | bytes 1000 | tf_op jit(solution)/shard_map/pallas_call | solution.py:253
  5.6 0.5 collective-permute-start
  6.1 1.6 collective-permute-done.mate_ref
  8.4 3.7 %collective-permute-start.3 = (f32[272,128]{1,0:T(8,128)S(1)}, f32[272,128]{1,0:T(8,128)S(1)}, u32[]{:S(2)}, u32[]{:S(2)}) collective-permute-start(f32[272,128]{1,0:T(8,128)S(1)} %get-tuple-element.195), channel_id=1, source_target_pairs={{0,6},{1,7},{2,4},{3,5},{4,2},{5,3},{6,0},{7,1},{8,14},{9,15},{10,... | collective-permute-start | bytes 417800 | tf_op jit(solution)/shard_map/ppermute | solution.py:266
  12.1 0.5 collective-permute-start.2
  12.7 7.7 %shard_map.85.nd_ref = f32[16,136,256]{2,1,0:T(8,128)S(1)} custom-call(s32[1]{0:T(128)} %bitcast.at_ref, bf16[256,2048]{1,0:T(8,128)(2,1)S(1)} %copy-done, bf16[256,2048]{1,0:T(8,128)(2,1)S(1)} %copy-done.5, bf16[256,2048]{1,0:T(8,128)(2,1)S(1)} %copy-done.9), custom_call_target="tpu_custom_call" | custom-call | flops 1000 | bytes 1000 | tf_op jit(solution)/shard_map/pallas_call | solution.py:253
  20.5 3.9 %collective-permute-start.5 = (f32[272,128]{1,0:T(8,128)S(1)}, f32[272,128]{1,0:T(8,128)S(1)}, u32[]{:S(2)}, u32[]{:S(2)}) collective-permute-start(f32[272,128]{1,0:T(8,128)S(1)} %get-tuple-element.99), channel_id=1, source_target_pairs={{0,8},{1,9},{2,10},{3,11},{4,12},{5,13},{6,14},{7,15},{8,16},{9,17... | collective-permute-start | bytes 417800 | tf_op jit(solution)/shard_map/ppermute | solution.py:279
  24.4 4.5 %collective-permute-start.6 = (f32[272,128]{1,0:T(8,128)S(1)}, f32[272,128]{1,0:T(8,128)S(1)}, u32[]{:S(2)}, u32[]{:S(2)}) collective-permute-start(f32[272,128]{1,0:T(8,128)S(1)} %get-tuple-element.99), channel_id=1, source_target_pairs={{0,16},{1,17},{2,18},{3,19},{4,20},{5,21},{6,22},{7,23},{8,24},{9,... | collective-permute-start | bytes 417800 | tf_op jit(solution)/shard_map/ppermute | solution.py:279
  28.9 1.3 collective-permute-start.7
  30.2 3.4 %copy-done.13 = bf16[2048,2048]{1,0:T(8,128)(2,1)S(1)} copy-done((bf16[2048,2048]{1,0:T(8,128)(2,1)S(1)}, bf16[2048,2048]{1,0:T(8,128)(2,1)}, u32[]{:S(2)}) %copy-start.13) | copy-done | bytes 8388632
  33.6 3.3 %shard_map.86 = (f32[16,128,256]{2,1,0:T(8,128)S(1)}, bf16[512,2048]{1,0:T(8,128)(2,1)S(1)}) custom-call(bf16[256,2048]{1,0:T(8,128)(2,1)S(1)} %copy-done.12, bf16[2048,2048]{1,0:T(8,128)(2,1)S(1)} %copy-done.13, bf16[256,2048]{1,0:T(8,128)(2,1)S(1)} %copy-done.12, f32[256,2048]{1,0:T(8,128)S(1)} %collective-permute-done.4.mate_ref), custom_call_target="tpu_custom_call" | custom-call | flops 1000 | bytes 1000 | tf_op jit(solution)/shard_map/pallas_call | solution.py:123
  37.0 1.3 copy-done.1
  38.3 1.3 copy-done.14
  39.6 0.8 shard_map.87
  40.5 1.5 collective-permute-start.8
  41.9 1.5 collective-permute-start.9
  43.5 0.5 collective-permute-start.10
  44.0 1.6 copy-done.2
  45.5 4.8 %shard_map.88 = (f32[4,272,128]{2,1,0:T(8,128)S(1)}, f32[4,272,128]{2,1,0:T(8,128)S(1)}, f32[16,8,256]{2,1,0:T(8,128)S(1)}) custom-call(s32[1]{0:T(128)} %bitcast.at_ref, bf16[256,2048]{1,0:T(8,128)(2,1)S(1)} %copy-done, f32[16,136,256]{2,1,0:T(8,128)S(1)} %shard_map.85.nd_ref, f32[16,128,256]{2,1,0:T(8,128)S(1)} %copy-done.2, ...), custom_call_target="tpu_custom_call" | custom-call | flops 1000 | bytes 1000 | tf_op jit(solution)/shard_map/pallas_call | solution.py:253
  50.5 1.1 fusion.26
  51.7 0.5 collective-permute-start.12
  52.4 0.9 add_bitcast_fusion.2
  53.8 2.8 %shard_map.89 = (f32[16,64,256]{2,1,0:T(8,128)S(1)}, f32[16,64,256]{2,1,0:T(8,128)S(1)}) custom-call(s32[1]{0:T(128)} %bitcast.at_ref, bf16[256,2048]{1,0:T(8,128)(2,1)S(1)} %copy-done, f32[16,136,256]{2,1,0:T(8,128)S(1)} %shard_map.85.nd_ref, f32[16,8,256]{2,1,0:T(8,128)S(1)} %get-tuple-element.116.inv_ref, f32[4,272,128]{2,1,0:T(8,128)S(1)} %pad_maximum_fusion.s0_ref, ...), custom_call_target="tpu_custom_call" | custom-call | flops 1000 | bytes 1000 | tf_op jit(solution)/shard_map/pallas_call | solution.py:253
  57.0 1.5 collective-permute-start.14
  58.5 1.5 collective-permute-start.15
  60.5 2.8 %shard_map.90 = (f32[8,64,768]{2,1,0:T(8,128)}, f32[8,64,768]{2,1,0:T(8,128)}, f32[8,64,512]{2,1,0:T(8,128)}) custom-call(f32[16,64,256]{2,1,0:T(8,128)S(1)} %get-tuple-element.121.a0_ref, f32[16,64,256]{2,1,0:T(8,128)S(1)} %collective-permute-done.13.a1_ref, bf16[512,2048]{1,0:T(8,128)(2,1)S(1)} %copy-done.15), custom_call_target="tpu_custom_call" | custom-call | flops 1000 | bytes 1000 | tf_op jit(solution)/shard_map/pallas_call | solution.py:253
  63.3 3.6 %collective-permute-done.15 = f32[272,128]{1,0:T(8,128)S(1)} collective-permute-done((f32[272,128]{1,0:T(8,128)S(1)}, f32[272,128]{1,0:T(8,128)S(1)}, u32[]{:S(2)}, u32[]{:S(2)}) %collective-permute-start.15) | collective-permute-done | bytes 139296 | tf_op jit(solution)/shard_map/ppermute | solution.py:266
  66.9 1.6 collective-permute-start.17
  68.5 0.5 collective-permute-start.18
  69.1 5.7 %shard_map.91 = (f32[16,8,256]{2,1,0:T(8,128)S(1)}, f32[16,128]{1,0:T(8,128)S(1)}) custom-call(s32[1]{0:T(128)} %bitcast.at_ref, bf16[256,2048]{1,0:T(8,128)(2,1)S(1)} %copy-done, f32[16,136,256]{2,1,0:T(8,128)S(1)} %shard_map.85.nd_ref, f32[16,128,256]{2,1,0:T(8,128)S(1)} %copy-done.3, f32[16,8,256]{2,1,0:T(8,128)S(1)} %get-tuple-element.116.inv_ref, ...), custom_call_target="tpu_custom_call" | custom-call | flops 1000 | bytes 1000 | tf_op jit(solution)/shard_map/pallas_call | solution.py:253
  74.9 2.1 %collective-permute-start.19 = (f32[272,128]{1,0:T(8,128)S(1)}, f32[272,128]{1,0:T(8,128)S(1)}, u32[]{:S(2)}, u32[]{:S(2)}) collective-permute-start(f32[272,128]{1,0:T(8,128)S(1)} %pad_maximum_fusion.9), channel_id=1, source_target_pairs={{0,8},{1,9},{2,10},{3,11},{4,12},{5,13},{6,14},{7,15},{8,0},{9,1},... | collective-permute-start | bytes 417800 | tf_op jit(solution)/shard_map/ppermute | solution.py:266
  77.0 14.4 %shard_map.92 = (bf16[256,2048]{1,0:T(8,128)(2,1)}, f32[256,2048]{1,0:T(8,128)S(1)}, f32[256,2048]{1,0:T(8,128)S(1)}) custom-call(s32[1]{0:T(128)} %bitcast.at_ref, bf16[256,2048]{1,0:T(8,128)(2,1)S(1)} %copy-done, bf16[256,2048]{1,0:T(8,128)(2,1)S(1)} %copy-done.6, bf16[256,2048]{1,0:T(8,128)(2,1)S(1)} %copy-done.10, f32[16,128,256]{2,1,0:T(8,128)S(1)} %copy-done.3, ...), custom_call_target="tpu_custom_call" | custom-call | flops 1000 | bytes 1000 | tf_op jit(solution)/shard_map/pallas_call | solution.py:253
  91.4 1.3 copy-done.25
  92.7 1.3 copy-done.27
  94.0 1.7 %collective-permute-done.19 = f32[272,128]{1,0:T(8,128)S(1)} collective-permute-done((f32[272,128]{1,0:T(8,128)S(1)}, f32[272,128]{1,0:T(8,128)S(1)}, u32[]{:S(2)}, u32[]{:S(2)}) %collective-permute-start.19) | collective-permute-done | bytes 139296 | tf_op jit(solution)/shard_map/ppermute | solution.py:266
  95.7 0.6 copy-done.41
  96.4 1.2 copy-done.20
  97.6 1.2 copy-done.22
  98.8 1.3 shard_map.93
  100.1 3.5 %collective-permute-done.20 = f32[272,128]{1,0:T(8,128)S(1)} collective-permute-done((f32[272,128]{1,0:T(8,128)S(1)}, f32[272,128]{1,0:T(8,128)S(1)}, u32[]{:S(2)}, u32[]{:S(2)}) %collective-permute-start.20) | collective-permute-done | bytes 139296 | tf_op jit(solution)/shard_map/ppermute | solution.py:266
  103.6 1.1 fusion.5
  104.7 1.6 collective-permute-start.31
  106.3 1.1 fusion.4
  107.4 1.2 fusion.1
  108.8 1.4 fusion.3
  110.1 0.6 collective-permute-start.22
  110.9 1.8 %collective-permute-start.23 = (f32[2,272,128]{2,1,0:T(8,128)S(1)}, f32[2,272,128]{2,1,0:T(8,128)S(1)}, u32[]{:S(2)}, u32[]{:S(2)}) collective-permute-start(f32[2,272,128]{2,1,0:T(8,128)S(1)} %pad_maximum_fusion.10), channel_id=1, source_target_pairs={{0,2},{1,3},{2,0},{3,1},{4,6},{5,7},{6,4},{7,5},{8,10},{9,11},{10,... | collective-permute-start | bytes 835592 | tf_op jit(solution)/shard_map/ppermute | solution.py:266
  112.8 1.2 slice_add_fusion
  114.0 1.2 fusion.2
  115.3 6.0 %collective-permute-done.23 = f32[2,272,128]{2,1,0:T(8,128)S(1)} collective-permute-done((f32[2,272,128]{2,1,0:T(8,128)S(1)}, f32[2,272,128]{2,1,0:T(8,128)S(1)}, u32[]{:S(2)}, u32[]{:S(2)}) %collective-permute-start.23) | collective-permute-done | bytes 278560 | tf_op jit(solution)/shard_map/ppermute | solution.py:266
  121.3 3.4 %collective-permute-done.21 = f32[2,2,64,768]{3,2,1,0:T(8,128)S(1)} collective-permute-done((f32[2,2,64,768]{3,2,1,0:T(8,128)S(1)}, f32[2,2,64,768]{3,2,1,0:T(8,128)S(1)}, u32[]{:S(2)}, u32[]{:S(2)}) %collective-permute-start.21) | collective-permute-done | bytes 786464 | tf_op jit(solution)/shard_map/ppermute | solution.py:266
  124.7 2.2 %collective-permute-done.22 = f32[2,2,64,768]{3,2,0,1:T(8,128)S(1)} collective-permute-done((f32[2,2,64,768]{3,2,0,1:T(8,128)S(1)}, f32[2,2,64,768]{3,2,0,1:T(8,128)S(1)}, u32[]{:S(2)}, u32[]{:S(2)}) %collective-permute-start.22) | collective-permute-done | bytes 786464 | tf_op jit(solution)/shard_map/ppermute | solution.py:266
  127.2 1.5 collective-permute-start.28
  128.7 1.8 %collective-permute-start.32 = (f32[2,64,512]{2,1,0:T(8,128)S(1)}, f32[2,64,512]{2,1,0:T(8,128)S(1)}, u32[]{:S(2)}, u32[]{:S(2)}) collective-permute-start(f32[2,64,512]{2,1,0:T(8,128)S(1)} %fusion.9), channel_id=1, source_target_pairs={{0,4},{1,5},{2,6},{3,7},{4,0},{5,1},{6,2},{7,3},{8,12},{9,13},{10,... | collective-permute-start | bytes 786440 | tf_op jit(solution)/shard_map/ppermute | solution.py:266
  131.5 8.3 %collective-permute-done.24 = f32[2,272,128]{2,1,0:T(8,128)S(1)} collective-permute-done((f32[2,272,128]{2,1,0:T(8,128)S(1)}, f32[2,272,128]{2,1,0:T(8,128)S(1)}, u32[]{:S(2)}, u32[]{:S(2)}) %collective-permute-start.24) | collective-permute-done | bytes 278560 | tf_op jit(solution)/shard_map/ppermute | solution.py:266
  140.3 2.7 %collective-permute-start.33 = (f32[64,512]{1,0:T(8,128)S(1)}, f32[64,512]{1,0:T(8,128)S(1)}, u32[]{:S(2)}, u32[]{:S(2)}) collective-permute-start(f32[64,512]{1,0:T(8,128)S(1)} %fusion.28), channel_id=1, source_target_pairs={{0,16},{1,17},{2,18},{3,19},{4,20},{5,21},{6,22},{7,23},{8,24},{9,... | collective-permute-start | bytes 393224 | tf_op jit(solution)/shard_map/ppermute | solution.py:266
  143.1 2.5 %collective-permute-start.29 = (f32[64,768]{1,0:T(8,128)S(1)}, f32[64,768]{1,0:T(8,128)S(1)}, u32[]{:S(2)}, u32[]{:S(2)}) collective-permute-start(f32[64,768]{1,0:T(8,128)S(1)} %fusion.11), channel_id=1, source_target_pairs={{0,16},{1,17},{2,18},{3,19},{4,20},{5,21},{6,22},{7,23},{8,24},{9,... | collective-permute-start | bytes 589832 | tf_op jit(solution)/shard_map/ppermute | solution.py:266
  145.7 4.1 %shard_map.94 = (bf16[256,2048]{1,0:T(8,128)(2,1)}, bf16[256,2048]{1,0:T(8,128)(2,1)}) custom-call(s32[1]{0:T(128)} %bitcast.at_ref, bf16[256,2048]{1,0:T(8,128)(2,1)S(1)} %copy-done.7, bf16[256,2048]{1,0:T(8,128)(2,1)S(1)} %copy-done.11, f32[256,2048]{1,0:T(8,128)S(1)} %copy-done.26, f32[256,2048]{1,0:T(8,128)S(1)} %copy-done.28, ...), custom_call_target="tpu_custom_call" | custom-call | flops 1000 | bytes 1000 | tf_op jit(solution)/shard_map/pallas_call | solution.py:253
  149.8 3.2 %collective-permute-start.27 = (f32[64,768]{1,0:T(8,128)S(1)}, f32[64,768]{1,0:T(8,128)S(1)}, u32[]{:S(2)}, u32[]{:S(2)}) collective-permute-start(f32[64,768]{1,0:T(8,128)S(1)} %fusion.13), channel_id=1, source_target_pairs={{0,2},{1,3},{2,0},{3,1},{4,6},{5,7},{6,4},{7,5},{8,10},{9,11},{10,... | collective-permute-start | bytes 589832 | tf_op jit(solution)/shard_map/ppermute | solution.py:266
  153.1 1.4 collective-permute-done.33
  154.4 3.9 %collective-permute-done.29 = f32[64,768]{1,0:T(8,128)S(1)} collective-permute-done((f32[64,768]{1,0:T(8,128)S(1)}, f32[64,768]{1,0:T(8,128)S(1)}, u32[]{:S(2)}, u32[]{:S(2)}) %collective-permute-start.29) | collective-permute-done | bytes 196640 | tf_op jit(solution)/shard_map/ppermute | solution.py:266
  158.5 0.8 pad_maximum_fusion.4
  (166 shorter events, 5.2 us)
Async XLA Ops:
  3.1 4.6 %copy-start.12 = (bf16[256,2048]{1,0:T(8,128)(2,1)S(1)}, bf16[256,2048]{1,0:T(8,128)(2,1)}, u32[]{:S(2)}) copy-start(bf16[256,2048]{1,0:T(8,128)(2,1)} %own_ref.1) | copy-start | bytes 3145732
  5.5 14.9 %copy-start.23 = (f32[4,272,128]{2,1,0:T(8,128)}, f32[4,272,128]{2,1,0:T(8,128)S(1)}, u32[]{:S(2)}) copy-start(f32[4,272,128]{2,1,0:T(8,128)S(1)} %get-tuple-element.95) | copy-start | bytes 1671172
  5.5 7.2 %copy-start = (bf16[256,2048]{1,0:T(8,128)(2,1)S(1)}, bf16[256,2048]{1,0:T(8,128)(2,1)}, u32[]{:S(2)}) copy-start(bf16[256,2048]{1,0:T(8,128)(2,1)} %q_ref.6) | copy-start | bytes 3145732
  5.5 7.2 %copy-start.5 = (bf16[256,2048]{1,0:T(8,128)(2,1)S(1)}, bf16[256,2048]{1,0:T(8,128)(2,1)}, u32[]{:S(2)}) copy-start(bf16[256,2048]{1,0:T(8,128)(2,1)} %k_ref.7) | copy-start | bytes 3145732
  5.6 7.1 %copy-start.9 = (bf16[256,2048]{1,0:T(8,128)(2,1)S(1)}, bf16[256,2048]{1,0:T(8,128)(2,1)}, u32[]{:S(2)}) copy-start(bf16[256,2048]{1,0:T(8,128)(2,1)} %v_ref.7) | copy-start | bytes 3145732
  5.6 2.1 %collective-permute-start = (f32[4,272,128]{2,1,0:T(8,128)S(1)}, f32[4,272,128]{2,1,0:T(8,128)S(1)}, u32[]{:S(2)}, u32[]{:S(2)}) collective-permute-start(f32[4,272,128]{2,1,0:T(8,128)S(1)} %get-tuple-element.96), channel_id=1, source_target_pairs={{0,1},{1,0},{2,3},{3,2},{4,5},{5,4},{6,7},{7,6},{8,9},{9,8},{10,11... | collective-permute-start | bytes 1671176 | tf_op jit(solution)/shard_map/ppermute | solution.py:266
  7.7 31.9 %copy-start.17 = (f32[4,272,128]{2,1,0:T(8,128)}, f32[4,272,128]{2,1,0:T(8,128)S(1)}, u32[]{:S(2)}) copy-start(f32[4,272,128]{2,1,0:T(8,128)S(1)} %collective-permute-done.mate_ref) | copy-start | bytes 1671172
  7.9 12.6 %collective-permute-start.4 = (f32[256,2048]{1,0:T(8,128)S(1)}, f32[256,2048]{1,0:T(8,128)S(1)}, u32[]{:S(2)}, u32[]{:S(2)}) collective-permute-start(f32[256,2048]{1,0:T(8,128)S(1)} %convert_element_type.3), channel_id=1, source_target_pairs={{0,1},{1,0},{2,3},{3,2},{4,5},{5,4},{6,7},{7,6},{8,9},{9,8},{10,11... | collective-permute-start | bytes 6291464 | tf_op jit(solution)/shard_map/ppermute | solution.py:266
  8.4 12.0 %collective-permute-start.3 = (f32[272,128]{1,0:T(8,128)S(1)}, f32[272,128]{1,0:T(8,128)S(1)}, u32[]{:S(2)}, u32[]{:S(2)}) collective-permute-start(f32[272,128]{1,0:T(8,128)S(1)} %get-tuple-element.195), channel_id=1, source_target_pairs={{0,6},{1,7},{2,4},{3,5},{4,2},{5,3},{6,0},{7,1},{8,14},{9,15},{10,... | collective-permute-start | bytes 417800 | tf_op jit(solution)/shard_map/ppermute | solution.py:266
  12.1 8.4 %collective-permute-start.2 = (f32[272,128]{1,0:T(8,128)S(1)}, f32[272,128]{1,0:T(8,128)S(1)}, u32[]{:S(2)}, u32[]{:S(2)}) collective-permute-start(f32[272,128]{1,0:T(8,128)S(1)} %get-tuple-element.196), channel_id=1, source_target_pairs={{0,4},{1,5},{2,6},{3,7},{4,0},{5,1},{6,2},{7,3},{8,12},{9,13},{10,... | collective-permute-start | bytes 417800 | tf_op jit(solution)/shard_map/ppermute | solution.py:266
  12.6 7.9 %collective-permute-start.1 = (f32[272,128]{1,0:T(8,128)S(1)}, f32[272,128]{1,0:T(8,128)S(1)}, u32[]{:S(2)}, u32[]{:S(2)}) collective-permute-start(f32[272,128]{1,0:T(8,128)S(1)} %get-tuple-element.194), channel_id=1, source_target_pairs={{0,2},{1,3},{2,0},{3,1},{4,6},{5,7},{6,4},{7,5},{8,10},{9,11},{10,... | collective-permute-start | bytes 417800 | tf_op jit(solution)/shard_map/ppermute | solution.py:266
  20.5 19.1 %collective-permute-start.5 = (f32[272,128]{1,0:T(8,128)S(1)}, f32[272,128]{1,0:T(8,128)S(1)}, u32[]{:S(2)}, u32[]{:S(2)}) collective-permute-start(f32[272,128]{1,0:T(8,128)S(1)} %get-tuple-element.99), channel_id=1, source_target_pairs={{0,8},{1,9},{2,10},{3,11},{4,12},{5,13},{6,14},{7,15},{8,16},{9,17... | collective-permute-start | bytes 417800 | tf_op jit(solution)/shard_map/ppermute | solution.py:279
  24.4 15.2 %collective-permute-start.6 = (f32[272,128]{1,0:T(8,128)S(1)}, f32[272,128]{1,0:T(8,128)S(1)}, u32[]{:S(2)}, u32[]{:S(2)}) collective-permute-start(f32[272,128]{1,0:T(8,128)S(1)} %get-tuple-element.99), channel_id=1, source_target_pairs={{0,16},{1,17},{2,18},{3,19},{4,20},{5,21},{6,22},{7,23},{8,24},{9,... | collective-permute-start | bytes 417800 | tf_op jit(solution)/shard_map/ppermute | solution.py:279
  28.9 10.7 %collective-permute-start.7 = (f32[272,128]{1,0:T(8,128)S(1)}, f32[272,128]{1,0:T(8,128)S(1)}, u32[]{:S(2)}, u32[]{:S(2)}) collective-permute-start(f32[272,128]{1,0:T(8,128)S(1)} %get-tuple-element.99), channel_id=1, source_target_pairs={{0,24},{1,25},{2,26},{3,27},{4,28},{5,29},{6,30},{7,31}} | collective-permute-start | bytes 417800 | tf_op jit(solution)/shard_map/ppermute | solution.py:279
  30.2 3.4 %copy-start.13 = (bf16[2048,2048]{1,0:T(8,128)(2,1)S(1)}, bf16[2048,2048]{1,0:T(8,128)(2,1)}, u32[]{:S(2)}) copy-start(bf16[2048,2048]{1,0:T(8,128)(2,1)} %w_ref.1) | copy-start | bytes 25165828
  40.5 9.9 %collective-permute-start.8 = (f32[272,128]{1,0:T(8,128)}, f32[272,128]{1,0:T(8,128)}, u32[]{:S(2)}, u32[]{:S(2)}) collective-permute-start(f32[272,128]{1,0:T(8,128)} %get-tuple-element.110), channel_id=1, source_target_pairs={{0,2},{1,3},{2,0},{3,1},{4,6},{5,7},{6,4},{7,5},{8,10},{9,11},{10,... | collective-permute-start | bytes 417800 | tf_op jit(solution)/shard_map/ppermute | solution.py:266
  41.9 8.4 %collective-permute-start.9 = (f32[272,128]{1,0:T(8,128)}, f32[272,128]{1,0:T(8,128)}, u32[]{:S(2)}, u32[]{:S(2)}) collective-permute-start(f32[272,128]{1,0:T(8,128)} %get-tuple-element.111), channel_id=1, source_target_pairs={{0,4},{1,5},{2,6},{3,7},{4,0},{5,1},{6,2},{7,3},{8,12},{9,13},{10,... | collective-permute-start | bytes 417800 | tf_op jit(solution)/shard_map/ppermute | solution.py:266
  43.5 6.9 %collective-permute-start.10 = (f32[272,128]{1,0:T(8,128)}, f32[272,128]{1,0:T(8,128)}, u32[]{:S(2)}, u32[]{:S(2)}) collective-permute-start(f32[272,128]{1,0:T(8,128)} %get-tuple-element.112), channel_id=1, source_target_pairs={{0,6},{1,7},{2,4},{3,5},{4,2},{5,3},{6,0},{7,1},{8,14},{9,15},{10,... | collective-permute-start | bytes 417800 | tf_op jit(solution)/shard_map/ppermute | solution.py:266
  45.5 4.9 %copy-start.18 = (f32[4,272,128]{2,1,0:T(8,128)S(1)}, f32[4,272,128]{2,1,0:T(8,128)}, u32[]{:S(2)}) copy-start(f32[4,272,128]{2,1,0:T(8,128)} %copy-done.17) | copy-start | bytes 1671172
  45.5 4.9 %copy-start.24 = (f32[4,272,128]{2,1,0:T(8,128)S(1)}, f32[4,272,128]{2,1,0:T(8,128)}, u32[]{:S(2)}) copy-start(f32[4,272,128]{2,1,0:T(8,128)} %copy-done.23) | copy-start | bytes 1671172
  50.4 2.0 %collective-permute-start.11 = (f32[4,272,128]{2,1,0:T(8,128)S(1)}, f32[4,272,128]{2,1,0:T(8,128)S(1)}, u32[]{:S(2)}, u32[]{:S(2)}) collective-permute-start(f32[4,272,128]{2,1,0:T(8,128)S(1)} %get-tuple-element.114), channel_id=1, source_target_pairs={{0,1},{1,0},{2,3},{3,2},{4,5},{5,4},{6,7},{7,6},{8,9},{9,8},{10,11... | collective-permute-start | bytes 1671176 | tf_op jit(solution)/shard_map/ppermute | solution.py:266
  51.7 2.1 %collective-permute-start.12 = (f32[4,272,128]{2,1,0:T(8,128)S(1)}, f32[4,272,128]{2,1,0:T(8,128)S(1)}, u32[]{:S(2)}, u32[]{:S(2)}) collective-permute-start(f32[4,272,128]{2,1,0:T(8,128)S(1)} %pad_maximum_fusion.1), channel_id=1, source_target_pairs={{0,1},{1,0},{2,3},{3,2},{4,5},{5,4},{6,7},{7,6},{8,9},{9,8},{10,11... | collective-permute-start | bytes 1671176 | tf_op jit(solution)/shard_map/ppermute | solution.py:266
  52.4 4.2 %copy-start.29 = (f32[4,272,128]{2,1,0:T(8,128)}, f32[4,272,128]{2,1,0:T(8,128)S(1)}, u32[]{:S(2)}) copy-start(f32[4,272,128]{2,1,0:T(8,128)S(1)} %collective-permute-done.11) | copy-start | bytes 1671172
  53.3 21.5 %copy-start.31 = (f32[272,128]{1,0:T(8,128)}, f32[272,128]{1,0:T(8,128)S(1)}, u32[]{:S(2)}) copy-start(f32[272,128]{1,0:T(8,128)S(1)} %get-tuple-element.127) | copy-start | bytes 417796
  53.8 6.7 %copy-start.15 = (bf16[512,2048]{1,0:T(8,128)(2,1)S(1)}, bf16[512,2048]{1,0:T(8,128)(2,1)}, u32[]{:S(2)}) copy-start(bf16[512,2048]{1,0:T(8,128)(2,1)} %copy-done.14) | copy-start | bytes 6291460
  56.6 6.7 %copy-start.19 = (f32[16,64,256]{2,1,0:T(8,128)}, f32[16,64,256]{2,1,0:T(8,128)S(1)}, u32[]{:S(2)}) copy-start(f32[16,64,256]{2,1,0:T(8,128)S(1)} %get-tuple-element.121.a0_ref) | copy-start | bytes 3145732
  56.6 3.9 %collective-permute-start.13 = (f32[16,64,256]{2,1,0:T(8,128)S(1)}, f32[16,64,256]{2,1,0:T(8,128)S(1)}, u32[]{:S(2)}, u32[]{:S(2)}) collective-permute-start(f32[16,64,256]{2,1,0:T(8,128)S(1)} %get-tuple-element.122), channel_id=1, source_target_pairs={{0,1},{1,0},{2,3},{3,2},{4,5},{5,4},{6,7},{7,6},{8,9},{9,8},{10,11... | collective-permute-start | bytes 3145736 | tf_op jit(solution)/shard_map/ppermute | solution.py:266
  57.0 6.3 %collective-permute-start.14 = (f32[272,128]{1,0:T(8,128)S(1)}, f32[272,128]{1,0:T(8,128)S(1)}, u32[]{:S(2)}, u32[]{:S(2)}) collective-permute-start(f32[272,128]{1,0:T(8,128)S(1)} %get-tuple-element.192), channel_id=1, source_target_pairs={{0,2},{1,3},{2,0},{3,1},{4,6},{5,7},{6,4},{7,5},{8,10},{9,11},{10,... | collective-permute-start | bytes 417800 | tf_op jit(solution)/shard_map/ppermute | solution.py:266
  58.5 8.4 %collective-permute-start.15 = (f32[272,128]{1,0:T(8,128)S(1)}, f32[272,128]{1,0:T(8,128)S(1)}, u32[]{:S(2)}, u32[]{:S(2)}) collective-permute-start(f32[272,128]{1,0:T(8,128)S(1)} %get-tuple-element.191), channel_id=1, source_target_pairs={{0,4},{1,5},{2,6},{3,7},{4,0},{5,1},{6,2},{7,3},{8,12},{9,13},{10,... | collective-permute-start | bytes 417800 | tf_op jit(solution)/shard_map/ppermute | solution.py:266
  60.0 6.9 %collective-permute-start.16 = (f32[272,128]{1,0:T(8,128)S(1)}, f32[272,128]{1,0:T(8,128)S(1)}, u32[]{:S(2)}, u32[]{:S(2)}) collective-permute-start(f32[272,128]{1,0:T(8,128)S(1)} %get-tuple-element.190), channel_id=1, source_target_pairs={{0,6},{1,7},{2,4},{3,5},{4,2},{5,3},{6,0},{7,1},{8,14},{9,15},{10,... | collective-permute-start | bytes 417800 | tf_op jit(solution)/shard_map/ppermute | solution.py:266
  60.5 2.8 %copy-start.21 = (f32[16,64,256]{2,1,0:T(8,128)}, f32[16,64,256]{2,1,0:T(8,128)S(1)}, u32[]{:S(2)}) copy-start(f32[16,64,256]{2,1,0:T(8,128)S(1)} %collective-permute-done.13.a1_ref) | copy-start | bytes 3145732
  60.5 8.5 %copy-start.3 = (f32[16,128,256]{2,1,0:T(8,128)S(1)}, f32[16,128,256]{2,1,0:T(8,128)}, u32[]{:S(2)}) copy-start(f32[16,128,256]{2,1,0:T(8,128)} %copy-done.1) | copy-start | bytes 6291460
  63.3 11.5 %copy-start.37 = (f32[272,128]{1,0:T(8,128)}, f32[272,128]{1,0:T(8,128)S(1)}, u32[]{:S(2)}) copy-start(f32[272,128]{1,0:T(8,128)S(1)} %collective-permute-done.14) | copy-start | bytes 417796
  66.9 7.9 %copy-start.33 = (f32[272,128]{1,0:T(8,128)}, f32[272,128]{1,0:T(8,128)S(1)}, u32[]{:S(2)}) copy-start(f32[272,128]{1,0:T(8,128)S(1)} %collective-permute-done.15) | copy-start | bytes 417796
  66.9 7.9 %copy-start.35 = (f32[272,128]{1,0:T(8,128)}, f32[272,128]{1,0:T(8,128)S(1)}, u32[]{:S(2)}) copy-start(f32[272,128]{1,0:T(8,128)S(1)} %collective-permute-done.16) | copy-start | bytes 417796
  66.9 40.5 %collective-permute-start.17 = (f32[8,64,768]{2,1,0:T(8,128)}, f32[8,64,768]{2,1,0:T(8,128)}, u32[]{:S(2)}, u32[]{:S(2)}) collective-permute-start(f32[8,64,768]{2,1,0:T(8,128)} %get-tuple-element.131), channel_id=1, source_target_pairs={{0,4},{1,5},{2,6},{3,7},{4,0},{5,1},{6,2},{7,3},{8,12},{9,13},{10,... | collective-permute-start | bytes 4718600 | tf_op jit(solution)/shard_map/ppermute | solution.py:266
  68.5 38.9 %collective-permute-start.18 = (f32[8,64,768]{2,1,0:T(8,128)}, f32[8,64,768]{2,1,0:T(8,128)}, u32[]{:S(2)}, u32[]{:S(2)}) collective-permute-start(f32[8,64,768]{2,1,0:T(8,128)} %get-tuple-element.132), channel_id=1, source_target_pairs={{0,2},{1,3},{2,0},{3,1},{4,6},{5,7},{6,4},{7,5},{8,10},{9,11},{10,... | collective-permute-start | bytes 4718600 | tf_op jit(solution)/shard_map/ppermute | solution.py:266
  69.1 34.5 %collective-permute-start.30 = (f32[8,64,512]{2,1,0:T(8,128)}, f32[8,64,512]{2,1,0:T(8,128)}, u32[]{:S(2)}, u32[]{:S(2)}) collective-permute-start(f32[8,64,512]{2,1,0:T(8,128)} %get-tuple-element.133), channel_id=1, source_target_pairs={{0,8},{1,9},{2,10},{3,11},{4,12},{5,13},{6,14},{7,15},{8,0},{9,1},... | collective-permute-start | bytes 3145736 | tf_op jit(solution)/shard_map/ppermute | solution.py:266
  69.1 7.9 %copy-start.6 = (bf16[256,2048]{1,0:T(8,128)(2,1)S(1)}, bf16[256,2048]{1,0:T(8,128)(2,1)}, u32[]{:S(2)}) copy-start(bf16[256,2048]{1,0:T(8,128)(2,1)} %k_ref.7) | copy-start | bytes 3145732
  69.1 7.9 %copy-start.10 = (bf16[256,2048]{1,0:T(8,128)(2,1)S(1)}, bf16[256,2048]{1,0:T(8,128)(2,1)}, u32[]{:S(2)}) copy-start(bf16[256,2048]{1,0:T(8,128)(2,1)} %v_ref.7) | copy-start | bytes 3145732
  74.9 20.8 %collective-permute-start.19 = (f32[272,128]{1,0:T(8,128)S(1)}, f32[272,128]{1,0:T(8,128)S(1)}, u32[]{:S(2)}, u32[]{:S(2)}) collective-permute-start(f32[272,128]{1,0:T(8,128)S(1)} %pad_maximum_fusion.9), channel_id=1, source_target_pairs={{0,8},{1,9},{2,10},{3,11},{4,12},{5,13},{6,14},{7,15},{8,0},{9,1},... | collective-permute-start | bytes 417800 | tf_op jit(solution)/shard_map/ppermute | solution.py:266
  77.0 19.4 %copy-start.16 = (bf16[512,2048]{1,0:T(8,128)(2,1)S(1)}, bf16[512,2048]{1,0:T(8,128)(2,1)}, u32[]{:S(2)}) copy-start(bf16[512,2048]{1,0:T(8,128)(2,1)} %copy-done.14) | copy-start | bytes 6291460
  96.4 7.2 %collective-permute-start.20 = (f32[272,128]{1,0:T(8,128)S(1)}, f32[272,128]{1,0:T(8,128)S(1)}, u32[]{:S(2)}, u32[]{:S(2)}) collective-permute-start(f32[272,128]{1,0:T(8,128)S(1)} %fusion.39), channel_id=1, source_target_pairs={{0,16},{1,17},{2,18},{3,19},{4,20},{5,21},{6,22},{7,23},{8,24},{9,... | collective-permute-start | bytes 417800 | tf_op jit(solution)/shard_map/ppermute | solution.py:266
  98.8 4.7 %copy-start.42 = (f32[272,128]{1,0:T(8,128)S(1)}, f32[272,128]{1,0:T(8,128)}, u32[]{:S(2)}) copy-start(f32[272,128]{1,0:T(8,128)} %copy-done.41) | copy-start | bytes 417796
  104.7 24.0 %collective-permute-start.31 = (f32[2,2,64,512]{3,2,0,1:T(8,128)S(1)}, f32[2,2,64,512]{3,2,0,1:T(8,128)S(1)}, u32[]{:S(2)}, u32[]{:S(2)}) collective-permute-start(f32[2,2,64,512]{3,2,0,1:T(8,128)S(1)} %fusion.5), channel_id=1, source_target_pairs={{0,2},{1,3},{2,0},{3,1},{4,6},{5,7},{6,4},{7,5},{8,10},{9,11},{10,... | collective-permute-start | bytes 1572872 | tf_op jit(solution)/shard_map/ppermute | solution.py:266
  108.7 16.0 %collective-permute-start.21 = (f32[2,2,64,768]{3,2,1,0:T(8,128)S(1)}, f32[2,2,64,768]{3,2,1,0:T(8,128)S(1)}, u32[]{:S(2)}, u32[]{:S(2)}) collective-permute-start(f32[2,2,64,768]{3,2,1,0:T(8,128)S(1)} %fusion.1), channel_id=1, source_target_pairs={{0,8},{1,9},{2,10},{3,11},{4,12},{5,13},{6,14},{7,15},{8,0},{9,1},... | collective-permute-start | bytes 2359304 | tf_op jit(solution)/shard_map/ppermute | solution.py:266
  110.1 16.7 %collective-permute-start.22 = (f32[2,2,64,768]{3,2,0,1:T(8,128)S(1)}, f32[2,2,64,768]{3,2,0,1:T(8,128)S(1)}, u32[]{:S(2)}, u32[]{:S(2)}) collective-permute-start(f32[2,2,64,768]{3,2,0,1:T(8,128)S(1)} %fusion.3), channel_id=1, source_target_pairs={{0,4},{1,5},{2,6},{3,7},{4,0},{5,1},{6,2},{7,3},{8,12},{9,13},{10,... | collective-permute-start | bytes 2359304 | tf_op jit(solution)/shard_map/ppermute | solution.py:266
  110.9 10.4 %collective-permute-start.23 = (f32[2,272,128]{2,1,0:T(8,128)S(1)}, f32[2,272,128]{2,1,0:T(8,128)S(1)}, u32[]{:S(2)}, u32[]{:S(2)}) collective-permute-start(f32[2,272,128]{2,1,0:T(8,128)S(1)} %pad_maximum_fusion.10), channel_id=1, source_target_pairs={{0,2},{1,3},{2,0},{3,1},{4,6},{5,7},{6,4},{7,5},{8,10},{9,11},{10,... | collective-permute-start | bytes 835592 | tf_op jit(solution)/shard_map/ppermute | solution.py:266
  121.3 7.4 %copy-start.39 = (f32[2,272,128]{2,1,0:T(8,128)}, f32[2,272,128]{2,1,0:T(8,128)S(1)}, u32[]{:S(2)}) copy-start(f32[2,272,128]{2,1,0:T(8,128)S(1)} %collective-permute-done.23) | copy-start | bytes 835588
  126.9 22.9 %collective-permute-start.26 = (f32[2,64,768]{2,1,0:T(8,128)S(1)}, f32[2,64,768]{2,1,0:T(8,128)S(1)}, u32[]{:S(2)}, u32[]{:S(2)}) collective-permute-start(f32[2,64,768]{2,1,0:T(8,128)S(1)} %fusion.8), channel_id=1, source_target_pairs={{0,16},{1,17},{2,18},{3,19},{4,20},{5,21},{6,22},{7,23},{8,24},{9,... | collective-permute-start | bytes 1179656 | tf_op jit(solution)/shard_map/ppermute | solution.py:266
  127.2 15.9 %collective-permute-start.28 = (f32[2,64,768]{2,1,0:T(8,128)S(1)}, f32[2,64,768]{2,1,0:T(8,128)S(1)}, u32[]{:S(2)}, u32[]{:S(2)}) collective-permute-start(f32[2,64,768]{2,1,0:T(8,128)S(1)} %fusion.6), channel_id=1, source_target_pairs={{0,8},{1,9},{2,10},{3,11},{4,12},{5,13},{6,14},{7,15},{8,0},{9,1},... | collective-permute-start | bytes 1179656 | tf_op jit(solution)/shard_map/ppermute | solution.py:266
  128.7 11.5 %collective-permute-start.32 = (f32[2,64,512]{2,1,0:T(8,128)S(1)}, f32[2,64,512]{2,1,0:T(8,128)S(1)}, u32[]{:S(2)}, u32[]{:S(2)}) collective-permute-start(f32[2,64,512]{2,1,0:T(8,128)S(1)} %fusion.9), channel_id=1, source_target_pairs={{0,4},{1,5},{2,6},{3,7},{4,0},{5,1},{6,2},{7,3},{8,12},{9,13},{10,... | collective-permute-start | bytes 786440 | tf_op jit(solution)/shard_map/ppermute | solution.py:266
  130.6 9.3 %collective-permute-start.24 = (f32[2,272,128]{2,1,0:T(8,128)S(1)}, f32[2,272,128]{2,1,0:T(8,128)S(1)}, u32[]{:S(2)}, u32[]{:S(2)}) collective-permute-start(f32[2,272,128]{2,1,0:T(8,128)S(1)} %pad_maximum_fusion.11), channel_id=1, source_target_pairs={{0,4},{1,5},{2,6},{3,7},{4,0},{5,1},{6,2},{7,3},{8,12},{9,13},{10,... | collective-permute-start | bytes 835592 | tf_op jit(solution)/shard_map/ppermute | solution.py:266
  131.0 8.9 %copy-start.40 = (f32[2,272,128]{2,1,0:T(8,128)S(1)}, f32[2,272,128]{2,1,0:T(8,128)}, u32[]{:S(2)}) copy-start(f32[2,272,128]{2,1,0:T(8,128)} %copy-done.39) | copy-start | bytes 835588
  131.0 8.9 %copy-start.45 = (f32[1,272,128]{2,1,0:T(8,128)S(1)}, f32[1,272,128]{2,1,0:T(8,128)}, u32[]{:S(2)}) copy-start(f32[1,272,128]{2,1,0:T(8,128)} %get-tuple-element.202) | copy-start | bytes 417796
  131.1 8.9 %copy-start.46 = (f32[1,272,128]{2,1,0:T(8,128)S(1)}, f32[1,272,128]{2,1,0:T(8,128)}, u32[]{:S(2)}) copy-start(f32[1,272,128]{2,1,0:T(8,128)} %get-tuple-element.203) | copy-start | bytes 417796
  139.9 5.8 %copy-start.28 = (f32[256,2048]{1,0:T(8,128)S(1)}, f32[256,2048]{1,0:T(8,128)}, u32[]{:S(2)}) copy-start(f32[256,2048]{1,0:T(8,128)} %copy-done.27) | copy-start | bytes 6291460
  140.1 5.6 %copy-start.26 = (f32[256,2048]{1,0:T(8,128)S(1)}, f32[256,2048]{1,0:T(8,128)}, u32[]{:S(2)}) copy-start(f32[256,2048]{1,0:T(8,128)} %copy-done.25) | copy-start | bytes 6291460
  140.1 5.6 %copy-start.7 = (bf16[256,2048]{1,0:T(8,128)(2,1)S(1)}, bf16[256,2048]{1,0:T(8,128)(2,1)}, u32[]{:S(2)}) copy-start(bf16[256,2048]{1,0:T(8,128)(2,1)} %k_ref.7) | copy-start | bytes 3145732
  140.2 5.6 %copy-start.11 = (bf16[256,2048]{1,0:T(8,128)(2,1)S(1)}, bf16[256,2048]{1,0:T(8,128)(2,1)}, u32[]{:S(2)}) copy-start(bf16[256,2048]{1,0:T(8,128)(2,1)} %v_ref.7) | copy-start | bytes 3145732
  140.2 5.5 %collective-permute-start.25 = (f32[4,272,128]{2,1,0:T(8,128)S(1)}, f32[4,272,128]{2,1,0:T(8,128)S(1)}, u32[]{:S(2)}, u32[]{:S(2)}) collective-permute-start(f32[4,272,128]{2,1,0:T(8,128)S(1)} %pad_maximum_fusion.2), channel_id=1, source_target_pairs={{0,1},{1,0},{2,3},{3,2},{4,5},{5,4},{6,7},{7,6},{8,9},{9,8},{10,11... | collective-permute-start | bytes 1671176 | tf_op jit(solution)/shard_map/ppermute | solution.py:266
  140.3 14.1 %collective-permute-start.33 = (f32[64,512]{1,0:T(8,128)S(1)}, f32[64,512]{1,0:T(8,128)S(1)}, u32[]{:S(2)}, u32[]{:S(2)}) collective-permute-start(f32[64,512]{1,0:T(8,128)S(1)} %fusion.28), channel_id=1, source_target_pairs={{0,16},{1,17},{2,18},{3,19},{4,20},{5,21},{6,22},{7,23},{8,24},{9,... | collective-permute-start | bytes 393224 | tf_op jit(solution)/shard_map/ppermute | solution.py:266
  143.1 15.3 %collective-permute-start.29 = (f32[64,768]{1,0:T(8,128)S(1)}, f32[64,768]{1,0:T(8,128)S(1)}, u32[]{:S(2)}, u32[]{:S(2)}) collective-permute-start(f32[64,768]{1,0:T(8,128)S(1)} %fusion.11), channel_id=1, source_target_pairs={{0,16},{1,17},{2,18},{3,19},{4,20},{5,21},{6,22},{7,23},{8,24},{9,... | collective-permute-start | bytes 589832 | tf_op jit(solution)/shard_map/ppermute | solution.py:266
  149.8 8.5 %collective-permute-start.27 = (f32[64,768]{1,0:T(8,128)S(1)}, f32[64,768]{1,0:T(8,128)S(1)}, u32[]{:S(2)}, u32[]{:S(2)}) collective-permute-start(f32[64,768]{1,0:T(8,128)S(1)} %fusion.13), channel_id=1, source_target_pairs={{0,2},{1,3},{2,0},{3,1},{4,6},{5,7},{6,4},{7,5},{8,10},{9,11},{10,... | collective-permute-start | bytes 589832 | tf_op jit(solution)/shard_map/ppermute | solution.py:266
  (18 other events, 28.5 us)

commit v6 on v5

--- a/solution.py
+++ b/solution.py
@@ -66,6 +66,10 @@
 
 def first_of(row):
     return jnp.where(lax.broadcasted_iota(jnp.int32, (8, row.shape[1]), 0) == 0, row, 0.0)
+
+
+def padded(row):
+    return jnp.where(lax.broadcasted_iota(jnp.int32, (16, row.shape[1]), 0) == 0, row, 0.0)
 
 
 def rows_of(r):
@@ -210,12 +214,13 @@
         fq = feature(q)
         fqs, fks = split(fq), split(feature(k_ref[:, cols].astype(F32)))
         ss = split(masked(mm(fks, fqs, NT), 1))
-        dn = split(gt_ref[head] * inv_ref[head, :1, :])
         dd = dd_ref[head, :1, :]
+        dn_dd = split(jnp.concatenate([gt_ref[head] * inv_ref[head, :1, :], padded(dd)], axis=0))
+        dn = tuple(x[:HEAD] for x in dn_dd)
         ds = split(masked(mm((v,), dn, NN) + dd, 1))
         z = z_ref[pl.ds(head, 1), :]
-        dd_rows, z_rows = (jnp.concatenate([first_of(x)] * 2, axis=0) for x in (dd, z))
-        dfq = mm(ds, fks, TN) + mm(dn, split(state), TN) + 0.5 * mm(split(dd_rows), split(z_rows), TN)
+        state_z = split(jnp.concatenate([state, padded(z)], axis=0))
+        dfq = mm(ds, fks, TN) + mm(dn_dd, state_z, TN)
         qg_ref[:, cols] = (dfq * slope(q, fq)).astype(BF16)
         dk_ref[:, cols] = mm(ds, fqs, NN)
         dv_ref[:, cols] = mm(ss, dn, NT)

time: 160 us -> 160 us (level)
  transfers between devices with their start and end apart: 34 -> 34, of which waited for: 12 -> 12; matrix products, arithmetic and copies ran while one was open for 7% -> 7% of each run, Pallas kernels for 28% -> 29%
where the time goes in v6:
time: 160 us; the launch traced here: 159 us
  Pallas kernels  51.5 us (32%)
  starting transfers between devices  43.5 us (27%)
  waiting for transfers between devices  34.8 us (22%)
  local copies, waits for them, and re-layouts  16.3 us (10%)
  other arithmetic  11.7 us (7%)
    pallas_call x10, Pallas kernels, call(): pl.pallas_call(kernel, out_shape=tuple(outs), in_specs=specs, out_specs=t...  48.2 us
    ppermute x31, waiting for transfers between devices, swap(): return lax.ppermute(x, 'seq', [(i, i ^ mask) for i in range(n)])  34.8 us
    ppermute x31, starting transfers between devices, swap(): return lax.ppermute(x, 'seq', [(i, i ^ mask) for i in range(n)])  33.8 us
    unnamed x94, local copies, waits for them, and re-layouts  16 us
    ppermute x3, starting transfers between devices, along(): lax.ppermute(layer, 'seq', [(b, a) for a, b in pairs] if later else pairs)  9.68 us
    pallas_call x1, Pallas kernels, attended_grad(): pl.pallas_call(grad_kernel, grid=(steps,), out_shape=(jax.ShapeDtypeStruc...  3.33 us
  transfers between devices with their start and end apart: 34, of which 12 were waited for; matrix products, arithmetic and copies ran while one was open for 7% of the time, Pallas kernels for 29%

profile of v6, /device:TPU:0, one launch (start us, length us, event | category | flops | bytes accessed | tf_op | source)
XLA Modules:
  0.0 159.3 jit_solution(3656049972027319050)
XLA Ops:
  0.6 1.2 copy-done.4
  1.9 1.2 copy-done.8
  3.1 2.4 %shard_map.84 = (f32[4,272,128]{2,1,0:T(8,128)S(1)}, f32[4,272,128]{2,1,0:T(8,128)S(1)}) custom-call(s32[1]{0:T(128)} %bitcast.at_ref, bf16[256,2048]{1,0:T(8,128)(2,1)S(1)} %copy-done.4, bf16[256,2048]{1,0:T(8,128)(2,1)S(1)} %copy-done.8), custom_call_target="tpu_custom_call" | custom-call | flops 1000 | bytes 1000 | tf_op jit(solution)/shard_map/pallas_call | solution.py:258
  5.6 0.5 collective-permute-start
  6.1 1.6 collective-permute-done.mate_ref
  8.4 3.7 %collective-permute-start.3 = (f32[272,128]{1,0:T(8,128)S(1)}, f32[272,128]{1,0:T(8,128)S(1)}, u32[]{:S(2)}, u32[]{:S(2)}) collective-permute-start(f32[272,128]{1,0:T(8,128)S(1)} %get-tuple-element.195), channel_id=1, source_target_pairs={{0,6},{1,7},{2,4},{3,5},{4,2},{5,3},{6,0},{7,1},{8,14},{9,15},{10,... | collective-permute-start | bytes 417800 | tf_op jit(solution)/shard_map/ppermute | solution.py:271
  12.1 0.5 collective-permute-start.2
  12.7 7.7 %shard_map.85.nd_ref = f32[16,136,256]{2,1,0:T(8,128)S(1)} custom-call(s32[1]{0:T(128)} %bitcast.at_ref, bf16[256,2048]{1,0:T(8,128)(2,1)S(1)} %copy-done, bf16[256,2048]{1,0:T(8,128)(2,1)S(1)} %copy-done.5, bf16[256,2048]{1,0:T(8,128)(2,1)S(1)} %copy-done.9), custom_call_target="tpu_custom_call" | custom-call | flops 1000 | bytes 1000 | tf_op jit(solution)/shard_map/pallas_call | solution.py:258
  20.5 3.9 %collective-permute-start.5 = (f32[272,128]{1,0:T(8,128)S(1)}, f32[272,128]{1,0:T(8,128)S(1)}, u32[]{:S(2)}, u32[]{:S(2)}) collective-permute-start(f32[272,128]{1,0:T(8,128)S(1)} %get-tuple-element.99), channel_id=1, source_target_pairs={{0,8},{1,9},{2,10},{3,11},{4,12},{5,13},{6,14},{7,15},{8,16},{9,17... | collective-permute-start | bytes 417800 | tf_op jit(solution)/shard_map/ppermute | solution.py:284
  24.4 4.5 %collective-permute-start.6 = (f32[272,128]{1,0:T(8,128)S(1)}, f32[272,128]{1,0:T(8,128)S(1)}, u32[]{:S(2)}, u32[]{:S(2)}) collective-permute-start(f32[272,128]{1,0:T(8,128)S(1)} %get-tuple-element.99), channel_id=1, source_target_pairs={{0,16},{1,17},{2,18},{3,19},{4,20},{5,21},{6,22},{7,23},{8,24},{9,... | collective-permute-start | bytes 417800 | tf_op jit(solution)/shard_map/ppermute | solution.py:284
  28.9 1.3 collective-permute-start.7
  30.2 3.4 %copy-done.13 = bf16[2048,2048]{1,0:T(8,128)(2,1)S(1)} copy-done((bf16[2048,2048]{1,0:T(8,128)(2,1)S(1)}, bf16[2048,2048]{1,0:T(8,128)(2,1)}, u32[]{:S(2)}) %copy-start.13) | copy-done | bytes 8388632
  33.6 3.3 %shard_map.86 = (f32[16,128,256]{2,1,0:T(8,128)S(1)}, bf16[512,2048]{1,0:T(8,128)(2,1)S(1)}) custom-call(bf16[256,2048]{1,0:T(8,128)(2,1)S(1)} %copy-done.12, bf16[2048,2048]{1,0:T(8,128)(2,1)S(1)} %copy-done.13, bf16[256,2048]{1,0:T(8,128)(2,1)S(1)} %copy-done.12, f32[256,2048]{1,0:T(8,128)S(1)} %collective-permute-done.4.mate_ref), custom_call_target="tpu_custom_call" | custom-call | flops 1000 | bytes 1000 | tf_op jit(solution)/shard_map/pallas_call | solution.py:127
  37.0 1.3 copy-done.1
  38.3 1.3 copy-done.14
  39.6 0.8 shard_map.87
  40.5 1.5 collective-permute-start.8
  41.9 1.5 collective-permute-start.9
  43.5 0.5 collective-permute-start.10
  44.0 1.6 copy-done.2
  45.5 4.8 %shard_map.88 = (f32[4,272,128]{2,1,0:T(8,128)S(1)}, f32[4,272,128]{2,1,0:T(8,128)S(1)}, f32[16,8,256]{2,1,0:T(8,128)S(1)}) custom-call(s32[1]{0:T(128)} %bitcast.at_ref, bf16[256,2048]{1,0:T(8,128)(2,1)S(1)} %copy-done, f32[16,136,256]{2,1,0:T(8,128)S(1)} %shard_map.85.nd_ref, f32[16,128,256]{2,1,0:T(8,128)S(1)} %copy-done.2, ...), custom_call_target="tpu_custom_call" | custom-call | flops 1000 | bytes 1000 | tf_op jit(solution)/shard_map/pallas_call | solution.py:258
  50.5 1.1 fusion.26
  51.7 0.5 collective-permute-start.12
  52.4 0.9 add_bitcast_fusion.2
  53.3 0.5 collective-permute-done.12.s1_ref
  53.8 2.8 %shard_map.89 = (f32[16,64,256]{2,1,0:T(8,128)S(1)}, f32[16,64,256]{2,1,0:T(8,128)S(1)}) custom-call(s32[1]{0:T(128)} %bitcast.at_ref, bf16[256,2048]{1,0:T(8,128)(2,1)S(1)} %copy-done, f32[16,136,256]{2,1,0:T(8,128)S(1)} %shard_map.85.nd_ref, f32[16,8,256]{2,1,0:T(8,128)S(1)} %get-tuple-element.116.inv_ref, f32[4,272,128]{2,1,0:T(8,128)S(1)} %pad_maximum_fusion.s0_ref, ...), custom_call_target="tpu_custom_call" | custom-call | flops 1000 | bytes 1000 | tf_op jit(solution)/shard_map/pallas_call | solution.py:258
  57.0 1.5 collective-permute-start.14
  58.5 1.5 collective-permute-start.15
  60.5 2.8 %shard_map.90 = (f32[8,64,768]{2,1,0:T(8,128)}, f32[8,64,768]{2,1,0:T(8,128)}, f32[8,64,512]{2,1,0:T(8,128)}) custom-call(f32[16,64,256]{2,1,0:T(8,128)S(1)} %get-tuple-element.121.a0_ref, f32[16,64,256]{2,1,0:T(8,128)S(1)} %collective-permute-done.13.a1_ref, bf16[512,2048]{1,0:T(8,128)(2,1)S(1)} %copy-done.15), custom_call_target="tpu_custom_call" | custom-call | flops 1000 | bytes 1000 | tf_op jit(solution)/shard_map/pallas_call | solution.py:258
  63.3 3.6 %collective-permute-done.15 = f32[272,128]{1,0:T(8,128)S(1)} collective-permute-done((f32[272,128]{1,0:T(8,128)S(1)}, f32[272,128]{1,0:T(8,128)S(1)}, u32[]{:S(2)}, u32[]{:S(2)}) %collective-permute-start.15) | collective-permute-done | bytes 139296 | tf_op jit(solution)/shard_map/ppermute | solution.py:271
  66.9 1.6 collective-permute-start.17
  68.5 0.5 collective-permute-start.18
  69.1 5.7 %shard_map.91 = (f32[16,8,256]{2,1,0:T(8,128)S(1)}, f32[16,128]{1,0:T(8,128)S(1)}) custom-call(s32[1]{0:T(128)} %bitcast.at_ref, bf16[256,2048]{1,0:T(8,128)(2,1)S(1)} %copy-done, f32[16,136,256]{2,1,0:T(8,128)S(1)} %shard_map.85.nd_ref, f32[16,128,256]{2,1,0:T(8,128)S(1)} %copy-done.3, f32[16,8,256]{2,1,0:T(8,128)S(1)} %get-tuple-element.116.inv_ref, ...), custom_call_target="tpu_custom_call" | custom-call | flops 1000 | bytes 1000 | tf_op jit(solution)/shard_map/pallas_call | solution.py:258
  74.9 2.1 %collective-permute-start.19 = (f32[272,128]{1,0:T(8,128)S(1)}, f32[272,128]{1,0:T(8,128)S(1)}, u32[]{:S(2)}, u32[]{:S(2)}) collective-permute-start(f32[272,128]{1,0:T(8,128)S(1)} %pad_maximum_fusion.9), channel_id=1, source_target_pairs={{0,8},{1,9},{2,10},{3,11},{4,12},{5,13},{6,14},{7,15},{8,0},{9,1},... | collective-permute-start | bytes 417800 | tf_op jit(solution)/shard_map/ppermute | solution.py:271
  77.0 15.9 %shard_map.92 = (bf16[256,2048]{1,0:T(8,128)(2,1)}, f32[256,2048]{1,0:T(8,128)S(1)}, f32[256,2048]{1,0:T(8,128)S(1)}) custom-call(s32[1]{0:T(128)} %bitcast.at_ref, bf16[256,2048]{1,0:T(8,128)(2,1)S(1)} %copy-done, bf16[256,2048]{1,0:T(8,128)(2,1)S(1)} %copy-done.6, bf16[256,2048]{1,0:T(8,128)(2,1)S(1)} %copy-done.10, f32[16,128,256]{2,1,0:T(8,128)S(1)} %copy-done.3, ...), custom_call_target="tpu_custom_call" | custom-call | flops 1000 | bytes 1000 | tf_op jit(solution)/shard_map/pallas_call | solution.py:258
  92.8 1.3 copy-done.25
  94.2 1.3 copy-done.27
  95.7 0.6 copy-done.41
  96.4 1.2 copy-done.20
  97.6 1.2 copy-done.22
  98.8 1.3 shard_map.93
  100.1 3.5 %collective-permute-done.20 = f32[272,128]{1,0:T(8,128)S(1)} collective-permute-done((f32[272,128]{1,0:T(8,128)S(1)}, f32[272,128]{1,0:T(8,128)S(1)}, u32[]{:S(2)}, u32[]{:S(2)}) %collective-permute-start.20) | collective-permute-done | bytes 139296 | tf_op jit(solution)/shard_map/ppermute | solution.py:271
  103.6 1.1 fusion.5
  104.7 1.6 collective-permute-start.31
  106.3 1.1 fusion.4
  107.4 1.2 fusion.1
  108.8 1.4 fusion.3
  110.1 0.6 collective-permute-start.22
  110.9 1.8 %collective-permute-start.23 = (f32[2,272,128]{2,1,0:T(8,128)S(1)}, f32[2,272,128]{2,1,0:T(8,128)S(1)}, u32[]{:S(2)}, u32[]{:S(2)}) collective-permute-start(f32[2,272,128]{2,1,0:T(8,128)S(1)} %pad_maximum_fusion.10), channel_id=1, source_target_pairs={{0,2},{1,3},{2,0},{3,1},{4,6},{5,7},{6,4},{7,5},{8,10},{9,11},{10,... | collective-permute-start | bytes 835592 | tf_op jit(solution)/shard_map/ppermute | solution.py:271
  112.8 1.2 slice_add_fusion
  114.0 1.2 fusion.2
  115.3 6.0 %collective-permute-done.23 = f32[2,272,128]{2,1,0:T(8,128)S(1)} collective-permute-done((f32[2,272,128]{2,1,0:T(8,128)S(1)}, f32[2,272,128]{2,1,0:T(8,128)S(1)}, u32[]{:S(2)}, u32[]{:S(2)}) %collective-permute-start.23) | collective-permute-done | bytes 278560 | tf_op jit(solution)/shard_map/ppermute | solution.py:271
  121.3 3.4 %collective-permute-done.21 = f32[2,2,64,768]{3,2,1,0:T(8,128)S(1)} collective-permute-done((f32[2,2,64,768]{3,2,1,0:T(8,128)S(1)}, f32[2,2,64,768]{3,2,1,0:T(8,128)S(1)}, u32[]{:S(2)}, u32[]{:S(2)}) %collective-permute-start.21) | collective-permute-done | bytes 786464 | tf_op jit(solution)/shard_map/ppermute | solution.py:271
  124.7 2.2 %collective-permute-done.22 = f32[2,2,64,768]{3,2,0,1:T(8,128)S(1)} collective-permute-done((f32[2,2,64,768]{3,2,0,1:T(8,128)S(1)}, f32[2,2,64,768]{3,2,0,1:T(8,128)S(1)}, u32[]{:S(2)}, u32[]{:S(2)}) %collective-permute-start.22) | collective-permute-done | bytes 786464 | tf_op jit(solution)/shard_map/ppermute | solution.py:271
  127.2 1.5 collective-permute-start.28
  128.7 1.8 %collective-permute-start.32 = (f32[2,64,512]{2,1,0:T(8,128)S(1)}, f32[2,64,512]{2,1,0:T(8,128)S(1)}, u32[]{:S(2)}, u32[]{:S(2)}) collective-permute-start(f32[2,64,512]{2,1,0:T(8,128)S(1)} %fusion.9), channel_id=1, source_target_pairs={{0,4},{1,5},{2,6},{3,7},{4,0},{5,1},{6,2},{7,3},{8,12},{9,13},{10,... | collective-permute-start | bytes 786440 | tf_op jit(solution)/shard_map/ppermute | solution.py:271
  131.5 8.3 %collective-permute-done.24 = f32[2,272,128]{2,1,0:T(8,128)S(1)} collective-permute-done((f32[2,272,128]{2,1,0:T(8,128)S(1)}, f32[2,272,128]{2,1,0:T(8,128)S(1)}, u32[]{:S(2)}, u32[]{:S(2)}) %collective-permute-start.24) | collective-permute-done | bytes 278560 | tf_op jit(solution)/shard_map/ppermute | solution.py:271
  140.3 2.7 %collective-permute-start.33 = (f32[64,512]{1,0:T(8,128)S(1)}, f32[64,512]{1,0:T(8,128)S(1)}, u32[]{:S(2)}, u32[]{:S(2)}) collective-permute-start(f32[64,512]{1,0:T(8,128)S(1)} %fusion.28), channel_id=1, source_target_pairs={{0,16},{1,17},{2,18},{3,19},{4,20},{5,21},{6,22},{7,23},{8,24},{9,... | collective-permute-start | bytes 393224 | tf_op jit(solution)/shard_map/ppermute | solution.py:271
  143.1 2.5 %collective-permute-start.29 = (f32[64,768]{1,0:T(8,128)S(1)}, f32[64,768]{1,0:T(8,128)S(1)}, u32[]{:S(2)}, u32[]{:S(2)}) collective-permute-start(f32[64,768]{1,0:T(8,128)S(1)} %fusion.11), channel_id=1, source_target_pairs={{0,16},{1,17},{2,18},{3,19},{4,20},{5,21},{6,22},{7,23},{8,24},{9,... | collective-permute-start | bytes 589832 | tf_op jit(solution)/shard_map/ppermute | solution.py:271
  145.7 4.1 %shard_map.94 = (bf16[256,2048]{1,0:T(8,128)(2,1)}, bf16[256,2048]{1,0:T(8,128)(2,1)}) custom-call(s32[1]{0:T(128)} %bitcast.at_ref, bf16[256,2048]{1,0:T(8,128)(2,1)S(1)} %copy-done.7, bf16[256,2048]{1,0:T(8,128)(2,1)S(1)} %copy-done.11, f32[256,2048]{1,0:T(8,128)S(1)} %copy-done.26, f32[256,2048]{1,0:T(8,128)S(1)} %copy-done.28, ...), custom_call_target="tpu_custom_call" | custom-call | flops 1000 | bytes 1000 | tf_op jit(solution)/shard_map/pallas_call | solution.py:258
  149.8 3.2 %collective-permute-start.27 = (f32[64,768]{1,0:T(8,128)S(1)}, f32[64,768]{1,0:T(8,128)S(1)}, u32[]{:S(2)}, u32[]{:S(2)}) collective-permute-start(f32[64,768]{1,0:T(8,128)S(1)} %fusion.13), channel_id=1, source_target_pairs={{0,2},{1,3},{2,0},{3,1},{4,6},{5,7},{6,4},{7,5},{8,10},{9,11},{10,... | collective-permute-start | bytes 589832 | tf_op jit(solution)/shard_map/ppermute | solution.py:271
  153.1 1.4 collective-permute-done.33
  154.4 3.9 %collective-permute-done.29 = f32[64,768]{1,0:T(8,128)S(1)} collective-permute-done((f32[64,768]{1,0:T(8,128)S(1)}, f32[64,768]{1,0:T(8,128)S(1)}, u32[]{:S(2)}, u32[]{:S(2)}) %collective-permute-start.29) | collective-permute-done | bytes 196640 | tf_op jit(solution)/shard_map/ppermute | solution.py:271
  158.5 0.8 pad_maximum_fusion.4
  (166 shorter events, 4.9 us)
Async XLA Ops:
  3.1 4.6 %copy-start.12 = (bf16[256,2048]{1,0:T(8,128)(2,1)S(1)}, bf16[256,2048]{1,0:T(8,128)(2,1)}, u32[]{:S(2)}) copy-start(bf16[256,2048]{1,0:T(8,128)(2,1)} %own_ref.1) | copy-start | bytes 3145732
  5.5 14.9 %copy-start.23 = (f32[4,272,128]{2,1,0:T(8,128)}, f32[4,272,128]{2,1,0:T(8,128)S(1)}, u32[]{:S(2)}) copy-start(f32[4,272,128]{2,1,0:T(8,128)S(1)} %get-tuple-element.95) | copy-start | bytes 1671172
  5.5 7.2 %copy-start = (bf16[256,2048]{1,0:T(8,128)(2,1)S(1)}, bf16[256,2048]{1,0:T(8,128)(2,1)}, u32[]{:S(2)}) copy-start(bf16[256,2048]{1,0:T(8,128)(2,1)} %q_ref.6) | copy-start | bytes 3145732
  5.5 7.2 %copy-start.5 = (bf16[256,2048]{1,0:T(8,128)(2,1)S(1)}, bf16[256,2048]{1,0:T(8,128)(2,1)}, u32[]{:S(2)}) copy-start(bf16[256,2048]{1,0:T(8,128)(2,1)} %k_ref.7) | copy-start | bytes 3145732
  5.6 7.1 %copy-start.9 = (bf16[256,2048]{1,0:T(8,128)(2,1)S(1)}, bf16[256,2048]{1,0:T(8,128)(2,1)}, u32[]{:S(2)}) copy-start(bf16[256,2048]{1,0:T(8,128)(2,1)} %v_ref.7) | copy-start | bytes 3145732
  5.6 2.1 %collective-permute-start = (f32[4,272,128]{2,1,0:T(8,128)S(1)}, f32[4,272,128]{2,1,0:T(8,128)S(1)}, u32[]{:S(2)}, u32[]{:S(2)}) collective-permute-start(f32[4,272,128]{2,1,0:T(8,128)S(1)} %get-tuple-element.96), channel_id=1, source_target_pairs={{0,1},{1,0},{2,3},{3,2},{4,5},{5,4},{6,7},{7,6},{8,9},{9,8},{10,11... | collective-permute-start | bytes 1671176 | tf_op jit(solution)/shard_map/ppermute | solution.py:271
  7.7 31.9 %copy-start.17 = (f32[4,272,128]{2,1,0:T(8,128)}, f32[4,272,128]{2,1,0:T(8,128)S(1)}, u32[]{:S(2)}) copy-start(f32[4,272,128]{2,1,0:T(8,128)S(1)} %collective-permute-done.mate_ref) | copy-start | bytes 1671172
  7.9 12.6 %collective-permute-start.4 = (f32[256,2048]{1,0:T(8,128)S(1)}, f32[256,2048]{1,0:T(8,128)S(1)}, u32[]{:S(2)}, u32[]{:S(2)}) collective-permute-start(f32[256,2048]{1,0:T(8,128)S(1)} %convert_element_type.3), channel_id=1, source_target_pairs={{0,1},{1,0},{2,3},{3,2},{4,5},{5,4},{6,7},{7,6},{8,9},{9,8},{10,11... | collective-permute-start | bytes 6291464 | tf_op jit(solution)/shard_map/ppermute | solution.py:271
  8.4 12.0 %collective-permute-start.3 = (f32[272,128]{1,0:T(8,128)S(1)}, f32[272,128]{1,0:T(8,128)S(1)}, u32[]{:S(2)}, u32[]{:S(2)}) collective-permute-start(f32[272,128]{1,0:T(8,128)S(1)} %get-tuple-element.195), channel_id=1, source_target_pairs={{0,6},{1,7},{2,4},{3,5},{4,2},{5,3},{6,0},{7,1},{8,14},{9,15},{10,... | collective-permute-start | bytes 417800 | tf_op jit(solution)/shard_map/ppermute | solution.py:271
  12.1 8.4 %collective-permute-start.2 = (f32[272,128]{1,0:T(8,128)S(1)}, f32[272,128]{1,0:T(8,128)S(1)}, u32[]{:S(2)}, u32[]{:S(2)}) collective-permute-start(f32[272,128]{1,0:T(8,128)S(1)} %get-tuple-element.196), channel_id=1, source_target_pairs={{0,4},{1,5},{2,6},{3,7},{4,0},{5,1},{6,2},{7,3},{8,12},{9,13},{10,... | collective-permute-start | bytes 417800 | tf_op jit(solution)/shard_map/ppermute | solution.py:271
  12.6 7.9 %collective-permute-start.1 = (f32[272,128]{1,0:T(8,128)S(1)}, f32[272,128]{1,0:T(8,128)S(1)}, u32[]{:S(2)}, u32[]{:S(2)}) collective-permute-start(f32[272,128]{1,0:T(8,128)S(1)} %get-tuple-element.194), channel_id=1, source_target_pairs={{0,2},{1,3},{2,0},{3,1},{4,6},{5,7},{6,4},{7,5},{8,10},{9,11},{10,... | collective-permute-start | bytes 417800 | tf_op jit(solution)/shard_map/ppermute | solution.py:271
  20.5 19.1 %collective-permute-start.5 = (f32[272,128]{1,0:T(8,128)S(1)}, f32[272,128]{1,0:T(8,128)S(1)}, u32[]{:S(2)}, u32[]{:S(2)}) collective-permute-start(f32[272,128]{1,0:T(8,128)S(1)} %get-tuple-element.99), channel_id=1, source_target_pairs={{0,8},{1,9},{2,10},{3,11},{4,12},{5,13},{6,14},{7,15},{8,16},{9,17... | collective-permute-start | bytes 417800 | tf_op jit(solution)/shard_map/ppermute | solution.py:284
  24.4 15.2 %collective-permute-start.6 = (f32[272,128]{1,0:T(8,128)S(1)}, f32[272,128]{1,0:T(8,128)S(1)}, u32[]{:S(2)}, u32[]{:S(2)}) collective-permute-start(f32[272,128]{1,0:T(8,128)S(1)} %get-tuple-element.99), channel_id=1, source_target_pairs={{0,16},{1,17},{2,18},{3,19},{4,20},{5,21},{6,22},{7,23},{8,24},{9,... | collective-permute-start | bytes 417800 | tf_op jit(solution)/shard_map/ppermute | solution.py:284
  28.9 10.7 %collective-permute-start.7 = (f32[272,128]{1,0:T(8,128)S(1)}, f32[272,128]{1,0:T(8,128)S(1)}, u32[]{:S(2)}, u32[]{:S(2)}) collective-permute-start(f32[272,128]{1,0:T(8,128)S(1)} %get-tuple-element.99), channel_id=1, source_target_pairs={{0,24},{1,25},{2,26},{3,27},{4,28},{5,29},{6,30},{7,31}} | collective-permute-start | bytes 417800 | tf_op jit(solution)/shard_map/ppermute | solution.py:284
  30.2 3.4 %copy-start.13 = (bf16[2048,2048]{1,0:T(8,128)(2,1)S(1)}, bf16[2048,2048]{1,0:T(8,128)(2,1)}, u32[]{:S(2)}) copy-start(bf16[2048,2048]{1,0:T(8,128)(2,1)} %w_ref.1) | copy-start | bytes 25165828
  40.5 9.9 %collective-permute-start.8 = (f32[272,128]{1,0:T(8,128)}, f32[272,128]{1,0:T(8,128)}, u32[]{:S(2)}, u32[]{:S(2)}) collective-permute-start(f32[272,128]{1,0:T(8,128)} %get-tuple-element.110), channel_id=1, source_target_pairs={{0,2},{1,3},{2,0},{3,1},{4,6},{5,7},{6,4},{7,5},{8,10},{9,11},{10,... | collective-permute-start | bytes 417800 | tf_op jit(solution)/shard_map/ppermute | solution.py:271
  41.9 8.4 %collective-permute-start.9 = (f32[272,128]{1,0:T(8,128)}, f32[272,128]{1,0:T(8,128)}, u32[]{:S(2)}, u32[]{:S(2)}) collective-permute-start(f32[272,128]{1,0:T(8,128)} %get-tuple-element.111), channel_id=1, source_target_pairs={{0,4},{1,5},{2,6},{3,7},{4,0},{5,1},{6,2},{7,3},{8,12},{9,13},{10,... | collective-permute-start | bytes 417800 | tf_op jit(solution)/shard_map/ppermute | solution.py:271
  43.5 6.9 %collective-permute-start.10 = (f32[272,128]{1,0:T(8,128)}, f32[272,128]{1,0:T(8,128)}, u32[]{:S(2)}, u32[]{:S(2)}) collective-permute-start(f32[272,128]{1,0:T(8,128)} %get-tuple-element.112), channel_id=1, source_target_pairs={{0,6},{1,7},{2,4},{3,5},{4,2},{5,3},{6,0},{7,1},{8,14},{9,15},{10,... | collective-permute-start | bytes 417800 | tf_op jit(solution)/shard_map/ppermute | solution.py:271
  45.5 4.9 %copy-start.18 = (f32[4,272,128]{2,1,0:T(8,128)S(1)}, f32[4,272,128]{2,1,0:T(8,128)}, u32[]{:S(2)}) copy-start(f32[4,272,128]{2,1,0:T(8,128)} %copy-done.17) | copy-start | bytes 1671172
  45.5 4.9 %copy-start.24 = (f32[4,272,128]{2,1,0:T(8,128)S(1)}, f32[4,272,128]{2,1,0:T(8,128)}, u32[]{:S(2)}) copy-start(f32[4,272,128]{2,1,0:T(8,128)} %copy-done.23) | copy-start | bytes 1671172
  50.4 2.0 %collective-permute-start.11 = (f32[4,272,128]{2,1,0:T(8,128)S(1)}, f32[4,272,128]{2,1,0:T(8,128)S(1)}, u32[]{:S(2)}, u32[]{:S(2)}) collective-permute-start(f32[4,272,128]{2,1,0:T(8,128)S(1)} %get-tuple-element.114), channel_id=1, source_target_pairs={{0,1},{1,0},{2,3},{3,2},{4,5},{5,4},{6,7},{7,6},{8,9},{9,8},{10,11... | collective-permute-start | bytes 1671176 | tf_op jit(solution)/shard_map/ppermute | solution.py:271
  51.7 2.1 %collective-permute-start.12 = (f32[4,272,128]{2,1,0:T(8,128)S(1)}, f32[4,272,128]{2,1,0:T(8,128)S(1)}, u32[]{:S(2)}, u32[]{:S(2)}) collective-permute-start(f32[4,272,128]{2,1,0:T(8,128)S(1)} %pad_maximum_fusion.1), channel_id=1, source_target_pairs={{0,1},{1,0},{2,3},{3,2},{4,5},{5,4},{6,7},{7,6},{8,9},{9,8},{10,11... | collective-permute-start | bytes 1671176 | tf_op jit(solution)/shard_map/ppermute | solution.py:271
  52.4 4.2 %copy-start.29 = (f32[4,272,128]{2,1,0:T(8,128)}, f32[4,272,128]{2,1,0:T(8,128)S(1)}, u32[]{:S(2)}) copy-start(f32[4,272,128]{2,1,0:T(8,128)S(1)} %collective-permute-done.11) | copy-start | bytes 1671172
  53.3 21.5 %copy-start.31 = (f32[272,128]{1,0:T(8,128)}, f32[272,128]{1,0:T(8,128)S(1)}, u32[]{:S(2)}) copy-start(f32[272,128]{1,0:T(8,128)S(1)} %get-tuple-element.127) | copy-start | bytes 417796
  53.8 6.7 %copy-start.15 = (bf16[512,2048]{1,0:T(8,128)(2,1)S(1)}, bf16[512,2048]{1,0:T(8,128)(2,1)}, u32[]{:S(2)}) copy-start(bf16[512,2048]{1,0:T(8,128)(2,1)} %copy-done.14) | copy-start | bytes 6291460
  56.6 6.7 %copy-start.19 = (f32[16,64,256]{2,1,0:T(8,128)}, f32[16,64,256]{2,1,0:T(8,128)S(1)}, u32[]{:S(2)}) copy-start(f32[16,64,256]{2,1,0:T(8,128)S(1)} %get-tuple-element.121.a0_ref) | copy-start | bytes 3145732
  56.6 3.9 %collective-permute-start.13 = (f32[16,64,256]{2,1,0:T(8,128)S(1)}, f32[16,64,256]{2,1,0:T(8,128)S(1)}, u32[]{:S(2)}, u32[]{:S(2)}) collective-permute-start(f32[16,64,256]{2,1,0:T(8,128)S(1)} %get-tuple-element.122), channel_id=1, source_target_pairs={{0,1},{1,0},{2,3},{3,2},{4,5},{5,4},{6,7},{7,6},{8,9},{9,8},{10,11... | collective-permute-start | bytes 3145736 | tf_op jit(solution)/shard_map/ppermute | solution.py:271
  57.0 6.3 %collective-permute-start.14 = (f32[272,128]{1,0:T(8,128)S(1)}, f32[272,128]{1,0:T(8,128)S(1)}, u32[]{:S(2)}, u32[]{:S(2)}) collective-permute-start(f32[272,128]{1,0:T(8,128)S(1)} %get-tuple-element.192), channel_id=1, source_target_pairs={{0,2},{1,3},{2,0},{3,1},{4,6},{5,7},{6,4},{7,5},{8,10},{9,11},{10,... | collective-permute-start | bytes 417800 | tf_op jit(solution)/shard_map/ppermute | solution.py:271
  58.5 8.4 %collective-permute-start.15 = (f32[272,128]{1,0:T(8,128)S(1)}, f32[272,128]{1,0:T(8,128)S(1)}, u32[]{:S(2)}, u32[]{:S(2)}) collective-permute-start(f32[272,128]{1,0:T(8,128)S(1)} %get-tuple-element.191), channel_id=1, source_target_pairs={{0,4},{1,5},{2,6},{3,7},{4,0},{5,1},{6,2},{7,3},{8,12},{9,13},{10,... | collective-permute-start | bytes 417800 | tf_op jit(solution)/shard_map/ppermute | solution.py:271
  60.0 6.9 %collective-permute-start.16 = (f32[272,128]{1,0:T(8,128)S(1)}, f32[272,128]{1,0:T(8,128)S(1)}, u32[]{:S(2)}, u32[]{:S(2)}) collective-permute-start(f32[272,128]{1,0:T(8,128)S(1)} %get-tuple-element.190), channel_id=1, source_target_pairs={{0,6},{1,7},{2,4},{3,5},{4,2},{5,3},{6,0},{7,1},{8,14},{9,15},{10,... | collective-permute-start | bytes 417800 | tf_op jit(solution)/shard_map/ppermute | solution.py:271
  60.5 2.8 %copy-start.21 = (f32[16,64,256]{2,1,0:T(8,128)}, f32[16,64,256]{2,1,0:T(8,128)S(1)}, u32[]{:S(2)}) copy-start(f32[16,64,256]{2,1,0:T(8,128)S(1)} %collective-permute-done.13.a1_ref) | copy-start | bytes 3145732
  60.5 8.5 %copy-start.3 = (f32[16,128,256]{2,1,0:T(8,128)S(1)}, f32[16,128,256]{2,1,0:T(8,128)}, u32[]{:S(2)}) copy-start(f32[16,128,256]{2,1,0:T(8,128)} %copy-done.1) | copy-start | bytes 6291460
  63.3 11.5 %copy-start.37 = (f32[272,128]{1,0:T(8,128)}, f32[272,128]{1,0:T(8,128)S(1)}, u32[]{:S(2)}) copy-start(f32[272,128]{1,0:T(8,128)S(1)} %collective-permute-done.14) | copy-start | bytes 417796
  66.9 7.9 %copy-start.33 = (f32[272,128]{1,0:T(8,128)}, f32[272,128]{1,0:T(8,128)S(1)}, u32[]{:S(2)}) copy-start(f32[272,128]{1,0:T(8,128)S(1)} %collective-permute-done.15) | copy-start | bytes 417796
  66.9 7.9 %copy-start.35 = (f32[272,128]{1,0:T(8,128)}, f32[272,128]{1,0:T(8,128)S(1)}, u32[]{:S(2)}) copy-start(f32[272,128]{1,0:T(8,128)S(1)} %collective-permute-done.16) | copy-start | bytes 417796
  66.9 40.5 %collective-permute-start.17 = (f32[8,64,768]{2,1,0:T(8,128)}, f32[8,64,768]{2,1,0:T(8,128)}, u32[]{:S(2)}, u32[]{:S(2)}) collective-permute-start(f32[8,64,768]{2,1,0:T(8,128)} %get-tuple-element.131), channel_id=1, source_target_pairs={{0,4},{1,5},{2,6},{3,7},{4,0},{5,1},{6,2},{7,3},{8,12},{9,13},{10,... | collective-permute-start | bytes 4718600 | tf_op jit(solution)/shard_map/ppermute | solution.py:271
  68.5 38.9 %collective-permute-start.18 = (f32[8,64,768]{2,1,0:T(8,128)}, f32[8,64,768]{2,1,0:T(8,128)}, u32[]{:S(2)}, u32[]{:S(2)}) collective-permute-start(f32[8,64,768]{2,1,0:T(8,128)} %get-tuple-element.132), channel_id=1, source_target_pairs={{0,2},{1,3},{2,0},{3,1},{4,6},{5,7},{6,4},{7,5},{8,10},{9,11},{10,... | collective-permute-start | bytes 4718600 | tf_op jit(solution)/shard_map/ppermute | solution.py:271
  69.1 34.5 %collective-permute-start.30 = (f32[8,64,512]{2,1,0:T(8,128)}, f32[8,64,512]{2,1,0:T(8,128)}, u32[]{:S(2)}, u32[]{:S(2)}) collective-permute-start(f32[8,64,512]{2,1,0:T(8,128)} %get-tuple-element.133), channel_id=1, source_target_pairs={{0,8},{1,9},{2,10},{3,11},{4,12},{5,13},{6,14},{7,15},{8,0},{9,1},... | collective-permute-start | bytes 3145736 | tf_op jit(solution)/shard_map/ppermute | solution.py:271
  69.1 7.9 %copy-start.6 = (bf16[256,2048]{1,0:T(8,128)(2,1)S(1)}, bf16[256,2048]{1,0:T(8,128)(2,1)}, u32[]{:S(2)}) copy-start(bf16[256,2048]{1,0:T(8,128)(2,1)} %k_ref.7) | copy-start | bytes 3145732
  69.1 7.9 %copy-start.10 = (bf16[256,2048]{1,0:T(8,128)(2,1)S(1)}, bf16[256,2048]{1,0:T(8,128)(2,1)}, u32[]{:S(2)}) copy-start(bf16[256,2048]{1,0:T(8,128)(2,1)} %v_ref.7) | copy-start | bytes 3145732
  74.9 20.8 %collective-permute-start.19 = (f32[272,128]{1,0:T(8,128)S(1)}, f32[272,128]{1,0:T(8,128)S(1)}, u32[]{:S(2)}, u32[]{:S(2)}) collective-permute-start(f32[272,128]{1,0:T(8,128)S(1)} %pad_maximum_fusion.9), channel_id=1, source_target_pairs={{0,8},{1,9},{2,10},{3,11},{4,12},{5,13},{6,14},{7,15},{8,0},{9,1},... | collective-permute-start | bytes 417800 | tf_op jit(solution)/shard_map/ppermute | solution.py:271
  77.0 19.4 %copy-start.16 = (bf16[512,2048]{1,0:T(8,128)(2,1)S(1)}, bf16[512,2048]{1,0:T(8,128)(2,1)}, u32[]{:S(2)}) copy-start(bf16[512,2048]{1,0:T(8,128)(2,1)} %copy-done.14) | copy-start | bytes 6291460
  96.4 7.2 %collective-permute-start.20 = (f32[272,128]{1,0:T(8,128)S(1)}, f32[272,128]{1,0:T(8,128)S(1)}, u32[]{:S(2)}, u32[]{:S(2)}) collective-permute-start(f32[272,128]{1,0:T(8,128)S(1)} %fusion.39), channel_id=1, source_target_pairs={{0,16},{1,17},{2,18},{3,19},{4,20},{5,21},{6,22},{7,23},{8,24},{9,... | collective-permute-start | bytes 417800 | tf_op jit(solution)/shard_map/ppermute | solution.py:271
  98.8 4.7 %copy-start.42 = (f32[272,128]{1,0:T(8,128)S(1)}, f32[272,128]{1,0:T(8,128)}, u32[]{:S(2)}) copy-start(f32[272,128]{1,0:T(8,128)} %copy-done.41) | copy-start | bytes 417796
  104.7 24.0 %collective-permute-start.31 = (f32[2,2,64,512]{3,2,0,1:T(8,128)S(1)}, f32[2,2,64,512]{3,2,0,1:T(8,128)S(1)}, u32[]{:S(2)}, u32[]{:S(2)}) collective-permute-start(f32[2,2,64,512]{3,2,0,1:T(8,128)S(1)} %fusion.5), channel_id=1, source_target_pairs={{0,2},{1,3},{2,0},{3,1},{4,6},{5,7},{6,4},{7,5},{8,10},{9,11},{10,... | collective-permute-start | bytes 1572872 | tf_op jit(solution)/shard_map/ppermute | solution.py:271
  108.7 16.0 %collective-permute-start.21 = (f32[2,2,64,768]{3,2,1,0:T(8,128)S(1)}, f32[2,2,64,768]{3,2,1,0:T(8,128)S(1)}, u32[]{:S(2)}, u32[]{:S(2)}) collective-permute-start(f32[2,2,64,768]{3,2,1,0:T(8,128)S(1)} %fusion.1), channel_id=1, source_target_pairs={{0,8},{1,9},{2,10},{3,11},{4,12},{5,13},{6,14},{7,15},{8,0},{9,1},... | collective-permute-start | bytes 2359304 | tf_op jit(solution)/shard_map/ppermute | solution.py:271
  110.1 16.7 %collective-permute-start.22 = (f32[2,2,64,768]{3,2,0,1:T(8,128)S(1)}, f32[2,2,64,768]{3,2,0,1:T(8,128)S(1)}, u32[]{:S(2)}, u32[]{:S(2)}) collective-permute-start(f32[2,2,64,768]{3,2,0,1:T(8,128)S(1)} %fusion.3), channel_id=1, source_target_pairs={{0,4},{1,5},{2,6},{3,7},{4,0},{5,1},{6,2},{7,3},{8,12},{9,13},{10,... | collective-permute-start | bytes 2359304 | tf_op jit(solution)/shard_map/ppermute | solution.py:271
  110.9 10.4 %collective-permute-start.23 = (f32[2,272,128]{2,1,0:T(8,128)S(1)}, f32[2,272,128]{2,1,0:T(8,128)S(1)}, u32[]{:S(2)}, u32[]{:S(2)}) collective-permute-start(f32[2,272,128]{2,1,0:T(8,128)S(1)} %pad_maximum_fusion.10), channel_id=1, source_target_pairs={{0,2},{1,3},{2,0},{3,1},{4,6},{5,7},{6,4},{7,5},{8,10},{9,11},{10,... | collective-permute-start | bytes 835592 | tf_op jit(solution)/shard_map/ppermute | solution.py:271
  121.3 7.4 %copy-start.39 = (f32[2,272,128]{2,1,0:T(8,128)}, f32[2,272,128]{2,1,0:T(8,128)S(1)}, u32[]{:S(2)}) copy-start(f32[2,272,128]{2,1,0:T(8,128)S(1)} %collective-permute-done.23) | copy-start | bytes 835588
  126.9 22.9 %collective-permute-start.26 = (f32[2,64,768]{2,1,0:T(8,128)S(1)}, f32[2,64,768]{2,1,0:T(8,128)S(1)}, u32[]{:S(2)}, u32[]{:S(2)}) collective-permute-start(f32[2,64,768]{2,1,0:T(8,128)S(1)} %fusion.8), channel_id=1, source_target_pairs={{0,16},{1,17},{2,18},{3,19},{4,20},{5,21},{6,22},{7,23},{8,24},{9,... | collective-permute-start | bytes 1179656 | tf_op jit(solution)/shard_map/ppermute | solution.py:271
  127.2 15.9 %collective-permute-start.28 = (f32[2,64,768]{2,1,0:T(8,128)S(1)}, f32[2,64,768]{2,1,0:T(8,128)S(1)}, u32[]{:S(2)}, u32[]{:S(2)}) collective-permute-start(f32[2,64,768]{2,1,0:T(8,128)S(1)} %fusion.6), channel_id=1, source_target_pairs={{0,8},{1,9},{2,10},{3,11},{4,12},{5,13},{6,14},{7,15},{8,0},{9,1},... | collective-permute-start | bytes 1179656 | tf_op jit(solution)/shard_map/ppermute | solution.py:271
  128.7 11.5 %collective-permute-start.32 = (f32[2,64,512]{2,1,0:T(8,128)S(1)}, f32[2,64,512]{2,1,0:T(8,128)S(1)}, u32[]{:S(2)}, u32[]{:S(2)}) collective-permute-start(f32[2,64,512]{2,1,0:T(8,128)S(1)} %fusion.9), channel_id=1, source_target_pairs={{0,4},{1,5},{2,6},{3,7},{4,0},{5,1},{6,2},{7,3},{8,12},{9,13},{10,... | collective-permute-start | bytes 786440 | tf_op jit(solution)/shard_map/ppermute | solution.py:271
  130.6 9.3 %collective-permute-start.24 = (f32[2,272,128]{2,1,0:T(8,128)S(1)}, f32[2,272,128]{2,1,0:T(8,128)S(1)}, u32[]{:S(2)}, u32[]{:S(2)}) collective-permute-start(f32[2,272,128]{2,1,0:T(8,128)S(1)} %pad_maximum_fusion.11), channel_id=1, source_target_pairs={{0,4},{1,5},{2,6},{3,7},{4,0},{5,1},{6,2},{7,3},{8,12},{9,13},{10,... | collective-permute-start | bytes 835592 | tf_op jit(solution)/shard_map/ppermute | solution.py:271
  131.0 8.9 %copy-start.40 = (f32[2,272,128]{2,1,0:T(8,128)S(1)}, f32[2,272,128]{2,1,0:T(8,128)}, u32[]{:S(2)}) copy-start(f32[2,272,128]{2,1,0:T(8,128)} %copy-done.39) | copy-start | bytes 835588
  131.0 8.9 %copy-start.45 = (f32[1,272,128]{2,1,0:T(8,128)S(1)}, f32[1,272,128]{2,1,0:T(8,128)}, u32[]{:S(2)}) copy-start(f32[1,272,128]{2,1,0:T(8,128)} %get-tuple-element.202) | copy-start | bytes 417796
  131.1 8.9 %copy-start.46 = (f32[1,272,128]{2,1,0:T(8,128)S(1)}, f32[1,272,128]{2,1,0:T(8,128)}, u32[]{:S(2)}) copy-start(f32[1,272,128]{2,1,0:T(8,128)} %get-tuple-element.203) | copy-start | bytes 417796
  139.9 5.8 %copy-start.28 = (f32[256,2048]{1,0:T(8,128)S(1)}, f32[256,2048]{1,0:T(8,128)}, u32[]{:S(2)}) copy-start(f32[256,2048]{1,0:T(8,128)} %copy-done.27) | copy-start | bytes 6291460
  140.1 5.6 %copy-start.26 = (f32[256,2048]{1,0:T(8,128)S(1)}, f32[256,2048]{1,0:T(8,128)}, u32[]{:S(2)}) copy-start(f32[256,2048]{1,0:T(8,128)} %copy-done.25) | copy-start | bytes 6291460
  140.1 5.6 %copy-start.7 = (bf16[256,2048]{1,0:T(8,128)(2,1)S(1)}, bf16[256,2048]{1,0:T(8,128)(2,1)}, u32[]{:S(2)}) copy-start(bf16[256,2048]{1,0:T(8,128)(2,1)} %k_ref.7) | copy-start | bytes 3145732
  140.2 5.6 %copy-start.11 = (bf16[256,2048]{1,0:T(8,128)(2,1)S(1)}, bf16[256,2048]{1,0:T(8,128)(2,1)}, u32[]{:S(2)}) copy-start(bf16[256,2048]{1,0:T(8,128)(2,1)} %v_ref.7) | copy-start | bytes 3145732
  140.2 5.5 %collective-permute-start.25 = (f32[4,272,128]{2,1,0:T(8,128)S(1)}, f32[4,272,128]{2,1,0:T(8,128)S(1)}, u32[]{:S(2)}, u32[]{:S(2)}) collective-permute-start(f32[4,272,128]{2,1,0:T(8,128)S(1)} %pad_maximum_fusion.2), channel_id=1, source_target_pairs={{0,1},{1,0},{2,3},{3,2},{4,5},{5,4},{6,7},{7,6},{8,9},{9,8},{10,11... | collective-permute-start | bytes 1671176 | tf_op jit(solution)/shard_map/ppermute | solution.py:271
  140.3 14.1 %collective-permute-start.33 = (f32[64,512]{1,0:T(8,128)S(1)}, f32[64,512]{1,0:T(8,128)S(1)}, u32[]{:S(2)}, u32[]{:S(2)}) collective-permute-start(f32[64,512]{1,0:T(8,128)S(1)} %fusion.28), channel_id=1, source_target_pairs={{0,16},{1,17},{2,18},{3,19},{4,20},{5,21},{6,22},{7,23},{8,24},{9,... | collective-permute-start | bytes 393224 | tf_op jit(solution)/shard_map/ppermute | solution.py:271
  143.1 15.3 %collective-permute-start.29 = (f32[64,768]{1,0:T(8,128)S(1)}, f32[64,768]{1,0:T(8,128)S(1)}, u32[]{:S(2)}, u32[]{:S(2)}) collective-permute-start(f32[64,768]{1,0:T(8,128)S(1)} %fusion.11), channel_id=1, source_target_pairs={{0,16},{1,17},{2,18},{3,19},{4,20},{5,21},{6,22},{7,23},{8,24},{9,... | collective-permute-start | bytes 589832 | tf_op jit(solution)/shard_map/ppermute | solution.py:271
  149.8 8.5 %collective-permute-start.27 = (f32[64,768]{1,0:T(8,128)S(1)}, f32[64,768]{1,0:T(8,128)S(1)}, u32[]{:S(2)}, u32[]{:S(2)}) collective-permute-start(f32[64,768]{1,0:T(8,128)S(1)} %fusion.13), channel_id=1, source_target_pairs={{0,2},{1,3},{2,0},{3,1},{4,6},{5,7},{6,4},{7,5},{8,10},{9,11},{10,... | collective-permute-start | bytes 589832 | tf_op jit(solution)/shard_map/ppermute | solution.py:271
  (18 other events, 28.5 us)
